TPU v7x, 32 devices: a whole 2x2x4 slice. The times are simulated.
32 devices in a mesh: groups: 2 (over y), feat: 4 (over z), tm: 2 (over x), sub: 2 (over core).
Axes of the slice: x: 2, y: 2, z: 4, core: 2. Of those that a mesh axis runs over, the one named last changes fastest.
Arguments:
- frames: bfloat16 [8, 256, 8192], P('groups', 'tm', ('feat', 'sub')), parts along dimension 0, may hold values from -16 to 19
- window_starts: int32 [8], P('groups'), parts along dimension 0, may hold values from 0 to 32, as said below
- lag_frames: int32 [8], P('groups'), parts along dimension 0, may hold values from 1 to 64
Outputs:
- covariance_zero: float32 [16384, 8192], P(('groups', 'feat'), ('tm', 'sub')), parts along dimension 0
- covariance_lag: float32 [16384, 8192], P(('groups', 'feat'), ('tm', 'sub')), parts along dimension 0
There are 2 independent parts, one for each index of `groups`. A program takes and returns all parts, laid end to end along the dimension named above; each array names one. Nothing has to cross between parts.
Inputs may be any that keep to these rules, and one draw needn't show every extreme that they name: `window_starts`: first frame of each trajectory's window.
All inputs are finite; a program needn't handle non-finite values.
Results may differ from a plain program's by a relative error of at most 0.0003.
Values may be sent and summed in bfloat16 or wider, within the bound.
No kernel may reach another device: no remote copies, remote signals or barrier semaphores. Data moves between devices by JAX's collectives and lax.ppermute only.
A program may use at most 128 MiB of HBM per device.

v0:
```python
import jax
import jax.numpy as jnp
from jax import lax
from jax.sharding import PartitionSpec as P

SLACK = 32
LAGMAX = 64


def spread(x, axis, root):
    mine = lax.axis_index(axis) == root
    return lax.psum(jnp.where(mine, x, jnp.zeros_like(x)), axis)


def window_masks(window_starts, lag_frames, stored):
    instant = jnp.arange(stored, dtype=jnp.int32)[None, :]
    window_begin = window_starts[:, None]
    shift_by = lag_frames[:, None]
    finish = window_begin + (stored - SLACK)
    base_mask = (instant >= window_begin) & (instant < finish - shift_by)
    lag_mask = (instant >= window_begin + shift_by) & (instant < finish)
    return (base_mask.astype(jnp.bfloat16), lag_mask.astype(jnp.bfloat16))


def shift_ahead(series, lag_frames):
    stored = series.shape[1]
    padded = jnp.pad(series, ((0, 0), (0, LAGMAX), (0, 0)))

    def one_series(padded_rows, shift_by):
        return lax.dynamic_slice_in_dim(padded_rows, shift_by, stored, 0)

    return jax.vmap(one_series)(padded, lag_frames)


def frame_product(left, right):
    return lax.dot_general(
        left, right, (((0, 1), (0, 1)), ((), ())), preferred_element_type=jnp.float32
    )


def frame_mean(mask, series, frame_count):
    return jnp.einsum("kt,ktf->f", mask, series, preferred_element_type=jnp.float32) / frame_count


def local(frames, window_starts, lag_frames):
    halves = lax.all_gather(frames, "sub", axis=2, tiled=True)
    row_data = lax.all_gather(halves, "tm", axis=1, tiled=True)
    stored = row_data.shape[1]
    base_mask, lag_mask = window_masks(window_starts, lag_frames, stored)
    frame_count = (row_data.shape[0] * (stored - SLACK) - jnp.sum(lag_frames)).astype(jnp.float32)
    masked_rows = row_data * base_mask[:, :, None]
    row_mean = frame_mean(base_mask, row_data, frame_count)
    groups = lax.axis_size("tm") * lax.axis_size("sub")
    per_group = lax.axis_size("feat") // groups
    column = lax.axis_index("tm") * lax.axis_size("sub") + lax.axis_index("sub")
    tile_parts = []
    for member in range(per_group):
        column_block = spread(row_data, "feat", column * per_group + member)
        zero_mean = frame_mean(base_mask, column_block, frame_count)
        later_mean = frame_mean(lag_mask, column_block, frame_count)
        zero_part = (
            frame_product(masked_rows, column_block) / frame_count
            - row_mean[:, None] * zero_mean[None, :]
        )
        crossed = frame_product(masked_rows, shift_ahead(column_block, lag_frames))
        lag_part = crossed / frame_count - row_mean[:, None] * later_mean[None, :]
        tile_parts.append((zero_part, lag_part))
    covariance_zero = jnp.concatenate([entries[0] for entries in tile_parts], axis=1)
    covariance_lag = jnp.concatenate([entries[1] for entries in tile_parts], axis=1)
    return (covariance_zero, covariance_lag)


def solution(mesh):
    placed = (P("groups", "tm", ("feat", "sub")), P("groups"), P("groups"))
    return jax.shard_map(
        local,
        mesh=mesh,
        in_specs=placed,
        out_specs=(P(("groups", "feat"), ("tm", "sub")), P(("groups", "feat"), ("tm", "sub"))),
        check_vma=False,
    )
```

profile of v0, /device:TPU:1, one launch (start us, length us, event | category | flops | bytes accessed | tf_op | source)
XLA Modules:
  0.0 300.3 jit_solution(14861193752405796205)
XLA Ops:
  7.2 0.7 all-gather.3.cloned.1.call-update
  7.9 14.7 %all-gather.3.cloned.1.call-done = bf16[4,128,2048]{2,1,0:T(8,128)(2,1)} async-done(((bf16[4,128,1024]{2,1,0:T(8,128)(2,1)}), bf16[4,128,2048]{2,1,0:T(8,128)(2,1)}) %all-gather.3.cloned.1.call-update) | async-done | bytes 2097168 | tf_op jit(solution)/shard_map/all_gather | solution.py:46
  22.7 59.0 %all-gather.5.cloned.1.call-done = bf16[4,256,2048]{2,1,0:T(8,128)(2,1)} async-done(((bf16[4,128,2048]{2,1,0:T(8,128)(2,1)}), bf16[4,256,2048]{2,1,0:T(8,128)(2,1)}) %all-gather.5.cloned.1.call-update) | async-done | bytes 4194320 | tf_op jit(solution)/shard_map/all_gather | solution.py:47
  81.7 2.3 broadcast_select_fusion
  84.1 0.6 copy-done.2
  84.7 0.6 fusion.20
  86.2 2.8 fusion.10
  89.1 151.7 %all-reduce.4.cloned.1.call-done = bf16[4,256,2048]{2,1,0:T(8,128)(2,1)} async-done(((bf16[4,256,2048]{2,1,0:T(8,128)(2,1)}), bf16[4,256,2048]{2,1,0:T(8,128)(2,1)}) %all-reduce.4.cloned.1.call-update) | async-done | bytes 4194320 | tf_op jit(solution)/shard_map/psum | solution.py:12
  240.8 5.3 %pad.5 = bf16[4,320,2048]{2,1,0:T(8,128)(2,1)} pad(bf16[4,256,2048]{2,1,0:T(8,128)(2,1)} %all-reduce.4.cloned.1.call-done, bf16[]{:T(256)} %constant.22.clone.1), padding=0_0x0_64x0_0 | pad | bytes 9437186 | tf_op jit(solution)/shard_map/jit(_pad)/pad | solution.py:27
  246.1 17.4 %while.2 = (s32[]{:T(128)}, bf16[4,320,2048]{2,1,0:T(8,128)(2,1)}, s32[4,3]{1,0:T(4,128)S(1)}, bf16[4,256,2048]{2,1,0:T(8,128)(2,1)}) while((s32[]{:T(128)}, bf16[4,320,2048]{2,1,0:T(8,128)(2,1)}, s32[4,3]{1,0:T(4,128)S(1)}, bf16[4,256,2048]{2,1,0:T(8,128)(2,1)}) %tuple.34), condition=%wide.while_cond.clone, body=%wide.while_body.sunk.clone | while | flops 2 | bytes 2098285 | solution.py:30
  246.1 0.6 fusion.28
  246.7 3.8 %dynamic-slice_dynamic-update-slice_fusion.3 = bf16[4,256,2048]{2,1,0:T(8,128)(2,1)} fusion(bf16[4,256,2048]{2,1,0:T(8,128)(2,1)} %get-tuple-element.81, s32[]{:T(128)S(6)} %copy.22, bf16[4,320,2048]{2,1,0:T(8,128)(2,1)} %get-tuple-element.83, s32[]{:T(128)} %bitcast.28, s32[]{:T(128)} %bitcast.29), kind=kLoop, calls=%fused_computation.clone.1.clone | loop fusion | bytes 2098180 | tf_op jit(solution)/shard_map/vmap()/gather
  250.5 0.6 fusion.28
  251.1 3.7 %dynamic-slice_dynamic-update-slice_fusion.3 = bf16[4,256,2048]{2,1,0:T(8,128)(2,1)} fusion(bf16[4,256,2048]{2,1,0:T(8,128)(2,1)} %get-tuple-element.81, s32[]{:T(128)S(6)} %copy.22, bf16[4,320,2048]{2,1,0:T(8,128)(2,1)} %get-tuple-element.83, s32[]{:T(128)} %bitcast.28, s32[]{:T(128)} %bitcast.29), kind=kLoop, calls=%fused_computation.clone.1.clone | loop fusion | bytes 2098180 | tf_op jit(solution)/shard_map/vmap()/gather
  254.8 0.6 fusion.28
  255.4 3.7 %dynamic-slice_dynamic-update-slice_fusion.3 = bf16[4,256,2048]{2,1,0:T(8,128)(2,1)} fusion(bf16[4,256,2048]{2,1,0:T(8,128)(2,1)} %get-tuple-element.81, s32[]{:T(128)S(6)} %copy.22, bf16[4,320,2048]{2,1,0:T(8,128)(2,1)} %get-tuple-element.83, s32[]{:T(128)} %bitcast.28, s32[]{:T(128)} %bitcast.29), kind=kLoop, calls=%fused_computation.clone.1.clone | loop fusion | bytes 2098180 | tf_op jit(solution)/shard_map/vmap()/gather
  259.2 0.6 fusion.28
  259.7 3.7 %dynamic-slice_dynamic-update-slice_fusion.3 = bf16[4,256,2048]{2,1,0:T(8,128)(2,1)} fusion(bf16[4,256,2048]{2,1,0:T(8,128)(2,1)} %get-tuple-element.81, s32[]{:T(128)S(6)} %copy.22, bf16[4,320,2048]{2,1,0:T(8,128)(2,1)} %get-tuple-element.83, s32[]{:T(128)} %bitcast.28, s32[]{:T(128)} %bitcast.29), kind=kLoop, calls=%fused_computation.clone.1.clone | loop fusion | bytes 2098180 | tf_op jit(solution)/shard_map/vmap()/gather
  263.5 3.0 fusion.8
  266.5 0.5 copy-done
  266.9 0.7 fusion.6
  267.6 1.5 copy-done.1
  269.1 12.3 %fusion.1 = f32[2048,2048]{1,0:T(8,128)} fusion(bf16[4,256,2048]{2,1,0:T(8,128)(2,1)S(1)} %copy-done, f32[2048]{0:T(1024)S(1)} %get-tuple-element.32, f32[2048]{0:T(1024)S(1)} %broadcast_divide_fusion.2, f32[]{:T(128)S(6)} %convert_element_type.14, bf16[4,256,2048]{2,1,0:T(8,128)(2,1)S(1)} %copy-done.1, bf16[4,256]{1,0:T(4,128)(2,1)S(1)} %get-tuple-element.26), kind=kOutput, calls=%fused_computation.5 | convolution fusion | flops 8604614656 | bytes 25184260 | tf_op jit(solution)/shard_map/dot_general | solution.py:36
  281.5 12.3 %fusion = f32[2048,2048]{1,0:T(8,128)} fusion(bf16[4,256,2048]{2,1,0:T(8,128)(2,1)S(1)} %copy-done.4, f32[2048]{0:T(1024)S(1)} %get-tuple-element.31, f32[2048]{0:T(1024)S(1)} %broadcast_divide_fusion.2, f32[]{:T(128)S(6)} %convert_element_type.14, bf16[4,256,2048]{2,1,0:T(8,128)(2,1)S(1)} %copy-done.1, bf16[4,256]{1,0:T(4,128)(2,1)S(1)} %get-tuple-element.26), kind=kOutput, calls=%fused_computation.3 | convolution fusion | flops 8604614656 | bytes 25184260 | tf_op jit(solution)/shard_map/dot_general | solution.py:36
  (24 shorter events, 0.5 us)
Async XLA Ops:
  7.2 15.4 %all-gather.3.cloned.1.call-start = ((), (), s32[]{:S(2)}) async-start(), calls=%async_computation | async-start | bytes 3145728 | tf_op jit(solution)/shard_map/all_gather | solution.py:46
  7.9 73.8 %all-gather.5.cloned.1.call-start = ((), (), s32[]{:S(2)}) async-start(), calls=%async_computation.1 | async-start | bytes 6291456 | tf_op jit(solution)/shard_map/all_gather | solution.py:47
  22.6 218.2 %all-reduce.4.cloned.1.call-start = ((), (), s32[]{:S(2)}) async-start(), calls=%async_computation.2 | async-start | bytes 8388608 | tf_op jit(solution)/shard_map/psum | solution.py:12
  84.0 0.7 copy-start.2
  84.0 0.7 copy-start.3
  263.5 3.4 %copy-start = (bf16[4,256,2048]{2,1,0:T(8,128)(2,1)S(1)}, bf16[4,256,2048]{2,1,0:T(8,128)(2,1)}, u32[]{:S(2)}) copy-start(bf16[4,256,2048]{2,1,0:T(8,128)(2,1)} %all-reduce.4.cloned.1.call-done) | copy-start | bytes 12582916
  266.9 2.2 copy-start.1
  269.1 12.4 %copy-start.4 = (bf16[4,256,2048]{2,1,0:T(8,128)(2,1)S(1)}, bf16[4,256,2048]{2,1,0:T(8,128)(2,1)}, u32[]{:S(2)}) copy-start(bf16[4,256,2048]{2,1,0:T(8,128)(2,1)} %get-tuple-element.9) | copy-start | bytes 12582916
Sparse Core Ops, SparseCore 0:
  9.5 13.0 all-gather.2
  24.2 57.5 all-gather.4
  84.7 156.1 all-reduce.3
where the time goes:
time: 301 us; the launch traced here: 300 us
  waiting for transfers between devices  226 us (75%)
  matrix products  31.1 us (10%)
  local copies, waits for them, and re-layouts  25.4 us (8%)
  between operations  14.4 us (5%)
  other arithmetic  3.09 us (1%)
    psum x1, waiting for transfers between devices, spread(): return lax.psum(jnp.where(mine, x, jnp.zeros_like(x)), axis)  152 us
    all_gather x1, waiting for transfers between devices, local(): row_data = lax.all_gather(halves, 'tm', axis=1, tiled=True)  59 us
    dot_general x2, matrix products, frame_product(): lax.dot_general(left, right, (((0, 1), (0, 1)), ((), ())), preferred_elem...  24.7 us
    gather x12, local copies, waits for them, and re-layouts  17.4 us
    all_gather x1, waiting for transfers between devices, local(): halves = lax.all_gather(frames, 'sub', axis=2, tiled=True)  14.7 us
    dot_general x3, matrix products, frame_mean(): jnp.einsum('kt,ktf->f', mask, series, preferred_element_type=jnp.float32)  6.48 us
  transfers between devices with their start and end apart: 3, of which 3 were waited for; matrix products, arithmetic and copies ran while one was open for 1% of the time, Pallas kernels for 0%

commit v1 on v0

--- a/solution.py
+++ b/solution.py
@@ -1,10 +1,16 @@
+import functools
+
 import jax
 import jax.numpy as jnp
 from jax import lax
+from jax.experimental import pallas as pl
+from jax.experimental.pallas import tpu as pltpu
 from jax.sharding import PartitionSpec as P
 
 SLACK = 32
 LAGMAX = 64
+AXES = ("feat", "tm", "sub")
+VMEM_LIMIT = 48 * 1024 * 1024
 
 
 def spread(x, axis, root):
@@ -42,7 +48,7 @@
     return jnp.einsum("kt,ktf->f", mask, series, preferred_element_type=jnp.float32) / frame_count
 
 
-def local(frames, window_starts, lag_frames):
+def general(frames, window_starts, lag_frames):
     halves = lax.all_gather(frames, "sub", axis=2, tiled=True)
     row_data = lax.all_gather(halves, "tm", axis=1, tiled=True)
     stored = row_data.shape[1]
@@ -70,10 +76,264 @@
     return (covariance_zero, covariance_lag)
 
 
+def rank(z, x, c):
+    return (z * 2 + x) * 2 + c
+
+
+def hops(links):
+    pairs = []
+    for x, src, dst in links:
+        for c in range(2):
+            pairs.append((rank(src, x, c), rank(dst, x, c)))
+            pairs.append((rank(3 - src, 1 - x, c), rank(3 - dst, 1 - x, c)))
+    return pairs
+
+
+def crossings(where):
+    return [(rank(z, x, c), rank(z, 1 - x, c)) for z, x in where for c in range(2)]
+
+
+CORES = [(rank(z, x, c), rank(z, x, 1 - c)) for z in range(4) for x in range(2) for c in range(2)]
+PLANES = crossings([(z, x) for z in range(4) for x in range(2)])
+NEXT = hops([(0, 0, 1), (0, 1, 2), (0, 2, 3)])
+FAR = hops([(1, 0, 1), (1, 1, 3)])
+FAR_AGAIN = hops([(1, 1, 3)])
+ENDS = crossings([(0, 0), (0, 1), (3, 0), (3, 1)])
+LAST = hops([(0, 1, 2), (0, 2, 3)])
+BACK = hops([(1, 2, 3), (0, 3, 2)])
+LAST_CROSS = crossings([(3, 1), (0, 0)])
+
+
+def send(x, pairs):
+    return lax.ppermute(x, AXES, pairs)
+
+
+def rows_kernel(
+    count_ref, starts_ref, lags_ref, x_ref, own_ref, other_ref, zero_ref, late_ref, sum_ref, *, window
+):
+    trajectories, half = own_ref.shape[0], own_ref.shape[1]
+    stored = 2 * half
+    first = x_ref[0] == 0
+    instant = lax.broadcasted_iota(jnp.int32, (stored, 1), 0)
+    total = jnp.zeros((own_ref.shape[2], half), jnp.float32)
+    for k in range(trajectories):
+        own = own_ref[k].astype(jnp.float32)
+        other = other_ref[k].astype(jnp.float32)
+        series = jnp.concatenate(
+            [jnp.where(first, own, other), jnp.where(first, other, own)], axis=0
+        )
+        start, lag = starts_ref[k], lags_ref[k]
+        kept = (instant >= start) & (instant < start + window - lag)
+        masked = jnp.where(kept, series, 0.0)
+        moved = pltpu.roll(masked, lag, axis=0)
+        for values, out_ref in ((masked, zero_ref), (moved, late_ref)):
+            turned = values.T
+            low, high = turned[:, :half], turned[:, half:]
+            mine = jnp.where(first, low, high)
+            theirs = jnp.where(first, high, low)
+            out_ref[:, k * half : (k + 1) * half] = mine.astype(jnp.bfloat16)
+            out_ref[:, (trajectories + k) * half : (trajectories + k + 1) * half] = theirs.astype(
+                jnp.bfloat16
+            )
+            if out_ref is zero_ref:
+                total = total + mine + theirs
+    mean = jnp.sum(total, axis=1, keepdims=True) / count_ref[0]
+    sum_ref[...] = jnp.broadcast_to(mean, sum_ref.shape)
+
+
+def prepare_rows(scalars, place, own, other, before, window):
+    trajectories, half, features = own.shape
+    tile = 256
+    depth = trajectories * 2 * half
+    count, starts, lags, x = scalars
+    steps = features // tile
+    out_shape = (
+        jax.ShapeDtypeStruct((2 * features, depth), jnp.bfloat16),
+        jax.ShapeDtypeStruct((2 * features, depth), jnp.bfloat16),
+        jax.ShapeDtypeStruct((2 * features, 128), jnp.float32),
+    )
+
+    def spot(i, place_ref, *_):
+        return (place_ref[0] * steps + i, 0)
+
+    data = pl.BlockSpec((trajectories, half, tile), lambda i, *_: (0, 0, i))
+    outs = [pl.BlockSpec((tile, depth), spot)] * 2 + [pl.BlockSpec((tile, 128), spot)]
+
+    def body(place_ref, count_ref, starts_ref, lags_ref, x_ref, own_ref, other_ref, *refs):
+        rows_kernel(
+            count_ref, starts_ref, lags_ref, x_ref, own_ref, other_ref, *refs[-3:], window=window
+        )
+
+    return pl.pallas_call(
+        body,
+        out_shape=out_shape,
+        grid_spec=pltpu.PrefetchScalarGridSpec(
+            num_scalar_prefetch=5,
+            grid=(steps,),
+            in_specs=[data, data] + [pl.BlockSpec(memory_space=pl.ANY)] * len(before),
+            out_specs=outs,
+        ),
+        input_output_aliases={7 + i: i for i in range(len(before))},
+        compiler_params=pltpu.CompilerParams(vmem_limit_bytes=VMEM_LIMIT),
+        cost_estimate=pl.CostEstimate(
+            flops=0, bytes_accessed=24 * features * depth, transcendentals=0
+        ),
+        name="rows",
+    )(place, count, starts, lags, x, own, other, *before)
+
+
+def product_kernel(
+    place_ref, count_ref, masks_ref, zero_ref, late_ref, mean_ref, mine_own_ref, mine_other_ref,
+    sib_ref, *refs
+):
+    cov_zero_ref, cov_late_ref, means_ref = refs[-3:]
+    i, j = pl.program_id(0), pl.program_id(1)
+    depth = mine_own_ref.shape[0]
+    scale = 1.0 / count_ref[0]
+
+    def dot(left, right):
+        return jnp.dot(left, right, preferred_element_type=jnp.float32)
+
+    def strip(own, other):
+        @pl.when(i == 0)
+        def _():
+            sums = dot(masks_ref[:, :depth], own) + dot(masks_ref[:, depth:], other)
+            means_ref[j] = sums * scale
+
+        row_mean = mean_ref[:, :1]
+        for left_ref, out_ref, which in ((zero_ref, cov_zero_ref, 0), (late_ref, cov_late_ref, 8)):
+            total = dot(left_ref[:, :depth], own) + dot(left_ref[:, depth:], other)
+            out_ref[...] = total * scale - row_mean * means_ref[j, which : which + 1, :]
+
+    @pl.when(j == 0)
+    def _():
+        strip(mine_own_ref[...], mine_other_ref[...])
+
+    @pl.when(j == 1)
+    def _():
+        strip(sib_ref[0], sib_ref[1])
+
+
+def product(place, count, masks, rows, mine_own, mine_other, sib, first, before, features):
+    zero, late, means = rows
+    height, depth = zero.shape
+    width = mine_own.shape[-1]
+    tile = min(512, height)
+    half = depth // 2
+    out = jax.ShapeDtypeStruct((height, 2 * features), jnp.float32)
+    strips = features // width
+
+    def spot(i, j, place_ref, *_):
+        part = jnp.where(j == 0, place_ref[0], 1 - place_ref[0])
+        return (i, part * strips + first // width)
+
+    left = pl.BlockSpec((tile, depth), lambda i, j, *_: (i, 0))
+    piece = pl.BlockSpec((half, width), lambda i, j, *_: (0, 0))
+    return pl.pallas_call(
+        product_kernel,
+        out_shape=(out, out),
+        grid_spec=pltpu.PrefetchScalarGridSpec(
+            num_scalar_prefetch=2,
+            grid=(height // tile, 2),
+            in_specs=[
+                pl.BlockSpec((16, depth), lambda i, j, *_: (0, 0)),
+                left,
+                left,
+                pl.BlockSpec((tile, 128), lambda i, j, *_: (i, 0)),
+                piece,
+                piece,
+                pl.BlockSpec((2, half, width), lambda i, j, *_: (0, 0, 0)),
+            ]
+            + [pl.BlockSpec(memory_space=pl.ANY)] * len(before),
+            out_specs=[pl.BlockSpec((tile, width), spot)] * 2,
+            scratch_shapes=[pltpu.VMEM((2, 16, width), jnp.float32)],
+        ),
+        input_output_aliases={9 + i: i for i in range(len(before))},
+        compiler_params=pltpu.CompilerParams(vmem_limit_bytes=VMEM_LIMIT),
+        cost_estimate=pl.CostEstimate(
+            flops=8 * height * depth * width,
+            bytes_accessed=4 * height * depth + 16 * height * width,
+            transcendentals=0,
+        ),
+        name="covariances",
+    )(place, count, masks, zero, late, means, mine_own, mine_other, sib, *before)
+
+
+def chunk_sizes(features):
+    return [features // 2, features // 2]
+
+
+def line_of_four(frames, window_starts, lag_frames):
+    trajectories, half, features = frames.shape
+    stored = 2 * half
+    window = stored - SLACK
+    z, x, c = (lax.axis_index(a) for a in AXES)
+    zm = jnp.where(x == 1, 3 - z, z)
+    far_mine = c == x
+    count = (trajectories * window - jnp.sum(lag_frames)).astype(jnp.float32).reshape(1)
+    plane = x.astype(jnp.int32).reshape(1)
+    scalars = (count, window_starts, lag_frames, plane)
+    place = c.astype(jnp.int32).reshape(1)
+
+    own = frames
+    cross = send(own, PLANES)
+    near1 = send(own, NEXT)
+    far1 = send(own, FAR)
+    sib_own = send(own, CORES)
+
+    near2 = send(jnp.where(zm == 0, cross, near1), NEXT)
+    far2 = send(far1, FAR_AGAIN)
+    ends = send(jnp.where(zm == 0, far1, near1), ENDS)
+    sib_cross = send(cross, CORES)
+
+    rows = prepare_rows(scalars, place, own, cross, (), window)
+    rows = prepare_rows(scalars, 1 - place, sib_own, sib_cross, rows, window)
+
+    base_mask, lag_mask = window_masks(window_starts, lag_frames, stored)
+
+    def relative(mask):
+        low, high = mask[:, :half].reshape(-1), mask[:, half:].reshape(-1)
+        return jnp.where(x == 0, jnp.concatenate([low, high]), jnp.concatenate([high, low]))
+
+    masks = jnp.concatenate(
+        [
+            jnp.broadcast_to(relative(m)[None, :], (8, trajectories * stored))
+            for m in (base_mask, lag_mask)
+        ]
+    )
+
+    outs = ()
+    first = 0
+    for width in chunk_sizes(features):
+        part = lambda a: a[:, :, first : first + width]
+        own_p, cross_p, near1_p, near2_p, far2_p, ends_p = (
+            part(a) for a in (own, cross, near1, near2, far2, ends)
+        )
+        near3 = send(near2_p, LAST)
+        back = send(jnp.where(zm == 1, own_p, ends_p), BACK)
+        cross3 = send(far2_p, LAST_CROSS)
+        far_own = lax.select_n(zm, own_p, near1_p, near2_p, near3)
+        far_other = lax.select_n(zm, cross_p, near2_p, near3, cross3)
+        close_own = lax.select_n(zm, back, own_p, near1_p, near2_p)
+        close_other = lax.select_n(zm, ends_p, cross_p, back, ends_p)
+        mine_own = jnp.where(far_mine, far_own, close_own)
+        mine_other = jnp.where(far_mine, far_other, close_other)
+        give_own = jnp.where(far_mine, close_own, far_own)
+        give_other = jnp.where(far_mine, close_other, far_other)
+        sib = send(jnp.stack([give_own, give_other]), CORES)
+        flat = lambda a: a.reshape(a.shape[:-3] + (trajectories * half, width))
+        outs = product(
+            place, count, masks, rows, flat(mine_own), flat(mine_other), flat(sib), first, outs, features
+        )
+        first += width
+    return outs
+
+
 def solution(mesh):
     placed = (P("groups", "tm", ("feat", "sub")), P("groups"), P("groups"))
+    line = mesh.shape["feat"] == 4 and mesh.shape["tm"] == 2 and mesh.shape["sub"] == 2
     return jax.shard_map(
-        local,
+        line_of_four if line else general,
         mesh=mesh,
         in_specs=placed,
         out_specs=(P(("groups", "feat"), ("tm", "sub")), P(("groups", "feat"), ("tm", "sub"))),

time: 301 us -> 147 us (0.49)
  waiting for transfers between devices: 226 us -> 55.4 us
  Pallas kernels: 0 us -> 44.6 us
  matrix products: 31.1 us -> 0 us
  starting transfers between devices: 0.11 us -> 28.6 us
  local copies, waits for them, and re-layouts: 25.4 us -> 3.4 us
  between operations: 14.4 us -> 1.48 us
  other arithmetic: 3.09 us -> 12.1 us
    psum x1 -> x0, waiting for transfers between devices: 152 us -> none  [spread(): return lax.psum(jnp.where(mine, x, jnp.zeros_like(x)), axis)]
    all_gather x2 -> x0, waiting for transfers between devices: 73.7 us -> none  [the longest x1 59 us: local(): row_data = lax.all_gather(halves, 'tm', axis=1, tiled=True)]
    ppermute x0 -> x16, waiting for transfers between devices: none -> 55.4 us  [send(): return lax.ppermute(x, AXES, pairs)]
    pallas_call x0 -> x4, Pallas kernels: none -> 44.6 us  [the longest x2 34 us: product(): pl.pallas_call(product_kernel, out_shape=(out, out), grid_spec=pltpu.Pref...]
    dot_general x5 -> x0, matrix products: 31.1 us -> none  [the longest x2 24.7 us: frame_product(): lax.dot_general(left, right, (((0, 1), (0, 1)), ((), ())), preferred_elem...]
    ppermute x0 -> x16, starting transfers between devices: none -> 28.6 us  [send(): return lax.ppermute(x, AXES, pairs)]
    gather x12 -> x0, local copies, waits for them, and re-layouts: 17.4 us -> none
    pad x1 -> x0, local copies, waits for them, and re-layouts: 5.27 us -> none  [shift_ahead(): padded = jnp.pad(series, ((0, 0), (0, LAGMAX), (0, 0)))]
  transfers between devices with their start and end apart: 3 -> 16, of which waited for: 3 -> 7; matrix products, arithmetic and copies ran while one was open for 1% -> 9% of each run, Pallas kernels for 0% -> 19%
where the time goes in v1:
time: 147 us; the launch traced here: 146 us
  waiting for transfers between devices  55.4 us (38%)
  Pallas kernels  44.6 us (30%)
  starting transfers between devices  28.6 us (19%)
  other arithmetic  12.1 us (8%)
  local copies, waits for them, and re-layouts  3.4 us (2%)
  between operations  1.48 us (1%)
    ppermute x16, waiting for transfers between devices, send(): return lax.ppermute(x, AXES, pairs)  55.4 us
    pallas_call x2, Pallas kernels, product(): pl.pallas_call(product_kernel, out_shape=(out, out), grid_spec=pltpu.Pref...  34 us
    ppermute x16, starting transfers between devices, send(): return lax.ppermute(x, AXES, pairs)  28.6 us
    pallas_call x2, Pallas kernels, prepare_rows(): pl.pallas_call(body, out_shape=out_shape, grid_spec=pltpu.PrefetchScalarG...  10.6 us
    another operation x4, other arithmetic, line_of_four(): sib = send(jnp.stack([give_own, give_other]), CORES)  4.63 us
    slice x2, local copies, waits for them, and re-layouts, line_of_four(): part = lambda a: a[:, :, first:first + width]  3.35 us
  transfers between devices with their start and end apart: 16, of which 7 were waited for; matrix products, arithmetic and copies ran while one was open for 9% of the time, Pallas kernels for 19%

profile of v1, /device:TPU:1, one launch (start us, length us, event | category | flops | bytes accessed | tf_op | source)
XLA Modules:
  0.0 145.5 jit_solution(6355246520734722852)
XLA Ops:
  0.7 4.2 %collective-permute-start.3 = (bf16[4,128,1024]{2,1,0:T(8,128)(2,1)}, bf16[4,128,1024]{2,1,0:T(8,128)(2,1)S(1)}, u32[]{:S(2)}, u32[]{:S(2)}) collective-permute-start(bf16[4,128,1024]{2,1,0:T(8,128)(2,1)} %own_ref.1), channel_id=1, source_target_pairs={{0,4},{14,10},{1,5},{15,11},{4,8},{10,6},{5,9},{11,7},{8,12},{6,2}... | collective-permute-start | bytes 3145736 | tf_op jit(solution)/shard_map/ppermute | solution.py:108
  6.3 20.7 %collective-permute-done.3 = bf16[4,128,1024]{2,1,0:T(8,128)(2,1)S(1)} collective-permute-done((bf16[4,128,1024]{2,1,0:T(8,128)(2,1)}, bf16[4,128,1024]{2,1,0:T(8,128)(2,1)S(1)}, u32[]{:S(2)}, u32[]{:S(2)}) %collective-permute-start.3) | collective-permute-done | bytes 1048608 | tf_op jit(solution)/shard_map/ppermute | solution.py:108
  27.0 2.0 %collective-permute-done.1.other_ref = bf16[4,128,1024]{2,1,0:T(8,128)(2,1)S(1)} collective-permute-done((bf16[4,128,1024]{2,1,0:T(8,128)(2,1)}, bf16[4,128,1024]{2,1,0:T(8,128)(2,1)S(1)}, u32[]{:S(2)}, u32[]{:S(2)}) %collective-permute-start.1) | collective-permute-done | bytes 1048608 | tf_op jit(solution)/shard_map/ppermute | solution.py:108
  29.0 2.8 %collective-permute-done.6 = bf16[4,128,1024]{2,1,0:T(8,128)(2,1)} collective-permute-done((bf16[4,128,1024]{2,1,0:T(8,128)(2,1)}, bf16[4,128,1024]{2,1,0:T(8,128)(2,1)}, u32[]{:S(2)}, u32[]{:S(2)}) %collective-permute-start.6) | collective-permute-done | bytes 1048608 | tf_op jit(solution)/shard_map/ppermute | solution.py:108
  31.8 2.8 %broadcast_select_fusion = (bf16[4,128,1024]{2,1,0:T(8,128)(2,1)}, bf16[4,128,1024]{2,1,0:T(8,128)(2,1)}) fusion(bf16[4,128,1024]{2,1,0:T(8,128)(2,1)} %collective-permute-done.6, bf16[4,128,1024]{2,1,0:T(8,128)(2,1)S(1)} %collective-permute-done.3, pred[]{:T(512)S(6)} %eq.21, bf16[4,128,1024]{2,1,0:T(8,128)(2,1)S(1)} %collective-permute-done.1.other_ref), kind=kLoop, calls=%fused_computation.2 | loop fusion | flops 1048576 | bytes 5242881 | tf_op jit(solution)/shard_map/jit(_where)/select_n | solution.py:286
  34.6 1.9 %collective-permute-start.7 = (bf16[4,128,1024]{2,1,0:T(8,128)(2,1)}, bf16[4,128,1024]{2,1,0:T(8,128)(2,1)}, u32[]{:S(2)}, u32[]{:S(2)}) collective-permute-start(bf16[4,128,1024]{2,1,0:T(8,128)(2,1)} %get-tuple-element.42), channel_id=1, source_target_pairs={{0,2},{1,3},{2,0},{3,1},{12,14},{13,15},{14,12},{15,13},{16,18},{1... | collective-permute-start | bytes 3145736 | tf_op jit(solution)/shard_map/ppermute | solution.py:108
  36.5 1.4 collective-permute-start.4
  41.2 18.3 %collective-permute-done.7 = bf16[4,128,1024]{2,1,0:T(8,128)(2,1)} collective-permute-done((bf16[4,128,1024]{2,1,0:T(8,128)(2,1)}, bf16[4,128,1024]{2,1,0:T(8,128)(2,1)}, u32[]{:S(2)}, u32[]{:S(2)}) %collective-permute-start.7) | collective-permute-done | bytes 1048608 | tf_op jit(solution)/shard_map/ppermute | solution.py:108
  59.6 2.4 %broadcast_select_fusion.2 = (bf16[4,128,512]{2,1,0:T(8,128)(2,1)S(1)}, bf16[4,128,512]{2,1,0:T(8,128)(2,1)}) fusion(pred[]{:T(512)S(6)} %eq.22, bf16[4,128,1024]{2,1,0:T(8,128)(2,1)} %collective-permute-done.7, bf16[4,128,1024]{2,1,0:T(8,128)(2,1)} %own_ref.1), kind=kLoop, calls=%fused_computation.16 | loop fusion | flops 524288 | bytes 3145729 | tf_op jit(solution)/shard_map/jit(_where)/select_n | solution.py:313
  65.7 1.5 %collective-permute-start.12 = (bf16[4,128,512]{2,1,0:T(8,128)(2,1)}, bf16[4,128,512]{2,1,0:T(8,128)(2,1)}, u32[]{:S(2)}, u32[]{:S(2)}) collective-permute-start(bf16[4,128,512]{2,1,0:T(8,128)(2,1)} %get-tuple-element.40), channel_id=1, source_target_pairs={{4,8},{10,6},{5,9},{11,7},{8,12},{6,2},{9,13},{7,3},{20,24},{26,22... | collective-permute-start | bytes 1572872 | tf_op jit(solution)/shard_map/ppermute | solution.py:108
  67.1 1.5 %collective-permute-start.5 = (bf16[4,128,512]{2,1,0:T(8,128)(2,1)}, bf16[4,128,512]{2,1,0:T(8,128)(2,1)}, u32[]{:S(2)}, u32[]{:S(2)}) collective-permute-start(bf16[4,128,512]{2,1,0:T(8,128)(2,1)} %get-tuple-element.41), channel_id=1, source_target_pairs={{4,8},{10,6},{5,9},{11,7},{8,12},{6,2},{9,13},{7,3},{20,24},{26,22... | collective-permute-start | bytes 1572872 | tf_op jit(solution)/shard_map/ppermute | solution.py:108
  68.6 2.3 %fusion.5 = (bf16[4,128,512]{2,1,0:T(8,128)(2,1)}, bf16[4,128,512]{2,1,0:T(8,128)(2,1)}) fusion(bf16[4,128,1024]{2,1,0:T(8,128)(2,1)} %collective-permute-done.9), kind=kLoop, calls=%fused_computation.39 | loop fusion | bytes 2097152 | tf_op jit(solution)/shard_map/slice | solution.py:308
  70.9 4.3 %collective-permute-start.14 = (bf16[4,128,512]{2,1,0:T(8,128)(2,1)}, bf16[4,128,512]{2,1,0:T(8,128)(2,1)}, u32[]{:S(2)}, u32[]{:S(2)}) collective-permute-start(bf16[4,128,512]{2,1,0:T(8,128)(2,1)} %get-tuple-element.38), channel_id=1, source_target_pairs={{14,12},{15,13},{0,2},{1,3},{30,28},{31,29},{16,18},{17,19}} | collective-permute-start | bytes 1572872 | tf_op jit(solution)/shard_map/ppermute | solution.py:108
  76.1 2.1 %collective-permute-start.10 = (bf16[4,128,512]{2,1,0:T(8,128)(2,1)}, bf16[4,128,512]{2,1,0:T(8,128)(2,1)}, u32[]{:S(2)}, u32[]{:S(2)}) collective-permute-start(bf16[4,128,512]{2,1,0:T(8,128)(2,1)} %get-tuple-element.39), channel_id=1, source_target_pairs={{14,12},{15,13},{0,2},{1,3},{30,28},{31,29},{16,18},{17,19}} | collective-permute-start | bytes 1572872 | tf_op jit(solution)/shard_map/ppermute | solution.py:108
  78.8 8.5 %collective-permute-done.8 = bf16[4,128,512]{2,1,0:T(8,128)(2,1)} collective-permute-done((bf16[4,128,512]{2,1,0:T(8,128)(2,1)}, bf16[4,128,512]{2,1,0:T(8,128)(2,1)}, u32[]{:S(2)}, u32[]{:S(2)}) %collective-permute-start.8) | collective-permute-done | bytes 524320 | tf_op jit(solution)/shard_map/ppermute | solution.py:108
  87.3 3.0 %collective-permute-start = (bf16[4,128,1024]{2,1,0:T(8,128)(2,1)}, bf16[4,128,1024]{2,1,0:T(8,128)(2,1)S(1)}, u32[]{:S(2)}, u32[]{:S(2)}) collective-permute-start(bf16[4,128,1024]{2,1,0:T(8,128)(2,1)} %own_ref.1), channel_id=1, source_target_pairs={{0,1},{1,0},{2,3},{3,2},{4,5},{5,4},{6,7},{7,6},{8,9},{9,8},{10,11... | collective-permute-start | bytes 3145736 | tf_op jit(solution)/shard_map/ppermute | solution.py:108
  90.3 2.2 %select_bitcast_fusion.1 = (bf16[1,4,128,512]{3,2,1,0:T(8,128)(2,1)S(1)}, bf16[4,128,512]{2,1,0:T(8,128)(2,1)S(1)}, bf16[4,128,512]{2,1,0:T(8,128)(2,1)S(1)}, bf...) fusion(pred[]{:T(512)S(6)} %eq.19, ...), kind=kLoop, calls=%fused_computation.5 | loop fusion | flops 3670016 | bytes 8388612 | tf_op jit(solution)/shard_map/stack | solution.py:323
  92.5 2.1 %collective-permute-done.10 = bf16[4,128,512]{2,1,0:T(8,128)(2,1)} collective-permute-done((bf16[4,128,512]{2,1,0:T(8,128)(2,1)}, bf16[4,128,512]{2,1,0:T(8,128)(2,1)}, u32[]{:S(2)}, u32[]{:S(2)}) %collective-permute-start.10) | collective-permute-done | bytes 524320 | tf_op jit(solution)/shard_map/ppermute | solution.py:108
  94.6 2.2 %select_bitcast_fusion = (bf16[1,4,128,512]{3,2,1,0:T(8,128)(2,1)S(1)}, bf16[4,128,512]{2,1,0:T(8,128)(2,1)S(1)}, bf16[4,128,512]{2,1,0:T(8,128)(2,1)S(1)}, bf16...) fusion(pred[]{:T(512)S(6)} %eq.19, ...), kind=kLoop, calls=%fused_computation.4 | loop fusion | flops 3670016 | bytes 9437188 | tf_op jit(solution)/shard_map/stack | solution.py:323
  96.9 3.5 %collective-permute-start.15 = (bf16[2,4,128,512]{3,2,1,0:T(8,128)(2,1)S(1)}, bf16[2,4,128,512]{3,2,1,0:T(8,128)(2,1)S(1)}, u32[]{:S(2)}, u32[]{:S(2)}) collective-permute-start(bf16[2,4,128,512]{3,2,1,0:T(8,128)(2,1)S(1)} %pad_maximum_fusion.1), channel_id=1, source_target_pairs={{0,1},{1,0},{2,3},{3,2},{4,5},{5,4},{6,7},{7,6},{8,9},{9,8},{10,11... | collective-permute-start | bytes 3145736 | tf_op jit(solution)/shard_map/ppermute | solution.py:108
  100.5 5.4 %rows.2 = (bf16[2048,1024]{1,0:T(8,128)(2,1)}, bf16[2048,1024]{1,0:T(8,128)(2,1)}, f32[2048,128]{1,0:T(8,128)S(1)}) custom-call(s32[1]{0:T(128)} %bitcast.place_ref, f32[1]{0:T(128)} %bitcast.1.count_ref, s32[4]{0:T(128)S(1)} %copy-done.1, s32[4]{0:T(128)S(1)} %copy-done.2, s32[1]{0:T(128)} %bitcast.6.x_ref, bf16[4,128,1024]{2,1,0:T(8,128)(2,1)S(1)} %copy-done, ...), custom_call_target="tpu_custom_call" | custom-call | bytes 25165824 | tf_op jit(solution)/shard_map/rows/pallas_call | solution.py:167
  105.9 5.3 %rows.3 = (bf16[2048,1024]{1,0:T(8,128)(2,1)}, bf16[2048,1024]{1,0:T(8,128)(2,1)}, f32[2048,128]{1,0:T(8,128)S(1)}) custom-call(s32[1]{0:T(128)S(6)} %sub.15.place_ref, f32[1]{0:T(128)} %bitcast.1.count_ref, s32[4]{0:T(128)S(1)} %copy-done.1, s32[4]{0:T(128)S(1)} %copy-done.2, ...), custom_call_target="tpu_custom_call", output_to_operand_aliasing={{0}: (7, {}), {1}: (8, {}), {2}: (9, {})} | custom-call | bytes 25165824 | tf_op jit(solution)/shard_map/rows/pallas_call | solution.py:167
  111.6 17.0 %covariances.2 = (f32[2048,2048]{1,0:T(8,128)}, f32[2048,2048]{1,0:T(8,128)}) custom-call(s32[1]{0:T(128)} %bitcast.place_ref, f32[1]{0:T(128)} %bitcast.1.count_ref, bf16[16,1024]{1,0:T(8,128)(2,1)S(1)} %pad_maximum_fusion.2.masks_ref, bf16[2048,1024]{1,0:T(8,128)(2,1)} %get-tuple-element.13.zero_ref, bf16[2048,1024]{1,0:T(8,128)(2,1)} %get-tuple-element.14.late_ref, ...), custom_call_target="tpu_custom_call" | custom-call | flops 8589934592 | bytes 25165824 | tf_op jit(solution)/shard_map/covariances/pallas_call | solution.py:232
  128.6 17.0 %covariances.3 = (f32[2048,2048]{1,0:T(8,128)}, f32[2048,2048]{1,0:T(8,128)}) custom-call(s32[1]{0:T(128)} %bitcast.place_ref, f32[1]{0:T(128)} %bitcast.1.count_ref, bf16[16,1024]{1,0:T(8,128)(2,1)S(1)} %pad_maximum_fusion.2.masks_ref, bf16[2048,1024]{1,0:T(8,128)(2,1)} %get-tuple-element.13.zero_ref, ...), custom_call_target="tpu_custom_call", output_to_operand_aliasing={{0}: (9, {}), {1}: (10, {})} | custom-call | flops 8589934592 | bytes 25165824 | tf_op jit(solution)/shard_map/covariances/pallas_call | solution.py:232
  (39 shorter events, 9.9 us)
Async XLA Ops:
  0.6 99.9 %copy-start = (bf16[4,128,1024]{2,1,0:T(8,128)(2,1)S(1)}, bf16[4,128,1024]{2,1,0:T(8,128)(2,1)}, u32[]{:S(2)}) copy-start(bf16[4,128,1024]{2,1,0:T(8,128)(2,1)} %own_ref.1) | copy-start | bytes 3145732
  0.6 99.9 %copy-start.1 = (s32[4]{0:T(128)S(1)}, s32[4]{0:T(128)}, u32[]{:S(2)}) copy-start(s32[4]{0:T(128)} %starts_ref.3) | copy-start | bytes 52
  0.7 99.9 %copy-start.2 = (s32[4]{0:T(128)S(1)}, s32[4]{0:T(128)}, u32[]{:S(2)}) copy-start(s32[4]{0:T(128)} %lags_ref.3) | copy-start | bytes 52
  0.7 26.3 %collective-permute-start.3 = (bf16[4,128,1024]{2,1,0:T(8,128)(2,1)}, bf16[4,128,1024]{2,1,0:T(8,128)(2,1)S(1)}, u32[]{:S(2)}, u32[]{:S(2)}) collective-permute-start(bf16[4,128,1024]{2,1,0:T(8,128)(2,1)} %own_ref.1), channel_id=1, source_target_pairs={{0,4},{14,10},{1,5},{15,11},{4,8},{10,6},{5,9},{11,7},{8,12},{6,2}... | collective-permute-start | bytes 3145736 | tf_op jit(solution)/shard_map/ppermute | solution.py:108
  4.9 24.1 %collective-permute-start.1 = (bf16[4,128,1024]{2,1,0:T(8,128)(2,1)}, bf16[4,128,1024]{2,1,0:T(8,128)(2,1)S(1)}, u32[]{:S(2)}, u32[]{:S(2)}) collective-permute-start(bf16[4,128,1024]{2,1,0:T(8,128)(2,1)} %own_ref.1), channel_id=1, source_target_pairs={{0,2},{1,3},{2,0},{3,1},{4,6},{5,7},{6,4},{7,5},{8,10},{9,11},{10,... | collective-permute-start | bytes 3145736 | tf_op jit(solution)/shard_map/ppermute | solution.py:108
  5.0 26.8 %collective-permute-start.6 = (bf16[4,128,1024]{2,1,0:T(8,128)(2,1)}, bf16[4,128,1024]{2,1,0:T(8,128)(2,1)}, u32[]{:S(2)}, u32[]{:S(2)}) collective-permute-start(bf16[4,128,1024]{2,1,0:T(8,128)(2,1)} %own_ref.1), channel_id=1, source_target_pairs={{2,6},{12,8},{3,7},{13,9},{6,14},{8,0},{7,15},{9,1},{18,22},{28,24... | collective-permute-start | bytes 3145736 | tf_op jit(solution)/shard_map/ppermute | solution.py:108
  27.0 9.5 %copy-start.3 = (bf16[4,128,1024]{2,1,0:T(8,128)(2,1)}, bf16[4,128,1024]{2,1,0:T(8,128)(2,1)S(1)}, u32[]{:S(2)}) copy-start(bf16[4,128,1024]{2,1,0:T(8,128)(2,1)S(1)} %collective-permute-done.3) | copy-start | bytes 3145732
  34.6 25.0 %collective-permute-start.7 = (bf16[4,128,1024]{2,1,0:T(8,128)(2,1)}, bf16[4,128,1024]{2,1,0:T(8,128)(2,1)}, u32[]{:S(2)}, u32[]{:S(2)}) collective-permute-start(bf16[4,128,1024]{2,1,0:T(8,128)(2,1)} %get-tuple-element.42), channel_id=1, source_target_pairs={{0,2},{1,3},{2,0},{3,1},{12,14},{13,15},{14,12},{15,13},{16,18},{1... | collective-permute-start | bytes 3145736 | tf_op jit(solution)/shard_map/ppermute | solution.py:108
  36.5 28.1 %collective-permute-start.4 = (bf16[4,128,1024]{2,1,0:T(8,128)(2,1)}, bf16[4,128,1024]{2,1,0:T(8,128)(2,1)S(1)}, u32[]{:S(2)}, u32[]{:S(2)}) collective-permute-start(bf16[4,128,1024]{2,1,0:T(8,128)(2,1)} %get-tuple-element.43), channel_id=1, source_target_pairs={{0,4},{14,10},{1,5},{15,11},{4,8},{10,6},{5,9},{11,7},{8,12},{6,2}... | collective-permute-start | bytes 3145736 | tf_op jit(solution)/shard_map/ppermute | solution.py:108
  37.9 30.7 %collective-permute-start.9 = (bf16[4,128,1024]{2,1,0:T(8,128)(2,1)}, bf16[4,128,1024]{2,1,0:T(8,128)(2,1)}, u32[]{:S(2)}, u32[]{:S(2)}) collective-permute-start(bf16[4,128,1024]{2,1,0:T(8,128)(2,1)} %collective-permute-done.6), channel_id=1, source_target_pairs={{6,14},{8,0},{7,15},{9,1},{22,30},{24,16},{23,31},{25,17}} | collective-permute-start | bytes 3145736 | tf_op jit(solution)/shard_map/ppermute | solution.py:108
  62.0 14.1 %collective-permute-start.13 = (bf16[4,128,512]{2,1,0:T(8,128)(2,1)S(1)}, bf16[4,128,512]{2,1,0:T(8,128)(2,1)}, u32[]{:S(2)}, u32[]{:S(2)}) collective-permute-start(bf16[4,128,512]{2,1,0:T(8,128)(2,1)S(1)} %get-tuple-element.36), channel_id=1, source_target_pairs={{10,14},{4,0},{11,15},{5,1},{12,8},{2,6},{13,9},{3,7},{26,30},{20,... | collective-permute-start | bytes 1572872 | tf_op jit(solution)/shard_map/ppermute | solution.py:108
  63.3 24.0 %collective-permute-start.8 = (bf16[4,128,512]{2,1,0:T(8,128)(2,1)}, bf16[4,128,512]{2,1,0:T(8,128)(2,1)}, u32[]{:S(2)}, u32[]{:S(2)}) collective-permute-start(bf16[4,128,512]{2,1,0:T(8,128)(2,1)} %get-tuple-element.37), channel_id=1, source_target_pairs={{10,14},{4,0},{11,15},{5,1},{12,8},{2,6},{13,9},{3,7},{26,30},{20,... | collective-permute-start | bytes 1572872 | tf_op jit(solution)/shard_map/ppermute | solution.py:108
  65.7 24.6 %collective-permute-start.12 = (bf16[4,128,512]{2,1,0:T(8,128)(2,1)}, bf16[4,128,512]{2,1,0:T(8,128)(2,1)}, u32[]{:S(2)}, u32[]{:S(2)}) collective-permute-start(bf16[4,128,512]{2,1,0:T(8,128)(2,1)} %get-tuple-element.40), channel_id=1, source_target_pairs={{4,8},{10,6},{5,9},{11,7},{8,12},{6,2},{9,13},{7,3},{20,24},{26,22... | collective-permute-start | bytes 1572872 | tf_op jit(solution)/shard_map/ppermute | solution.py:108
  67.1 23.2 %collective-permute-start.5 = (bf16[4,128,512]{2,1,0:T(8,128)(2,1)}, bf16[4,128,512]{2,1,0:T(8,128)(2,1)}, u32[]{:S(2)}, u32[]{:S(2)}) collective-permute-start(bf16[4,128,512]{2,1,0:T(8,128)(2,1)} %get-tuple-element.41), channel_id=1, source_target_pairs={{4,8},{10,6},{5,9},{11,7},{8,12},{6,2},{9,13},{7,3},{20,24},{26,22... | collective-permute-start | bytes 1572872 | tf_op jit(solution)/shard_map/ppermute | solution.py:108
  70.9 21.6 %collective-permute-start.14 = (bf16[4,128,512]{2,1,0:T(8,128)(2,1)}, bf16[4,128,512]{2,1,0:T(8,128)(2,1)}, u32[]{:S(2)}, u32[]{:S(2)}) collective-permute-start(bf16[4,128,512]{2,1,0:T(8,128)(2,1)} %get-tuple-element.38), channel_id=1, source_target_pairs={{14,12},{15,13},{0,2},{1,3},{30,28},{31,29},{16,18},{17,19}} | collective-permute-start | bytes 1572872 | tf_op jit(solution)/shard_map/ppermute | solution.py:108
  76.1 18.5 %collective-permute-start.10 = (bf16[4,128,512]{2,1,0:T(8,128)(2,1)}, bf16[4,128,512]{2,1,0:T(8,128)(2,1)}, u32[]{:S(2)}, u32[]{:S(2)}) collective-permute-start(bf16[4,128,512]{2,1,0:T(8,128)(2,1)} %get-tuple-element.39), channel_id=1, source_target_pairs={{14,12},{15,13},{0,2},{1,3},{30,28},{31,29},{16,18},{17,19}} | collective-permute-start | bytes 1572872 | tf_op jit(solution)/shard_map/ppermute | solution.py:108
  87.3 18.6 %collective-permute-start = (bf16[4,128,1024]{2,1,0:T(8,128)(2,1)}, bf16[4,128,1024]{2,1,0:T(8,128)(2,1)S(1)}, u32[]{:S(2)}, u32[]{:S(2)}) collective-permute-start(bf16[4,128,1024]{2,1,0:T(8,128)(2,1)} %own_ref.1), channel_id=1, source_target_pairs={{0,1},{1,0},{2,3},{3,2},{4,5},{5,4},{6,7},{7,6},{8,9},{9,8},{10,11... | collective-permute-start | bytes 3145736 | tf_op jit(solution)/shard_map/ppermute | solution.py:108
  90.3 15.6 %collective-permute-start.2 = (bf16[4,128,1024]{2,1,0:T(8,128)(2,1)S(1)}, bf16[4,128,1024]{2,1,0:T(8,128)(2,1)S(1)}, u32[]{:S(2)}, u32[]{:S(2)}) collective-permute-start(bf16[4,128,1024]{2,1,0:T(8,128)(2,1)S(1)} %collective-permute-done.1.other_ref), channel_id=1, source_target_pairs={{0,1},{1,0},{2,3},{3,2},{4,5},{5,4},{6,7},{7,6},{8,9},{9,8},{10,11... | collective-permute-start | bytes 3145736 | tf_op jit(solution)/shard_map/ppermute | solution.py:108
  96.9 14.6 %collective-permute-start.15 = (bf16[2,4,128,512]{3,2,1,0:T(8,128)(2,1)S(1)}, bf16[2,4,128,512]{3,2,1,0:T(8,128)(2,1)S(1)}, u32[]{:S(2)}, u32[]{:S(2)}) collective-permute-start(bf16[2,4,128,512]{3,2,1,0:T(8,128)(2,1)S(1)} %pad_maximum_fusion.1), channel_id=1, source_target_pairs={{0,1},{1,0},{2,3},{3,2},{4,5},{5,4},{6,7},{7,6},{8,9},{9,8},{10,11... | collective-permute-start | bytes 3145736 | tf_op jit(solution)/shard_map/ppermute | solution.py:108
  111.3 17.3 %collective-permute-start.11 = (bf16[2,4,128,512]{3,2,1,0:T(8,128)(2,1)S(1)}, bf16[2,4,128,512]{3,2,1,0:T(8,128)(2,1)S(1)}, u32[]{:S(2)}, u32[]{:S(2)}) collective-permute-start(bf16[2,4,128,512]{3,2,1,0:T(8,128)(2,1)S(1)} %pad_maximum_fusion), channel_id=1, source_target_pairs={{0,1},{1,0},{2,3},{3,2},{4,5},{5,4},{6,7},{7,6},{8,9},{9,8},{10,11... | collective-permute-start | bytes 3145736 | tf_op jit(solution)/shard_map/ppermute | solution.py:108

commit v2 on v0

--- a/solution.py
+++ b/solution.py
@@ -1,10 +1,19 @@
+import functools
+
 import jax
 import jax.numpy as jnp
 from jax import lax
+from jax.experimental import pallas as pl
+from jax.experimental.pallas import tpu as pltpu
 from jax.sharding import PartitionSpec as P
 
 SLACK = 32
 LAGMAX = 64
+AXES = ("feat", "tm", "sub")
+VMEM_LIMIT = 60 * 1024 * 1024
+TILE = 512
+DEPTH = 2
+ROWS_TILE = 1024
 
 
 def spread(x, axis, root):
@@ -42,7 +51,7 @@
     return jnp.einsum("kt,ktf->f", mask, series, preferred_element_type=jnp.float32) / frame_count
 
 
-def local(frames, window_starts, lag_frames):
+def general(frames, window_starts, lag_frames):
     halves = lax.all_gather(frames, "sub", axis=2, tiled=True)
     row_data = lax.all_gather(halves, "tm", axis=1, tiled=True)
     stored = row_data.shape[1]
@@ -70,10 +79,311 @@
     return (covariance_zero, covariance_lag)
 
 
+def rank(s, x, c):
+    return ((3 - s if x else s) * 2 + x) * 2 + c
+
+
+def home(s, x):
+    return (3 - s if x else s) % 2
+
+
+def hops(links):
+    pairs = []
+    for s, d, b in links:
+        for x in range(2):
+            to = rank(d, x, home(b, x)) if d >= 0 else rank(3 - s, 1 - x, home(b, x))
+            pairs.append((rank(s, x, home(b, x)), to))
+    return pairs
+
+
+PLACES = [(s, x) for s in range(4) for x in range(2)]
+CORES = [(rank(s, x, c), rank(s, x, 1 - c)) for s, x in PLACES for c in range(2)]
+FROM_HOME = [(rank(s, x, home(s, x)), rank(s, x, 1 - home(s, x))) for s, x in PLACES]
+CROSS_HOME = [(rank(s, x, home(s, x)), rank(3 - s, 1 - x, home(s, x))) for s, x in PLACES]
+CROSS_AWAY = [(rank(s, x, 1 - home(s, x)), rank(3 - s, 1 - x, home(s, x))) for s, x in PLACES]
+NEAR_1 = hops([(0, 1, 0), (1, 2, 1), (2, 3, 2)])
+FAR_1 = hops([(3, 2, 3), (2, 0, 2)])
+NEAR_2 = hops([(0, 1, 0), (1, 2, 0), (2, 3, 1), (3, -1, 2)])
+FAR_2 = hops([(2, 0, 3), (0, -1, 2)])
+NEAR_3 = hops([(1, 2, 0), (2, 3, 0)])
+BACK_3 = hops([(1, 0, 1), (3, 2, 1), (0, -1, 3)])
+
+
+def send(x, pairs):
+    return lax.ppermute(x, AXES, pairs)
+
+
+def after(value, *others):
+    return lax.optimization_barrier((value, *others))[0]
+
+
+def dot(left, right):
+    return jnp.dot(left, right, preferred_element_type=jnp.float32)
+
+
+def rows_kernel(
+    starts_ref, lags_ref, x_ref, count_ref, parts, zero_ref, late_ref, mean_ref, moves_ref, *, window
+):
+    trajectories, half = parts[0][0].shape[0], parts[0][0].shape[1]
+    stored = 2 * half
+    p, i = pl.program_id(0), pl.program_id(1)
+
+    @pl.when((p == 0) & (i == 0))
+    def _():
+        def instant(axis):
+            n = lax.broadcasted_iota(jnp.int32, (stored, stored), axis)
+            return jnp.where(x_ref[0] == 0, n, lax.rem(n + half, stored))
+
+        frame, column = instant(0), instant(1)
+        for k in range(trajectories):
+            start, lag = starts_ref[k], lags_ref[k]
+            kept = (frame >= start) & (frame < start + window - lag)
+            for n, ahead in enumerate((0, lag)):
+                moves_ref[k, :, n * stored : (n + 1) * stored] = jnp.where(
+                    kept & (column == frame + ahead), 1.0, 0.0
+                ).astype(jnp.bfloat16)
+
+    def fill(own_ref, cross_refs):
+        total = None
+        for k in range(trajectories):
+            series = jnp.concatenate([own_ref[k], cross_refs[0][k] + cross_refs[1][k]], axis=0)
+            moved = lax.dot_general(
+                series,
+                moves_ref[k],
+                (((0,), (0,)), ((), ())),
+                preferred_element_type=jnp.float32,
+            )
+            total = moved[:, :stored] if total is None else total + moved[:, :stored]
+            moved = moved.astype(jnp.bfloat16)
+            for n, ref in enumerate((zero_ref, late_ref)):
+                for side in range(2):
+                    to, at = (side * trajectories + k) * half, n * stored + side * half
+                    ref[:, to : to + half] = moved[:, at : at + half]
+        mean = jnp.sum(total, axis=1, keepdims=True) / count_ref[0]
+        mean_ref[...] = jnp.broadcast_to(mean, mean_ref.shape)
+
+    for n, (own_ref, *cross_refs) in enumerate(parts):
+        pl.when(p == n)(functools.partial(fill, own_ref, cross_refs))
+
+
+def prepare_rows(part, starts, lags, x, count, arrays, window):
+    trajectories, half, features = arrays[0][0].shape
+    tile = min(ROWS_TILE, features)
+    steps = features // tile
+    depth = trajectories * 2 * half
+    row = jax.ShapeDtypeStruct((2 * features, depth), jnp.bfloat16)
+    mean = jax.ShapeDtypeStruct((2 * features, 128), jnp.float32)
+
+    def spot(p, i, part_ref, *_):
+        return (jnp.where(p == 0, part_ref[0], 1 - part_ref[0]) * steps + i, 0)
+
+    def body(part_ref, starts_ref, lags_ref, x_ref, count_ref, *refs):
+        rows_kernel(
+            starts_ref, lags_ref, x_ref, count_ref, (refs[:3], refs[3:6]), *refs[6:], window=window
+        )
+
+    return pl.pallas_call(
+        body,
+        out_shape=(row, row, mean),
+        grid_spec=pltpu.PrefetchScalarGridSpec(
+            num_scalar_prefetch=5,
+            grid=(2, steps),
+            in_specs=[
+                pl.BlockSpec((trajectories, half, tile), lambda p, i, *_: (0, 0, jnp.where(p == 0, i, steps - 1)))
+            ]
+            * 3
+            + [
+                pl.BlockSpec((trajectories, half, tile), lambda p, i, *_: (0, 0, jnp.where(p == 0, 0, i)))
+            ]
+            * 3,
+            out_specs=[
+                pl.BlockSpec((tile, depth), spot),
+                pl.BlockSpec((tile, depth), spot),
+                pl.BlockSpec((tile, 128), spot),
+            ],
+            scratch_shapes=[pltpu.VMEM((trajectories, 2 * half, 4 * half), jnp.bfloat16)],
+        ),
+        compiler_params=pltpu.CompilerParams(vmem_limit_bytes=VMEM_LIMIT),
+        cost_estimate=pl.CostEstimate(
+            flops=0, bytes_accessed=28 * arrays[0][0].size, transcendentals=0
+        ),
+        name="rows",
+    )(part, starts, lags, x, count, *arrays[0], *arrays[1])
+
+
+def product_kernel(part_ref, pick_ref, count_ref, masks_ref, mean_ref, zero_ref, late_ref, *refs, n_pieces):
+    pieces = refs[:n_pieces]
+    cov_zero_ref, cov_late_ref, left_ref, columns_ref, made_ref, arrived, fetched, stored = refs[-8:]
+    half, width = columns_ref.shape[0] // 2, columns_ref.shape[1]
+    tile = left_ref.shape[2]
+    steps = left_ref.shape[1]
+    depth_out = made_ref.shape[0]
+    scale = 1.0 / count_ref[0]
+    first = pl.multiple_of(part_ref[0] * width, width)
+
+    def piece_copy(piece, side):
+        return pltpu.make_async_copy(
+            piece, columns_ref.at[pl.ds(side * half, half)], arrived.at[side]
+        )
+
+    def left_copy(n, i):
+        return pltpu.make_async_copy(
+            (zero_ref, late_ref)[n].at[pl.ds(i * tile, tile)], left_ref.at[n, i], fetched.at[n, i]
+        )
+
+    def out_copy(n, i):
+        slot = lax.rem(i, depth_out)
+        return pltpu.make_async_copy(
+            made_ref.at[slot, n],
+            (cov_zero_ref, cov_late_ref)[n].at[pl.ds(i * tile, tile), pl.ds(first, width)],
+            stored.at[slot, n],
+        )
+
+    for side in range(2):
+        for m, piece in enumerate(pieces):
+
+            @pl.when(pick_ref[side] == m)
+            def _():
+                piece_copy(piece, side).start()
+
+    def fetch(i):
+        for n in range(2):
+            left_copy(n, i).start()
+
+    fetch(0)
+    for side in range(2):
+        piece_copy(pieces[0], side).wait()
+    means = dot(masks_ref[...], columns_ref[...]) * scale
+
+    def step(i, carry):
+        @pl.when(i + 1 < steps)
+        def _():
+            fetch(i + 1)
+
+        row_mean = mean_ref[pl.ds(pl.multiple_of(i * tile, tile), tile), :1]
+        for n in range(2):
+            left_copy(n, i).wait()
+
+            @pl.when(i >= depth_out)
+            def _():
+                out_copy(n, i - depth_out).wait()
+
+            total = dot(left_ref[n, i], columns_ref[...])
+            made_ref[lax.rem(i, depth_out), n] = total * scale - row_mean * means[8 * n : 8 * n + 1]
+            out_copy(n, i).start()
+        return carry
+
+    lax.fori_loop(0, steps, step, 0)
+    for i in range(max(0, steps - depth_out), steps):
+        for n in range(2):
+            out_copy(n, i).wait()
+
+
+def product(part, pick, count, masks, rows, pieces, before):
+    zero, late, means = rows
+    height, depth = zero.shape
+    width = pieces[0].shape[-1]
+    tile = min(TILE, height)
+    steps = height // tile
+    out = jax.ShapeDtypeStruct((height, 2 * width), jnp.float32)
+    anywhere = pl.BlockSpec(memory_space=pl.ANY)
+    return pl.pallas_call(
+        functools.partial(product_kernel, n_pieces=len(pieces)),
+        out_shape=(out, out),
+        grid_spec=pltpu.PrefetchScalarGridSpec(
+            num_scalar_prefetch=3,
+            grid=(1,),
+            in_specs=[
+                pl.BlockSpec((16, depth), lambda i, *_: (0, 0)),
+                pl.BlockSpec((height, 128), lambda i, *_: (0, 0)),
+            ]
+            + [anywhere] * (2 + len(pieces) + len(before)),
+            out_specs=[anywhere] * 2,
+            scratch_shapes=[
+                pltpu.VMEM((2, steps, tile, depth), jnp.bfloat16),
+                pltpu.VMEM((depth, width), jnp.bfloat16),
+                pltpu.VMEM((DEPTH, 2, tile, width), jnp.float32),
+                pltpu.SemaphoreType.DMA((2,)),
+                pltpu.SemaphoreType.DMA((2, steps)),
+                pltpu.SemaphoreType.DMA((DEPTH, 2)),
+            ],
+        ),
+        input_output_aliases={7 + len(pieces) + i: i for i in range(len(before))},
+        compiler_params=pltpu.CompilerParams(vmem_limit_bytes=VMEM_LIMIT),
+        cost_estimate=pl.CostEstimate(
+            flops=4 * height * depth * width,
+            bytes_accessed=4 * height * depth + 8 * height * width,
+            transcendentals=0,
+        ),
+        name="covariances",
+    )(part, pick, count, masks, means, zero, late, *pieces, *before)
+
+
+def line_of_four(frames, window_starts, lag_frames):
+    trajectories, half, features = frames.shape
+    stored = 2 * half
+    window = stored - SLACK
+    z, x, c = (lax.axis_index(a) for a in AXES)
+    s = jnp.where(x == 1, 3 - z, z)
+    count = (trajectories * window - jnp.sum(lag_frames)).astype(jnp.float32).reshape(1)
+    plane = x.astype(jnp.int32).reshape(1)
+    part = c.astype(jnp.int32).reshape(1)
+
+    base_mask, lag_mask = window_masks(window_starts, lag_frames, stored)
+
+    def relative(mask):
+        low, high = mask[:, :half].reshape(-1), mask[:, half:].reshape(-1)
+        return jnp.where(x == 0, jnp.concatenate([low, high]), jnp.concatenate([high, low]))
+
+    masks = jnp.concatenate(
+        [
+            jnp.broadcast_to(relative(m)[None, :], (8, trajectories * stored))
+            for m in (base_mask, lag_mask)
+        ]
+    )
+
+    picks = jnp.array([[[0, 2, 3, 4], [1, 3, 4, 5]], [[5, 0, 2, 3], [3, 1, 5, 6]]], jnp.int32)
+    pick = picks[jnp.where(c == x, 0, 1), :, s]
+
+    own = frames
+    cross_a = send(own, CROSS_HOME)
+    near1_a, far1_a = send(own, NEAR_1), send(own, FAR_1)
+    sib = send(own, CORES)
+    sib_b = sib
+    near1_b, far1_b = send(sib_b, NEAR_1), send(sib_b, FAR_1)
+    cross_b = send(after(own, cross_a), CROSS_AWAY)
+    near2_a, far2_a = send(jnp.where(s == 0, cross_a, near1_a), NEAR_2), send(far1_a, FAR_2)
+    sib_cross_a, sib_cross_b = send(cross_a, FROM_HOME), send(cross_b, FROM_HOME)
+    pick, masks = lax.optimization_barrier((pick, masks, near1_a))[:2]
+    near3_a, back_a = send(near2_a, NEAR_3), send(jnp.where(s == 1, own, far2_a), BACK_3)
+    near2_b, far2_b = send(jnp.where(s == 0, cross_b, near1_b), NEAR_2), send(far1_b, FAR_2)
+    rows = prepare_rows(
+        part,
+        window_starts,
+        lag_frames,
+        plane,
+        count,
+        ((own, cross_a, sib_cross_b), (sib, cross_b, sib_cross_a)),
+        window,
+    )
+    near2_b, far2_b, *rows = lax.optimization_barrier((near2_b, far2_b, *rows))
+    near3_b, back_b = send(near2_b, NEAR_3), send(jnp.where(s == 1, sib, far2_b), BACK_3)
+
+    outs = ()
+    for where_to, pieces in (
+        (part, (own, cross_a, near1_a, near2_a, near3_a, back_a, far2_a)),
+        (1 - part, (sib, cross_b, near1_b, near2_b, near3_b, back_b, far2_b)),
+    ):
+        pieces = [piece.reshape(trajectories * half, features) for piece in pieces]
+        outs = product(where_to, pick, count, masks, rows, pieces, outs)
+    return outs
+
+
 def solution(mesh):
     placed = (P("groups", "tm", ("feat", "sub")), P("groups"), P("groups"))
+    line = mesh.shape["feat"] == 4 and mesh.shape["tm"] == 2 and mesh.shape["sub"] == 2
     return jax.shard_map(
-        local,
+        line_of_four if line else general,
         mesh=mesh,
         in_specs=placed,
         out_specs=(P(("groups", "feat"), ("tm", "sub")), P(("groups", "feat"), ("tm", "sub"))),

time: 301 us -> 112 us (0.37)
  the two profiles are of different devices: /device:TPU:1 before, /device:TPU:2 now
where the time goes in v2:
time: 112 us; the launch traced here: 111 us
  starting transfers between devices  46.8 us (42%)
  Pallas kernels  40.5 us (36%)
  waiting for transfers between devices  10.1 us (9%)
  other arithmetic  9.93 us (9%)
  local copies, waits for them, and re-layouts  2.6 us (2%)
  between operations  1.52 us (1%)
    ppermute x17, starting transfers between devices, send(): return lax.ppermute(x, AXES, pairs)  46.8 us
    pallas_call x2, Pallas kernels, product(): pl.pallas_call(functools.partial(product_kernel, n_pieces=len(pieces)), o...  31.5 us
    ppermute x17, waiting for transfers between devices, send(): return lax.ppermute(x, AXES, pairs)  10.1 us
    pallas_call x1, Pallas kernels, prepare_rows(): pl.pallas_call(body, out_shape=(row, row, mean), grid_spec=pltpu.Prefetch...  8.96 us
    select_n x1, other arithmetic, line_of_four(): jnp.where(s == 1, sib, far2_b)  2.33 us
    select_n x1, other arithmetic, line_of_four(): jnp.where(s == 1, own, far2_a)  2.31 us
  transfers between devices with their start and end apart: 17, of which 2 were waited for; matrix products, arithmetic and copies ran while one was open for 10% of the time, Pallas kernels for 22%

profile of v2, /device:TPU:2, one launch (start us, length us, event | category | flops | bytes accessed | tf_op | source)
XLA Modules:
  0.0 111.4 jit_solution(5181448825689725242)
XLA Ops:
  0.7 1.9 %collective-permute-start.1 = (bf16[4,128,1024]{2,1,0:T(8,128)(2,1)}, bf16[4,128,1024]{2,1,0:T(8,128)(2,1)}, u32[]{:S(2)}, u32[]{:S(2)}) collective-permute-start(bf16[4,128,1024]{2,1,0:T(8,128)(2,1)} %refs_0_.1), channel_id=1, source_target_pairs={{0,2},{15,13},{5,7},{10,8},{8,10},{7,5},{13,15},{2,0},{16,18},{31,... | collective-permute-start | bytes 3145736 | tf_op jit(solution)/shard_map/ppermute | solution.py:113
  2.6 4.2 %collective-permute-start.14 = (bf16[4,128,1024]{2,1,0:T(8,128)(2,1)}, bf16[4,128,1024]{2,1,0:T(8,128)(2,1)}, u32[]{:S(2)}, u32[]{:S(2)}) collective-permute-start(bf16[4,128,1024]{2,1,0:T(8,128)(2,1)} %refs_0_.1), channel_id=1, source_target_pairs={{13,9},{2,6},{8,0},{7,15},{29,25},{18,22},{24,16},{23,31}} | collective-permute-start | bytes 3145736 | tf_op jit(solution)/shard_map/ppermute | solution.py:113
  6.9 1.7 %collective-permute-start = (bf16[4,128,1024]{2,1,0:T(8,128)(2,1)}, bf16[4,128,1024]{2,1,0:T(8,128)(2,1)}, u32[]{:S(2)}, u32[]{:S(2)}) collective-permute-start(bf16[4,128,1024]{2,1,0:T(8,128)(2,1)} %refs_0_.1), channel_id=1, source_target_pairs={{0,4},{15,11},{5,9},{10,6},{8,12},{7,3},{16,20},{31,27},{21,25},{2... | collective-permute-start | bytes 3145736 | tf_op jit(solution)/shard_map/ppermute | solution.py:113
  9.3 8.4 %collective-permute-done.1.refs_1_ = bf16[4,128,1024]{2,1,0:T(8,128)(2,1)} collective-permute-done((bf16[4,128,1024]{2,1,0:T(8,128)(2,1)}, bf16[4,128,1024]{2,1,0:T(8,128)(2,1)}, u32[]{:S(2)}, u32[]{:S(2)}) %collective-permute-start.1) | collective-permute-done | bytes 1048608 | tf_op jit(solution)/shard_map/ppermute | solution.py:113
  17.7 1.3 %collective-permute-start.2 = (bf16[4,128,1024]{2,1,0:T(8,128)(2,1)}, bf16[4,128,1024]{2,1,0:T(8,128)(2,1)S(1)}, u32[]{:S(2)}, u32[]{:S(2)}) collective-permute-start(bf16[4,128,1024]{2,1,0:T(8,128)(2,1)} %refs_0_.1), channel_id=1, source_target_pairs={{1,2},{14,13},{4,7},{11,8},{9,10},{6,5},{12,15},{3,0},{17,18},{30,... | collective-permute-start | bytes 3145736 | tf_op jit(solution)/shard_map/ppermute | solution.py:113
  19.0 4.9 %collective-permute-start.6 = (bf16[4,128,1024]{2,1,0:T(8,128)(2,1)S(1)}, bf16[4,128,1024]{2,1,0:T(8,128)(2,1)}, u32[]{:S(2)}, u32[]{:S(2)}) collective-permute-start(bf16[4,128,1024]{2,1,0:T(8,128)(2,1)S(1)} %collective-permute-done.3.refs_3_), channel_id=1, source_target_pairs={{13,9},{2,6},{8,0},{7,15},{29,25},{18,22},{24,16},{23,31}} | collective-permute-start | bytes 3145736 | tf_op jit(solution)/shard_map/ppermute | solution.py:113
  23.9 1.3 %collective-permute-start.15 = (bf16[4,128,1024]{2,1,0:T(8,128)(2,1)}, bf16[4,128,1024]{2,1,0:T(8,128)(2,1)}, u32[]{:S(2)}, u32[]{:S(2)}) collective-permute-start(bf16[4,128,1024]{2,1,0:T(8,128)(2,1)} %collective-permute-done.14), channel_id=1, source_target_pairs={{9,1},{6,14},{0,2},{15,13},{25,17},{22,30},{16,18},{31,29}} | collective-permute-start | bytes 3145736 | tf_op jit(solution)/shard_map/ppermute | solution.py:113
  25.3 1.3 %broadcast_select_fusion.2 = bf16[4,128,1024]{2,1,0:T(8,128)(2,1)S(1)} fusion(bf16[4,128,1024]{2,1,0:T(8,128)(2,1)} %collective-permute-done.1.refs_1_, bf16[4,128,1024]{2,1,0:T(8,128)(2,1)} %collective-permute-done, pred[]{:T(512)S(6)} %eq.21), kind=kLoop, calls=%fused_computation.2 | loop fusion | flops 524288 | bytes 3145729 | tf_op jit(solution)/shard_map/jit(_where)/select_n | solution.py:355
  26.6 1.3 %collective-permute-start.12 = (bf16[4,128,1024]{2,1,0:T(8,128)(2,1)S(1)}, bf16[4,128,1024]{2,1,0:T(8,128)(2,1)}, u32[]{:S(2)}, u32[]{:S(2)}) collective-permute-start(bf16[4,128,1024]{2,1,0:T(8,128)(2,1)S(1)} %broadcast_select_fusion.2), channel_id=1, source_target_pairs={{0,4},{15,11},{4,8},{11,7},{9,13},{6,2},{12,14},{3,1},{16,20},{31,... | collective-permute-start | bytes 3145736 | tf_op jit(solution)/shard_map/ppermute | solution.py:113
  27.9 11.8 %collective-permute-start.9 = (bf16[4,128,1024]{2,1,0:T(8,128)(2,1)}, bf16[4,128,1024]{2,1,0:T(8,128)(2,1)S(1)}, u32[]{:S(2)}, u32[]{:S(2)}) collective-permute-start(bf16[4,128,1024]{2,1,0:T(8,128)(2,1)} %collective-permute-done.1.refs_1_), channel_id=1, source_target_pairs={{0,1},{15,14},{5,4},{10,11},{8,9},{7,6},{13,12},{2,3},{16,17},{31,... | collective-permute-start | bytes 3145736 | tf_op jit(solution)/shard_map/ppermute | solution.py:113
  39.7 1.3 %fusion.4 = (s32[4]{0:T(128)S(1)}, s32[4]{0:T(128)S(1)}, s32[]{:T(128)}, s32[4]{0:T(128)S(1)}) fusion(s32[4]{0:T(128)} %lags_ref.1, s32[4]{0:T(128)} %starts_ref.1), kind=kLoop, calls=%fused_computation.21 | loop fusion | flops 15 | bytes 84 | tf_op jit(solution)/shard_map/sub | solution.py:29
  41.0 1.2 %broadcast_select_fusion.3 = bf16[4,128,1024]{2,1,0:T(8,128)(2,1)} fusion(bf16[4,128,1024]{2,1,0:T(8,128)(2,1)S(1)} %collective-permute-done.2.refs_4_, bf16[4,128,1024]{2,1,0:T(8,128)(2,1)S(1)} %collective-permute-done.4, pred[]{:T(512)S(6)} %eq.21), kind=kLoop, calls=%fused_computation.3 | loop fusion | flops 524288 | bytes 3145729 | tf_op jit(solution)/shard_map/jit(_where)/select_n | solution.py:359
  42.3 1.3 %collective-permute-start.5 = (bf16[4,128,1024]{2,1,0:T(8,128)(2,1)}, bf16[4,128,1024]{2,1,0:T(8,128)(2,1)}, u32[]{:S(2)}, u32[]{:S(2)}) collective-permute-start(bf16[4,128,1024]{2,1,0:T(8,128)(2,1)} %broadcast_select_fusion.3), channel_id=1, source_target_pairs={{0,4},{15,11},{4,8},{11,7},{9,13},{6,2},{12,14},{3,1},{16,20},{31,... | collective-permute-start | bytes 3145736 | tf_op jit(solution)/shard_map/ppermute | solution.py:113
  43.6 3.2 %collective-permute-start.8 = (bf16[4,128,1024]{2,1,0:T(8,128)(2,1)S(1)}, bf16[4,128,1024]{2,1,0:T(8,128)(2,1)}, u32[]{:S(2)}, u32[]{:S(2)}) collective-permute-start(bf16[4,128,1024]{2,1,0:T(8,128)(2,1)S(1)} %collective-permute-done.2.refs_4_), channel_id=1, source_target_pairs={{0,1},{15,14},{5,4},{10,11},{8,9},{7,6},{13,12},{2,3},{16,17},{31,... | collective-permute-start | bytes 3145736 | tf_op jit(solution)/shard_map/ppermute | solution.py:113
  46.7 1.3 %collective-permute-start.7 = (bf16[4,128,1024]{2,1,0:T(8,128)(2,1)}, bf16[4,128,1024]{2,1,0:T(8,128)(2,1)}, u32[]{:S(2)}, u32[]{:S(2)}) collective-permute-start(bf16[4,128,1024]{2,1,0:T(8,128)(2,1)} %collective-permute-done.6), channel_id=1, source_target_pairs={{9,1},{6,14},{0,2},{15,13},{25,17},{22,30},{16,18},{31,29}} | collective-permute-start | bytes 3145736 | tf_op jit(solution)/shard_map/ppermute | solution.py:113
  48.8 2.3 %broadcast_select_fusion = bf16[4,128,1024]{2,1,0:T(8,128)(2,1)} fusion(bf16[4,128,1024]{2,1,0:T(8,128)(2,1)} %refs_0_.1, bf16[4,128,1024]{2,1,0:T(8,128)(2,1)} %collective-permute-done.15, pred[]{:T(512)S(6)} %eq.22), kind=kLoop, calls=%fused_computation | loop fusion | flops 524288 | bytes 3145729 | tf_op jit(solution)/shard_map/jit(_where)/select_n | solution.py:358
  51.1 8.2 %collective-permute-start.16 = (bf16[4,128,1024]{2,1,0:T(8,128)(2,1)}, bf16[4,128,1024]{2,1,0:T(8,128)(2,1)}, u32[]{:S(2)}, u32[]{:S(2)}) collective-permute-start(bf16[4,128,1024]{2,1,0:T(8,128)(2,1)} %broadcast_select_fusion), channel_id=1, source_target_pairs={{5,1},{10,14},{13,9},{2,6},{1,3},{14,12},{21,17},{26,30},{29,25},{... | collective-permute-start | bytes 3145736 | tf_op jit(solution)/shard_map/ppermute | solution.py:113
  59.3 1.6 %collective-permute-start.13 = (bf16[4,128,1024]{2,1,0:T(8,128)(2,1)}, bf16[4,128,1024]{2,1,0:T(8,128)(2,1)}, u32[]{:S(2)}, u32[]{:S(2)}) collective-permute-start(bf16[4,128,1024]{2,1,0:T(8,128)(2,1)} %collective-permute-done.12), channel_id=1, source_target_pairs={{4,8},{11,7},{8,12},{7,3},{20,24},{27,23},{24,28},{23,19}} | collective-permute-start | bytes 3145736 | tf_op jit(solution)/shard_map/ppermute | solution.py:113
  61.6 9.0 %rows.1 = (bf16[2048,1024]{1,0:T(8,128)(2,1)}, bf16[2048,1024]{1,0:T(8,128)(2,1)}, f32[2048,128]{1,0:T(8,128)}) custom-call(s32[1]{0:T(128)} %bitcast.part_ref, s32[4]{0:T(128)} %starts_ref.1, s32[4]{0:T(128)} %lags_ref.1, s32[1]{0:T(128)} %bitcast.7.x_ref, f32[1]{0:T(128)} %bitcast.6.count_ref, bf16[4,128,1024]{2,1,0:T(8,128)(2,1)} %refs_0_.1, ...), custom_call_target="tpu_custom_call" | custom-call | bytes 14680064 | tf_op jit(solution)/shard_map/rows/pallas_call | solution.py:185
  70.6 1.6 %collective-permute-done.7 = bf16[4,128,1024]{2,1,0:T(8,128)(2,1)} collective-permute-done((bf16[4,128,1024]{2,1,0:T(8,128)(2,1)}, bf16[4,128,1024]{2,1,0:T(8,128)(2,1)}, u32[]{:S(2)}, u32[]{:S(2)}) %collective-permute-start.7) | collective-permute-done | bytes 1048608 | tf_op jit(solution)/shard_map/ppermute | solution.py:113
  72.2 2.3 %broadcast_select_fusion.1 = bf16[4,128,1024]{2,1,0:T(8,128)(2,1)} fusion(bf16[4,128,1024]{2,1,0:T(8,128)(2,1)} %copy-done, bf16[4,128,1024]{2,1,0:T(8,128)(2,1)} %collective-permute-done.7, pred[]{:T(512)S(6)} %eq.22), kind=kLoop, calls=%fused_computation.1 | loop fusion | flops 524288 | bytes 3145729 | tf_op jit(solution)/shard_map/jit(_where)/select_n | solution.py:370
  74.6 1.3 %collective-permute-start.11 = (bf16[4,128,1024]{2,1,0:T(8,128)(2,1)}, bf16[4,128,1024]{2,1,0:T(8,128)(2,1)S(1)}, u32[]{:S(2)}, u32[]{:S(2)}) collective-permute-start(bf16[4,128,1024]{2,1,0:T(8,128)(2,1)} %broadcast_select_fusion.1), channel_id=1, source_target_pairs={{5,1},{10,14},{13,9},{2,6},{1,3},{14,12},{21,17},{26,30},{29,25},{... | collective-permute-start | bytes 3145736 | tf_op jit(solution)/shard_map/ppermute | solution.py:113
  78.5 15.8 %covariances.2 = (f32[2048,2048]{1,0:T(8,128)}, f32[2048,2048]{1,0:T(8,128)}) custom-call(s32[1]{0:T(128)} %bitcast.part_ref, s32[2]{0:T(128)} %dynamic-slice_bitcast_fusion.pick_ref, f32[1]{0:T(128)} %bitcast.6.count_ref, bf16[16,1024]{1,0:T(8,128)(2,1)} %pad_maximum_fusion.masks_ref, f32[2048,128]{1,0:T(8,128)} %get-tuple-element.21.mean_ref, ...), custom_call_target="tpu_custom_call" | custom-call | flops 8589934592 | bytes 25165824 | tf_op jit(solution)/shard_map/covariances/pallas_call | solution.py:290
  95.7 15.8 %covariances.3 = (f32[2048,2048]{1,0:T(8,128)}, f32[2048,2048]{1,0:T(8,128)}) custom-call(s32[1]{0:T(128)S(6)} %sub.13.part_ref, s32[2]{0:T(128)} %dynamic-slice_bitcast_fusion.pick_ref, f32[1]{0:T(128)} %bitcast.6.count_ref, bf16[16,1024]{1,0:T(8,128)(2,1)} %pad_maximum_fusion.masks_ref, ...), custom_call_target="tpu_custom_call", output_to_operand_aliasing={{0}: (14, {}), {1}: (15, {})} | custom-call | flops 8589934592 | bytes 25165824 | tf_op jit(solution)/shard_map/covariances/pallas_call | solution.py:290
  (39 shorter events, 5.5 us)
Async XLA Ops:
  0.6 7.9 %collective-permute-start.3 = (bf16[4,128,1024]{2,1,0:T(8,128)(2,1)}, bf16[4,128,1024]{2,1,0:T(8,128)(2,1)S(1)}, u32[]{:S(2)}, u32[]{:S(2)}) collective-permute-start(bf16[4,128,1024]{2,1,0:T(8,128)(2,1)} %refs_0_.1), channel_id=1, source_target_pairs={{0,1},{1,0},{14,15},{15,14},{4,5},{5,4},{10,11},{11,10},{8,9},{9,8... | collective-permute-start | bytes 3145736 | tf_op jit(solution)/shard_map/ppermute | solution.py:113
  0.7 17.0 %collective-permute-start.1 = (bf16[4,128,1024]{2,1,0:T(8,128)(2,1)}, bf16[4,128,1024]{2,1,0:T(8,128)(2,1)}, u32[]{:S(2)}, u32[]{:S(2)}) collective-permute-start(bf16[4,128,1024]{2,1,0:T(8,128)(2,1)} %refs_0_.1), channel_id=1, source_target_pairs={{0,2},{15,13},{5,7},{10,8},{8,10},{7,5},{13,15},{2,0},{16,18},{31,... | collective-permute-start | bytes 3145736 | tf_op jit(solution)/shard_map/ppermute | solution.py:113
  2.6 21.3 %collective-permute-start.14 = (bf16[4,128,1024]{2,1,0:T(8,128)(2,1)}, bf16[4,128,1024]{2,1,0:T(8,128)(2,1)}, u32[]{:S(2)}, u32[]{:S(2)}) collective-permute-start(bf16[4,128,1024]{2,1,0:T(8,128)(2,1)} %refs_0_.1), channel_id=1, source_target_pairs={{13,9},{2,6},{8,0},{7,15},{29,25},{18,22},{24,16},{23,31}} | collective-permute-start | bytes 3145736 | tf_op jit(solution)/shard_map/ppermute | solution.py:113
  6.9 18.4 %collective-permute-start = (bf16[4,128,1024]{2,1,0:T(8,128)(2,1)}, bf16[4,128,1024]{2,1,0:T(8,128)(2,1)}, u32[]{:S(2)}, u32[]{:S(2)}) collective-permute-start(bf16[4,128,1024]{2,1,0:T(8,128)(2,1)} %refs_0_.1), channel_id=1, source_target_pairs={{0,4},{15,11},{5,9},{10,6},{8,12},{7,3},{16,20},{31,27},{21,25},{2... | collective-permute-start | bytes 3145736 | tf_op jit(solution)/shard_map/ppermute | solution.py:113
  8.5 53.1 %copy-start = (bf16[4,128,1024]{2,1,0:T(8,128)(2,1)}, bf16[4,128,1024]{2,1,0:T(8,128)(2,1)S(1)}, u32[]{:S(2)}) copy-start(bf16[4,128,1024]{2,1,0:T(8,128)(2,1)S(1)} %collective-permute-done.3.refs_3_) | copy-start | bytes 3145732
  8.6 19.4 %collective-permute-start.4 = (bf16[4,128,1024]{2,1,0:T(8,128)(2,1)S(1)}, bf16[4,128,1024]{2,1,0:T(8,128)(2,1)S(1)}, u32[]{:S(2)}, u32[]{:S(2)}) collective-permute-start(bf16[4,128,1024]{2,1,0:T(8,128)(2,1)S(1)} %collective-permute-done.3.refs_3_), channel_id=1, source_target_pairs={{0,4},{15,11},{5,9},{10,6},{8,12},{7,3},{16,20},{31,27},{21,25},{2... | collective-permute-start | bytes 3145736 | tf_op jit(solution)/shard_map/ppermute | solution.py:113
  17.7 23.3 %collective-permute-start.2 = (bf16[4,128,1024]{2,1,0:T(8,128)(2,1)}, bf16[4,128,1024]{2,1,0:T(8,128)(2,1)S(1)}, u32[]{:S(2)}, u32[]{:S(2)}) collective-permute-start(bf16[4,128,1024]{2,1,0:T(8,128)(2,1)} %refs_0_.1), channel_id=1, source_target_pairs={{1,2},{14,13},{4,7},{11,8},{9,10},{6,5},{12,15},{3,0},{17,18},{30,... | collective-permute-start | bytes 3145736 | tf_op jit(solution)/shard_map/ppermute | solution.py:113
  19.0 24.5 %collective-permute-start.6 = (bf16[4,128,1024]{2,1,0:T(8,128)(2,1)S(1)}, bf16[4,128,1024]{2,1,0:T(8,128)(2,1)}, u32[]{:S(2)}, u32[]{:S(2)}) collective-permute-start(bf16[4,128,1024]{2,1,0:T(8,128)(2,1)S(1)} %collective-permute-done.3.refs_3_), channel_id=1, source_target_pairs={{13,9},{2,6},{8,0},{7,15},{29,25},{18,22},{24,16},{23,31}} | collective-permute-start | bytes 3145736 | tf_op jit(solution)/shard_map/ppermute | solution.py:113
  23.9 22.8 %collective-permute-start.15 = (bf16[4,128,1024]{2,1,0:T(8,128)(2,1)}, bf16[4,128,1024]{2,1,0:T(8,128)(2,1)}, u32[]{:S(2)}, u32[]{:S(2)}) collective-permute-start(bf16[4,128,1024]{2,1,0:T(8,128)(2,1)} %collective-permute-done.14), channel_id=1, source_target_pairs={{9,1},{6,14},{0,2},{15,13},{25,17},{22,30},{16,18},{31,29}} | collective-permute-start | bytes 3145736 | tf_op jit(solution)/shard_map/ppermute | solution.py:113
  26.6 32.7 %collective-permute-start.12 = (bf16[4,128,1024]{2,1,0:T(8,128)(2,1)S(1)}, bf16[4,128,1024]{2,1,0:T(8,128)(2,1)}, u32[]{:S(2)}, u32[]{:S(2)}) collective-permute-start(bf16[4,128,1024]{2,1,0:T(8,128)(2,1)S(1)} %broadcast_select_fusion.2), channel_id=1, source_target_pairs={{0,4},{15,11},{4,8},{11,7},{9,13},{6,2},{12,14},{3,1},{16,20},{31,... | collective-permute-start | bytes 3145736 | tf_op jit(solution)/shard_map/ppermute | solution.py:113
  27.9 66.4 %copy-start.2 = (bf16[4,128,1024]{2,1,0:T(8,128)(2,1)}, bf16[4,128,1024]{2,1,0:T(8,128)(2,1)S(1)}, u32[]{:S(2)}) copy-start(bf16[4,128,1024]{2,1,0:T(8,128)(2,1)S(1)} %collective-permute-done.4) | copy-start | bytes 3145732
  27.9 23.1 %collective-permute-start.9 = (bf16[4,128,1024]{2,1,0:T(8,128)(2,1)}, bf16[4,128,1024]{2,1,0:T(8,128)(2,1)S(1)}, u32[]{:S(2)}, u32[]{:S(2)}) collective-permute-start(bf16[4,128,1024]{2,1,0:T(8,128)(2,1)} %collective-permute-done.1.refs_1_), channel_id=1, source_target_pairs={{0,1},{15,14},{5,4},{10,11},{8,9},{7,6},{13,12},{2,3},{16,17},{31,... | collective-permute-start | bytes 3145736 | tf_op jit(solution)/shard_map/ppermute | solution.py:113
  41.0 20.6 %copy-start.1 = (bf16[4,128,1024]{2,1,0:T(8,128)(2,1)}, bf16[4,128,1024]{2,1,0:T(8,128)(2,1)S(1)}, u32[]{:S(2)}) copy-start(bf16[4,128,1024]{2,1,0:T(8,128)(2,1)S(1)} %collective-permute-done.2.refs_4_) | copy-start | bytes 3145732
  42.3 30.0 %collective-permute-start.5 = (bf16[4,128,1024]{2,1,0:T(8,128)(2,1)}, bf16[4,128,1024]{2,1,0:T(8,128)(2,1)}, u32[]{:S(2)}, u32[]{:S(2)}) collective-permute-start(bf16[4,128,1024]{2,1,0:T(8,128)(2,1)} %broadcast_select_fusion.3), channel_id=1, source_target_pairs={{0,4},{15,11},{4,8},{11,7},{9,13},{6,2},{12,14},{3,1},{16,20},{31,... | collective-permute-start | bytes 3145736 | tf_op jit(solution)/shard_map/ppermute | solution.py:113
  43.6 18.1 %collective-permute-start.8 = (bf16[4,128,1024]{2,1,0:T(8,128)(2,1)S(1)}, bf16[4,128,1024]{2,1,0:T(8,128)(2,1)}, u32[]{:S(2)}, u32[]{:S(2)}) collective-permute-start(bf16[4,128,1024]{2,1,0:T(8,128)(2,1)S(1)} %collective-permute-done.2.refs_4_), channel_id=1, source_target_pairs={{0,1},{15,14},{5,4},{10,11},{8,9},{7,6},{13,12},{2,3},{16,17},{31,... | collective-permute-start | bytes 3145736 | tf_op jit(solution)/shard_map/ppermute | solution.py:113
  46.7 25.5 %collective-permute-start.7 = (bf16[4,128,1024]{2,1,0:T(8,128)(2,1)}, bf16[4,128,1024]{2,1,0:T(8,128)(2,1)}, u32[]{:S(2)}, u32[]{:S(2)}) collective-permute-start(bf16[4,128,1024]{2,1,0:T(8,128)(2,1)} %collective-permute-done.6), channel_id=1, source_target_pairs={{9,1},{6,14},{0,2},{15,13},{25,17},{22,30},{16,18},{31,29}} | collective-permute-start | bytes 3145736 | tf_op jit(solution)/shard_map/ppermute | solution.py:113
  51.1 8.2 %copy-start.5 = (bf16[4,128,1024]{2,1,0:T(8,128)(2,1)}, bf16[4,128,1024]{2,1,0:T(8,128)(2,1)S(1)}, u32[]{:S(2)}) copy-start(bf16[4,128,1024]{2,1,0:T(8,128)(2,1)S(1)} %collective-permute-done.9.refs_5_) | copy-start | bytes 3145732
  51.1 27.4 %collective-permute-start.16 = (bf16[4,128,1024]{2,1,0:T(8,128)(2,1)}, bf16[4,128,1024]{2,1,0:T(8,128)(2,1)}, u32[]{:S(2)}, u32[]{:S(2)}) collective-permute-start(bf16[4,128,1024]{2,1,0:T(8,128)(2,1)} %broadcast_select_fusion), channel_id=1, source_target_pairs={{5,1},{10,14},{13,9},{2,6},{1,3},{14,12},{21,17},{26,30},{29,25},{... | collective-permute-start | bytes 3145736 | tf_op jit(solution)/shard_map/ppermute | solution.py:113
  59.3 19.2 %collective-permute-start.13 = (bf16[4,128,1024]{2,1,0:T(8,128)(2,1)}, bf16[4,128,1024]{2,1,0:T(8,128)(2,1)}, u32[]{:S(2)}, u32[]{:S(2)}) collective-permute-start(bf16[4,128,1024]{2,1,0:T(8,128)(2,1)} %collective-permute-done.12), channel_id=1, source_target_pairs={{4,8},{11,7},{8,12},{7,3},{20,24},{27,23},{24,28},{23,19}} | collective-permute-start | bytes 3145736 | tf_op jit(solution)/shard_map/ppermute | solution.py:113
  74.6 19.7 %collective-permute-start.11 = (bf16[4,128,1024]{2,1,0:T(8,128)(2,1)}, bf16[4,128,1024]{2,1,0:T(8,128)(2,1)S(1)}, u32[]{:S(2)}, u32[]{:S(2)}) collective-permute-start(bf16[4,128,1024]{2,1,0:T(8,128)(2,1)} %broadcast_select_fusion.1), channel_id=1, source_target_pairs={{5,1},{10,14},{13,9},{2,6},{1,3},{14,12},{21,17},{26,30},{29,25},{... | collective-permute-start | bytes 3145736 | tf_op jit(solution)/shard_map/ppermute | solution.py:113
  75.9 18.4 %collective-permute-start.10 = (bf16[4,128,1024]{2,1,0:T(8,128)(2,1)}, bf16[4,128,1024]{2,1,0:T(8,128)(2,1)S(1)}, u32[]{:S(2)}, u32[]{:S(2)}) collective-permute-start(bf16[4,128,1024]{2,1,0:T(8,128)(2,1)} %collective-permute-done.5), channel_id=1, source_target_pairs={{4,8},{11,7},{8,12},{7,3},{20,24},{27,23},{24,28},{23,19}} | collective-permute-start | bytes 3145736 | tf_op jit(solution)/shard_map/ppermute | solution.py:113
  94.3 1.0 copy-start.3
  94.3 1.4 %copy-start.4 = (bf16[4,128,1024]{2,1,0:T(8,128)(2,1)}, bf16[4,128,1024]{2,1,0:T(8,128)(2,1)S(1)}, u32[]{:S(2)}) copy-start(bf16[4,128,1024]{2,1,0:T(8,128)(2,1)S(1)} %collective-permute-done.10) | copy-start | bytes 3145732

commit v3 on v2

--- a/solution.py
+++ b/solution.py
@@ -10,7 +10,7 @@
 SLACK = 32
 LAGMAX = 64
 AXES = ("feat", "tm", "sub")
-VMEM_LIMIT = 60 * 1024 * 1024
+VMEM_LIMIT = 28 * 1024 * 1024
 TILE = 512
 DEPTH = 2
 ROWS_TILE = 1024
@@ -98,15 +98,15 @@
 
 PLACES = [(s, x) for s in range(4) for x in range(2)]
 CORES = [(rank(s, x, c), rank(s, x, 1 - c)) for s, x in PLACES for c in range(2)]
-FROM_HOME = [(rank(s, x, home(s, x)), rank(s, x, 1 - home(s, x))) for s, x in PLACES]
-CROSS_HOME = [(rank(s, x, home(s, x)), rank(3 - s, 1 - x, home(s, x))) for s, x in PLACES]
-CROSS_AWAY = [(rank(s, x, 1 - home(s, x)), rank(3 - s, 1 - x, home(s, x))) for s, x in PLACES]
+PLANES = [(rank(s, x, c), rank(3 - s, 1 - x, c)) for s, x in PLACES for c in range(2)]
 NEAR_1 = hops([(0, 1, 0), (1, 2, 1), (2, 3, 2)])
 FAR_1 = hops([(3, 2, 3), (2, 0, 2)])
 NEAR_2 = hops([(0, 1, 0), (1, 2, 0), (2, 3, 1), (3, -1, 2)])
 FAR_2 = hops([(2, 0, 3), (0, -1, 2)])
 NEAR_3 = hops([(1, 2, 0), (2, 3, 0)])
-BACK_3 = hops([(1, 0, 1), (3, 2, 1), (0, -1, 3)])
+BACK_3 = hops([(3, 2, 1), (0, -1, 3)])
+OWN_3 = hops([(1, 0, 1)])
+PICKS = (((0, 2, 3, 4), (1, 3, 4, 5)), ((7, 0, 2, 3), (3, 1, 5, 6)))
 
 
 def send(x, pairs):
@@ -143,10 +143,10 @@
                     kept & (column == frame + ahead), 1.0, 0.0
                 ).astype(jnp.bfloat16)
 
-    def fill(own_ref, cross_refs):
+    def fill(own_ref, cross_ref):
         total = None
         for k in range(trajectories):
-            series = jnp.concatenate([own_ref[k], cross_refs[0][k] + cross_refs[1][k]], axis=0)
+            series = jnp.concatenate([own_ref[k], cross_ref[k]], axis=0)
             moved = lax.dot_general(
                 series,
                 moves_ref[k],
@@ -162,8 +162,8 @@
         mean = jnp.sum(total, axis=1, keepdims=True) / count_ref[0]
         mean_ref[...] = jnp.broadcast_to(mean, mean_ref.shape)
 
-    for n, (own_ref, *cross_refs) in enumerate(parts):
-        pl.when(p == n)(functools.partial(fill, own_ref, cross_refs))
+    for n, (own_ref, cross_ref) in enumerate(parts):
+        pl.when(p == n)(functools.partial(fill, own_ref, cross_ref))
 
 
 def prepare_rows(part, starts, lags, x, count, arrays, window):
@@ -177,9 +177,13 @@
     def spot(p, i, part_ref, *_):
         return (jnp.where(p == 0, part_ref[0], 1 - part_ref[0]) * steps + i, 0)
 
+    shape = (trajectories, half, tile)
+    first = pl.BlockSpec(shape, lambda p, i, *_: (0, 0, jnp.where(p == 0, i, steps - 1)))
+    second = pl.BlockSpec(shape, lambda p, i, *_: (0, 0, jnp.where(p == 0, 0, i)))
+
     def body(part_ref, starts_ref, lags_ref, x_ref, count_ref, *refs):
         rows_kernel(
-            starts_ref, lags_ref, x_ref, count_ref, (refs[:3], refs[3:6]), *refs[6:], window=window
+            starts_ref, lags_ref, x_ref, count_ref, (refs[:2], refs[2:4]), *refs[4:], window=window
         )
 
     return pl.pallas_call(
@@ -188,14 +192,7 @@
         grid_spec=pltpu.PrefetchScalarGridSpec(
             num_scalar_prefetch=5,
             grid=(2, steps),
-            in_specs=[
-                pl.BlockSpec((trajectories, half, tile), lambda p, i, *_: (0, 0, jnp.where(p == 0, i, steps - 1)))
-            ]
-            * 3
-            + [
-                pl.BlockSpec((trajectories, half, tile), lambda p, i, *_: (0, 0, jnp.where(p == 0, 0, i)))
-            ]
-            * 3,
+            in_specs=[first] * 2 + [second] * 2,
             out_specs=[
                 pl.BlockSpec((tile, depth), spot),
                 pl.BlockSpec((tile, depth), spot),
@@ -211,7 +208,7 @@
     )(part, starts, lags, x, count, *arrays[0], *arrays[1])
 
 
-def product_kernel(part_ref, pick_ref, count_ref, masks_ref, mean_ref, zero_ref, late_ref, *refs, n_pieces):
+def product_kernel(part_ref, place_ref, count_ref, masks_ref, mean_ref, zero_ref, late_ref, *refs, n_pieces):
     pieces = refs[:n_pieces]
     cov_zero_ref, cov_late_ref, left_ref, columns_ref, made_ref, arrived, fetched, stored = refs[-8:]
     half, width = columns_ref.shape[0] // 2, columns_ref.shape[1]
@@ -239,12 +236,13 @@
             stored.at[slot, n],
         )
 
-    for side in range(2):
-        for m, piece in enumerate(pieces):
-
-            @pl.when(pick_ref[side] == m)
-            def _():
-                piece_copy(piece, side).start()
+    for kind, sides in enumerate(PICKS):
+        for side, places in enumerate(sides):
+            for place, m in enumerate(places):
+
+                @pl.when((place_ref[0] == place) & (place_ref[1] == kind))
+                def _():
+                    piece_copy(pieces[m], side).start()
 
     def fetch(i):
         for n in range(2):
@@ -279,7 +277,7 @@
             out_copy(n, i).wait()
 
 
-def product(part, pick, count, masks, rows, pieces, before):
+def product(part, place, count, masks, rows, pieces, before):
     zero, late, means = rows
     height, depth = zero.shape
     width = pieces[0].shape[-1]
@@ -316,7 +314,7 @@
             transcendentals=0,
         ),
         name="covariances",
-    )(part, pick, count, masks, means, zero, late, *pieces, *before)
+    )(part, place, count, masks, means, zero, late, *pieces, *before)
 
 
 def line_of_four(frames, window_starts, lag_frames):
@@ -345,37 +343,32 @@
     picks = jnp.array([[[0, 2, 3, 4], [1, 3, 4, 5]], [[5, 0, 2, 3], [3, 1, 5, 6]]], jnp.int32)
     pick = picks[jnp.where(c == x, 0, 1), :, s]
 
+    place = jnp.stack([s, jnp.where(c == x, 0, 1)]).astype(jnp.int32)
     own = frames
-    cross_a = send(own, CROSS_HOME)
     near1_a, far1_a = send(own, NEAR_1), send(own, FAR_1)
+    cross = send(own, PLANES)
     sib = send(own, CORES)
-    sib_b = sib
-    near1_b, far1_b = send(sib_b, NEAR_1), send(sib_b, FAR_1)
-    cross_b = send(after(own, cross_a), CROSS_AWAY)
-    near2_a, far2_a = send(jnp.where(s == 0, cross_a, near1_a), NEAR_2), send(far1_a, FAR_2)
-    sib_cross_a, sib_cross_b = send(cross_a, FROM_HOME), send(cross_b, FROM_HOME)
-    pick, masks = lax.optimization_barrier((pick, masks, near1_a))[:2]
-    near3_a, back_a = send(near2_a, NEAR_3), send(jnp.where(s == 1, own, far2_a), BACK_3)
-    near2_b, far2_b = send(jnp.where(s == 0, cross_b, near1_b), NEAR_2), send(far1_b, FAR_2)
+    near1_b, far1_b = send(sib, NEAR_1), send(sib, FAR_1)
+    near1_a, far1_a, masks, count, place = lax.optimization_barrier(
+        (near1_a, far1_a, masks, count, place)
+    )
+    near2_a, far2_a = send(jnp.where(s == 0, cross, near1_a), NEAR_2), send(far1_a, FAR_2)
+    sib_cross = send(cross, CORES)
+    near2_b, far2_b = send(jnp.where(s == 0, sib_cross, near1_b), NEAR_2), send(far1_b, FAR_2)
+    near3_a, back_a, close_a = send(near2_a, NEAR_3), send(far2_a, BACK_3), send(own, OWN_3)
     rows = prepare_rows(
-        part,
-        window_starts,
-        lag_frames,
-        plane,
-        count,
-        ((own, cross_a, sib_cross_b), (sib, cross_b, sib_cross_a)),
-        window,
+        part, window_starts, lag_frames, plane, count, ((own, cross), (sib, sib_cross)), window
     )
     near2_b, far2_b, *rows = lax.optimization_barrier((near2_b, far2_b, *rows))
-    near3_b, back_b = send(near2_b, NEAR_3), send(jnp.where(s == 1, sib, far2_b), BACK_3)
+    near3_b, back_b, close_b = send(near2_b, NEAR_3), send(far2_b, BACK_3), send(sib, OWN_3)
 
     outs = ()
     for where_to, pieces in (
-        (part, (own, cross_a, near1_a, near2_a, near3_a, back_a, far2_a)),
-        (1 - part, (sib, cross_b, near1_b, near2_b, near3_b, back_b, far2_b)),
+        (part, (own, cross, near1_a, near2_a, near3_a, back_a, far2_a, close_a)),
+        (1 - part, (sib, sib_cross, near1_b, near2_b, near3_b, back_b, far2_b, close_b)),
     ):
         pieces = [piece.reshape(trajectories * half, features) for piece in pieces]
-        outs = product(where_to, pick, count, masks, rows, pieces, outs)
+        outs = product(where_to, place, count, masks, rows, pieces, outs)
     return outs
 
 

time: 112 us -> 102 us (0.911)
  the two profiles are of different devices: /device:TPU:2 before, /device:TPU:1 now
where the time goes in v3:
time: 102 us; the launch traced here: 101 us
  waiting for transfers between devices  41 us (40%)
  Pallas kernels  31.6 us (31%)
  starting transfers between devices  20.9 us (20%)
  local copies, waits for them, and re-layouts  3.77 us (4%)
  other arithmetic  2.42 us (2%)
  between operations  1.54 us (2%)
    ppermute x17, waiting for transfers between devices, send(): return lax.ppermute(x, AXES, pairs)  41 us
    pallas_call x2, Pallas kernels, product(): pl.pallas_call(functools.partial(product_kernel, n_pieces=len(pieces)), o...  26.7 us
    ppermute x17, starting transfers between devices, send(): return lax.ppermute(x, AXES, pairs)  20.9 us
    pallas_call x1, Pallas kernels, prepare_rows(): pl.pallas_call(body, out_shape=(row, row, mean), grid_spec=pltpu.Prefetch...  4.86 us
    unnamed x8, local copies, waits for them, and re-layouts  3.75 us
  transfers between devices with their start and end apart: 17, of which 5 were waited for; matrix products, arithmetic and copies ran while one was open for 2% of the time, Pallas kernels for 18%

profile of v3, /device:TPU:1, one launch (start us, length us, event | category | flops | bytes accessed | tf_op | source)
XLA Modules:
  0.0 101.2 jit_solution(17343625490281832621)
XLA Ops:
  0.8 2.7 %collective-permute-start.2 = (bf16[4,128,1024]{2,1,0:T(8,128)(2,1)}, bf16[4,128,1024]{2,1,0:T(8,128)(2,1)S(1)}, u32[]{:S(2)}, u32[]{:S(2)}) collective-permute-start(bf16[4,128,1024]{2,1,0:T(8,128)(2,1)} %refs_0_.1), channel_id=1, source_target_pairs={{0,2},{1,3},{14,12},{15,13},{4,6},{5,7},{10,8},{11,9},{8,10},{9,11... | collective-permute-start | bytes 3145736 | tf_op jit(solution)/shard_map/ppermute | solution.py:113
  3.4 1.6 %collective-permute-start.1 = (bf16[4,128,1024]{2,1,0:T(8,128)(2,1)}, bf16[4,128,1024]{2,1,0:T(8,128)(2,1)}, u32[]{:S(2)}, u32[]{:S(2)}) collective-permute-start(bf16[4,128,1024]{2,1,0:T(8,128)(2,1)} %refs_0_.1), channel_id=1, source_target_pairs={{13,9},{2,6},{8,0},{7,15},{29,25},{18,22},{24,16},{23,31}} | collective-permute-start | bytes 3145736 | tf_op jit(solution)/shard_map/ppermute | solution.py:113
  5.1 1.6 %collective-permute-start = (bf16[4,128,1024]{2,1,0:T(8,128)(2,1)}, bf16[4,128,1024]{2,1,0:T(8,128)(2,1)}, u32[]{:S(2)}, u32[]{:S(2)}) collective-permute-start(bf16[4,128,1024]{2,1,0:T(8,128)(2,1)} %refs_0_.1), channel_id=1, source_target_pairs={{0,4},{15,11},{5,9},{10,6},{8,12},{7,3},{16,20},{31,27},{21,25},{2... | collective-permute-start | bytes 3145736 | tf_op jit(solution)/shard_map/ppermute | solution.py:113
  6.7 1.4 %fusion.4 = (s32[4]{0:T(128)S(1)}, s32[4]{0:T(128)S(1)}, s32[]{:T(128)}, s32[4]{0:T(128)S(1)}) fusion(s32[4]{0:T(128)} %lags_ref.1, s32[4]{0:T(128)} %starts_ref.1), kind=kLoop, calls=%fused_computation.19 | loop fusion | flops 15 | bytes 84 | tf_op jit(solution)/shard_map/sub | solution.py:29
  8.1 0.7 fusion.1
  8.8 1.6 %collective-permute-start.7 = (bf16[4,128,1024]{2,1,0:T(8,128)(2,1)}, bf16[4,128,1024]{2,1,0:T(8,128)(2,1)}, u32[]{:S(2)}, u32[]{:S(2)}) collective-permute-start(bf16[4,128,1024]{2,1,0:T(8,128)(2,1)} %collective-permute-done.4.refs_2_), channel_id=1, source_target_pairs={{13,9},{2,6},{8,0},{7,15},{29,25},{18,22},{24,16},{23,31}} | collective-permute-start | bytes 3145736 | tf_op jit(solution)/shard_map/ppermute | solution.py:113
  11.2 16.0 %collective-permute-done.2.refs_1_ = bf16[4,128,1024]{2,1,0:T(8,128)(2,1)S(1)} collective-permute-done((bf16[4,128,1024]{2,1,0:T(8,128)(2,1)}, bf16[4,128,1024]{2,1,0:T(8,128)(2,1)S(1)}, u32[]{:S(2)}, u32[]{:S(2)}) %collective-permute-start.2) | collective-permute-done | bytes 1048608 | tf_op jit(solution)/shard_map/ppermute | solution.py:113
  28.6 1.3 %collective-permute-start.12 = (bf16[4,128,1024]{2,1,0:T(8,128)(2,1)S(1)}, bf16[4,128,1024]{2,1,0:T(8,128)(2,1)S(1)}, u32[]{:S(2)}, u32[]{:S(2)}) collective-permute-start(bf16[4,128,1024]{2,1,0:T(8,128)(2,1)S(1)} %broadcast_select_fusion), channel_id=1, source_target_pairs={{0,4},{15,11},{4,8},{11,7},{9,13},{6,2},{12,14},{3,1},{16,20},{31,... | collective-permute-start | bytes 3145736 | tf_op jit(solution)/shard_map/ppermute | solution.py:113
  29.9 1.3 %collective-permute-start.14 = (bf16[4,128,1024]{2,1,0:T(8,128)(2,1)}, bf16[4,128,1024]{2,1,0:T(8,128)(2,1)S(1)}, u32[]{:S(2)}, u32[]{:S(2)}) collective-permute-start(bf16[4,128,1024]{2,1,0:T(8,128)(2,1)} %collective-permute-done.1), channel_id=1, source_target_pairs={{9,1},{6,14},{0,2},{15,13},{25,17},{22,30},{16,18},{31,29}} | collective-permute-start | bytes 3145736 | tf_op jit(solution)/shard_map/ppermute | solution.py:113
  31.3 1.3 %collective-permute-start.8 = (bf16[4,128,1024]{2,1,0:T(8,128)(2,1)}, bf16[4,128,1024]{2,1,0:T(8,128)(2,1)S(1)}, u32[]{:S(2)}, u32[]{:S(2)}) collective-permute-start(bf16[4,128,1024]{2,1,0:T(8,128)(2,1)} %collective-permute-done.7), channel_id=1, source_target_pairs={{9,1},{6,14},{0,2},{15,13},{25,17},{22,30},{16,18},{31,29}} | collective-permute-start | bytes 3145736 | tf_op jit(solution)/shard_map/ppermute | solution.py:113
  32.7 1.3 %collective-permute-start.6 = (bf16[4,128,1024]{2,1,0:T(8,128)(2,1)S(1)}, bf16[4,128,1024]{2,1,0:T(8,128)(2,1)S(1)}, u32[]{:S(2)}, u32[]{:S(2)}) collective-permute-start(bf16[4,128,1024]{2,1,0:T(8,128)(2,1)S(1)} %broadcast_select_fusion.1), channel_id=1, source_target_pairs={{0,4},{15,11},{4,8},{11,7},{9,13},{6,2},{12,14},{3,1},{16,20},{31,... | collective-permute-start | bytes 3145736 | tf_op jit(solution)/shard_map/ppermute | solution.py:113
  34.0 1.3 %collective-permute-start.16 = (bf16[4,128,1024]{2,1,0:T(8,128)(2,1)}, bf16[4,128,1024]{2,1,0:T(8,128)(2,1)S(1)}, u32[]{:S(2)}, u32[]{:S(2)}) collective-permute-start(bf16[4,128,1024]{2,1,0:T(8,128)(2,1)} %refs_0_.1), channel_id=1, source_target_pairs={{5,1},{10,14},{21,17},{26,30}} | collective-permute-start | bytes 3145736 | tf_op jit(solution)/shard_map/ppermute | solution.py:113
  35.3 9.5 %collective-permute-done.12 = bf16[4,128,1024]{2,1,0:T(8,128)(2,1)S(1)} collective-permute-done((bf16[4,128,1024]{2,1,0:T(8,128)(2,1)S(1)}, bf16[4,128,1024]{2,1,0:T(8,128)(2,1)S(1)}, u32[]{:S(2)}, u32[]{:S(2)}) %collective-permute-start.12) | collective-permute-done | bytes 1048608 | tf_op jit(solution)/shard_map/ppermute | solution.py:113
  45.5 4.0 %collective-permute-done.14 = bf16[4,128,1024]{2,1,0:T(8,128)(2,1)S(1)} collective-permute-done((bf16[4,128,1024]{2,1,0:T(8,128)(2,1)}, bf16[4,128,1024]{2,1,0:T(8,128)(2,1)S(1)}, u32[]{:S(2)}, u32[]{:S(2)}) %collective-permute-start.14) | collective-permute-done | bytes 1048608 | tf_op jit(solution)/shard_map/ppermute | solution.py:113
  49.5 1.3 %collective-permute-start.15 = (bf16[4,128,1024]{2,1,0:T(8,128)(2,1)S(1)}, bf16[4,128,1024]{2,1,0:T(8,128)(2,1)S(1)}, u32[]{:S(2)}, u32[]{:S(2)}) collective-permute-start(bf16[4,128,1024]{2,1,0:T(8,128)(2,1)S(1)} %collective-permute-done.14), channel_id=1, source_target_pairs={{13,9},{2,6},{1,3},{14,12},{29,25},{18,22},{17,19},{30,28}} | collective-permute-start | bytes 3145736 | tf_op jit(solution)/shard_map/ppermute | solution.py:113
  50.9 1.2 %copy-done = bf16[4,128,1024]{2,1,0:T(8,128)(2,1)S(1)} copy-done((bf16[4,128,1024]{2,1,0:T(8,128)(2,1)S(1)}, bf16[4,128,1024]{2,1,0:T(8,128)(2,1)}, u32[]{:S(2)}) %copy-start) | copy-done | bytes 1048600
  53.4 4.9 %rows.1 = (bf16[2048,1024]{1,0:T(8,128)(2,1)S(1)}, bf16[2048,1024]{1,0:T(8,128)(2,1)S(1)}, f32[2048,128]{1,0:T(8,128)S(1)}) custom-call(s32[1]{0:T(128)} %bitcast.part_ref, s32[4]{0:T(128)S(1)} %copy-done.2, s32[4]{0:T(128)S(1)} %copy-done.3, s32[1]{0:T(128)} %bitcast.8.x_ref, f32[1]{0:T(128)} %bitcast.5.count_ref, bf16[4,128,1024]{2,1,0:T(8,128)(2,1)S(1)} %copy-done, ...), custom_call_target="tpu_custom_call" | custom-call | bytes 14680064 | tf_op jit(solution)/shard_map/rows/pallas_call | solution.py:189
  58.2 2.5 %collective-permute-done.8 = bf16[4,128,1024]{2,1,0:T(8,128)(2,1)S(1)} collective-permute-done((bf16[4,128,1024]{2,1,0:T(8,128)(2,1)}, bf16[4,128,1024]{2,1,0:T(8,128)(2,1)S(1)}, u32[]{:S(2)}, u32[]{:S(2)}) %collective-permute-start.8) | collective-permute-done | bytes 1048608 | tf_op jit(solution)/shard_map/ppermute | solution.py:113
  60.7 1.3 %collective-permute-start.11 = (bf16[4,128,1024]{2,1,0:T(8,128)(2,1)}, bf16[4,128,1024]{2,1,0:T(8,128)(2,1)S(1)}, u32[]{:S(2)}, u32[]{:S(2)}) collective-permute-start(bf16[4,128,1024]{2,1,0:T(8,128)(2,1)} %collective-permute-done.4.refs_2_), channel_id=1, source_target_pairs={{5,1},{10,14},{21,17},{26,30}} | collective-permute-start | bytes 3145736 | tf_op jit(solution)/shard_map/ppermute | solution.py:113
  62.8 9.1 %collective-permute-done.16 = bf16[4,128,1024]{2,1,0:T(8,128)(2,1)S(1)} collective-permute-done((bf16[4,128,1024]{2,1,0:T(8,128)(2,1)}, bf16[4,128,1024]{2,1,0:T(8,128)(2,1)S(1)}, u32[]{:S(2)}, u32[]{:S(2)}) %collective-permute-start.16) | collective-permute-done | bytes 1048608 | tf_op jit(solution)/shard_map/ppermute | solution.py:113
  71.9 1.3 %collective-permute-start.10 = (bf16[4,128,1024]{2,1,0:T(8,128)(2,1)S(1)}, bf16[4,128,1024]{2,1,0:T(8,128)(2,1)S(1)}, u32[]{:S(2)}, u32[]{:S(2)}) collective-permute-start(bf16[4,128,1024]{2,1,0:T(8,128)(2,1)S(1)} %collective-permute-done.8), channel_id=1, source_target_pairs={{13,9},{2,6},{1,3},{14,12},{29,25},{18,22},{17,19},{30,28}} | collective-permute-start | bytes 3145736 | tf_op jit(solution)/shard_map/ppermute | solution.py:113
  73.2 1.2 %copy-done.1 = bf16[4,128,1024]{2,1,0:T(8,128)(2,1)S(1)} copy-done((bf16[4,128,1024]{2,1,0:T(8,128)(2,1)S(1)}, bf16[4,128,1024]{2,1,0:T(8,128)(2,1)}, u32[]{:S(2)}) %copy-start.1) | copy-done | bytes 1048600
  74.5 13.3 %covariances.2 = (f32[2048,2048]{1,0:T(8,128)}, f32[2048,2048]{1,0:T(8,128)}) custom-call(s32[1]{0:T(128)} %bitcast.part_ref, s32[2]{0:T(128)S(1)} %pad_add_fusion.place_ref, f32[1]{0:T(128)} %bitcast.5.count_ref, bf16[16,1024]{1,0:T(8,128)(2,1)S(1)} %pad_maximum_fusion.masks_ref, f32[2048,128]{1,0:T(8,128)S(1)} %get-tuple-element.23.mean_ref, ...), custom_call_target="tpu_custom_call" | custom-call | flops 8589934592 | bytes 25165824 | tf_op jit(solution)/shard_map/covariances/pallas_call | solution.py:288
  87.8 13.4 %covariances.3 = (f32[2048,2048]{1,0:T(8,128)}, f32[2048,2048]{1,0:T(8,128)}) custom-call(s32[1]{0:T(128)S(6)} %sub.13.part_ref, s32[2]{0:T(128)S(1)} %pad_add_fusion.place_ref, f32[1]{0:T(128)} %bitcast.5.count_ref, bf16[16,1024]{1,0:T(8,128)(2,1)S(1)} %pad_maximum_fusion.masks_ref, ...), custom_call_target="tpu_custom_call", output_to_operand_aliasing={{0}: (15, {}), {1}: (16, {})} | custom-call | flops 8589934592 | bytes 25165824 | tf_op jit(solution)/shard_map/covariances/pallas_call | solution.py:288
  (33 shorter events, 4.5 us)
Async XLA Ops:
  0.6 8.2 %collective-permute-start.4 = (bf16[4,128,1024]{2,1,0:T(8,128)(2,1)}, bf16[4,128,1024]{2,1,0:T(8,128)(2,1)}, u32[]{:S(2)}, u32[]{:S(2)}) collective-permute-start(bf16[4,128,1024]{2,1,0:T(8,128)(2,1)} %refs_0_.1), channel_id=1, source_target_pairs={{0,1},{1,0},{14,15},{15,14},{4,5},{5,4},{10,11},{11,10},{8,9},{9,8... | collective-permute-start | bytes 3145736 | tf_op jit(solution)/shard_map/ppermute | solution.py:113
  0.8 26.4 %collective-permute-start.2 = (bf16[4,128,1024]{2,1,0:T(8,128)(2,1)}, bf16[4,128,1024]{2,1,0:T(8,128)(2,1)S(1)}, u32[]{:S(2)}, u32[]{:S(2)}) collective-permute-start(bf16[4,128,1024]{2,1,0:T(8,128)(2,1)} %refs_0_.1), channel_id=1, source_target_pairs={{0,2},{1,3},{14,12},{15,13},{4,6},{5,7},{10,8},{11,9},{8,10},{9,11... | collective-permute-start | bytes 3145736 | tf_op jit(solution)/shard_map/ppermute | solution.py:113
  3.4 25.1 %collective-permute-start.1 = (bf16[4,128,1024]{2,1,0:T(8,128)(2,1)}, bf16[4,128,1024]{2,1,0:T(8,128)(2,1)}, u32[]{:S(2)}, u32[]{:S(2)}) collective-permute-start(bf16[4,128,1024]{2,1,0:T(8,128)(2,1)} %refs_0_.1), channel_id=1, source_target_pairs={{13,9},{2,6},{8,0},{7,15},{29,25},{18,22},{24,16},{23,31}} | collective-permute-start | bytes 3145736 | tf_op jit(solution)/shard_map/ppermute | solution.py:113
  5.1 23.4 %collective-permute-start = (bf16[4,128,1024]{2,1,0:T(8,128)(2,1)}, bf16[4,128,1024]{2,1,0:T(8,128)(2,1)}, u32[]{:S(2)}, u32[]{:S(2)}) collective-permute-start(bf16[4,128,1024]{2,1,0:T(8,128)(2,1)} %refs_0_.1), channel_id=1, source_target_pairs={{0,4},{15,11},{5,9},{10,6},{8,12},{7,3},{16,20},{31,27},{21,25},{2... | collective-permute-start | bytes 3145736 | tf_op jit(solution)/shard_map/ppermute | solution.py:113
  8.8 22.4 %collective-permute-start.7 = (bf16[4,128,1024]{2,1,0:T(8,128)(2,1)}, bf16[4,128,1024]{2,1,0:T(8,128)(2,1)}, u32[]{:S(2)}, u32[]{:S(2)}) collective-permute-start(bf16[4,128,1024]{2,1,0:T(8,128)(2,1)} %collective-permute-done.4.refs_2_), channel_id=1, source_target_pairs={{13,9},{2,6},{8,0},{7,15},{29,25},{18,22},{24,16},{23,31}} | collective-permute-start | bytes 3145736 | tf_op jit(solution)/shard_map/ppermute | solution.py:113
  10.5 22.1 %collective-permute-start.5 = (bf16[4,128,1024]{2,1,0:T(8,128)(2,1)}, bf16[4,128,1024]{2,1,0:T(8,128)(2,1)S(1)}, u32[]{:S(2)}, u32[]{:S(2)}) collective-permute-start(bf16[4,128,1024]{2,1,0:T(8,128)(2,1)} %collective-permute-done.4.refs_2_), channel_id=1, source_target_pairs={{0,4},{15,11},{5,9},{10,6},{8,12},{7,3},{16,20},{31,27},{21,25},{2... | collective-permute-start | bytes 3145736 | tf_op jit(solution)/shard_map/ppermute | solution.py:113
  27.2 5.4 %collective-permute-start.3 = (bf16[4,128,1024]{2,1,0:T(8,128)(2,1)S(1)}, bf16[4,128,1024]{2,1,0:T(8,128)(2,1)S(1)}, u32[]{:S(2)}, u32[]{:S(2)}) collective-permute-start(bf16[4,128,1024]{2,1,0:T(8,128)(2,1)S(1)} %collective-permute-done.2.refs_1_), channel_id=1, source_target_pairs={{0,1},{1,0},{14,15},{15,14},{4,5},{5,4},{10,11},{11,10},{8,9},{9,8... | collective-permute-start | bytes 3145736 | tf_op jit(solution)/shard_map/ppermute | solution.py:113
  28.6 16.2 %collective-permute-start.12 = (bf16[4,128,1024]{2,1,0:T(8,128)(2,1)S(1)}, bf16[4,128,1024]{2,1,0:T(8,128)(2,1)S(1)}, u32[]{:S(2)}, u32[]{:S(2)}) collective-permute-start(bf16[4,128,1024]{2,1,0:T(8,128)(2,1)S(1)} %broadcast_select_fusion), channel_id=1, source_target_pairs={{0,4},{15,11},{4,8},{11,7},{9,13},{6,2},{12,14},{3,1},{16,20},{31,... | collective-permute-start | bytes 3145736 | tf_op jit(solution)/shard_map/ppermute | solution.py:113
  29.9 19.5 %collective-permute-start.14 = (bf16[4,128,1024]{2,1,0:T(8,128)(2,1)}, bf16[4,128,1024]{2,1,0:T(8,128)(2,1)S(1)}, u32[]{:S(2)}, u32[]{:S(2)}) collective-permute-start(bf16[4,128,1024]{2,1,0:T(8,128)(2,1)} %collective-permute-done.1), channel_id=1, source_target_pairs={{9,1},{6,14},{0,2},{15,13},{25,17},{22,30},{16,18},{31,29}} | collective-permute-start | bytes 3145736 | tf_op jit(solution)/shard_map/ppermute | solution.py:113
  31.3 29.5 %collective-permute-start.8 = (bf16[4,128,1024]{2,1,0:T(8,128)(2,1)}, bf16[4,128,1024]{2,1,0:T(8,128)(2,1)S(1)}, u32[]{:S(2)}, u32[]{:S(2)}) collective-permute-start(bf16[4,128,1024]{2,1,0:T(8,128)(2,1)} %collective-permute-done.7), channel_id=1, source_target_pairs={{9,1},{6,14},{0,2},{15,13},{25,17},{22,30},{16,18},{31,29}} | collective-permute-start | bytes 3145736 | tf_op jit(solution)/shard_map/ppermute | solution.py:113
  32.7 29.3 %collective-permute-start.6 = (bf16[4,128,1024]{2,1,0:T(8,128)(2,1)S(1)}, bf16[4,128,1024]{2,1,0:T(8,128)(2,1)S(1)}, u32[]{:S(2)}, u32[]{:S(2)}) collective-permute-start(bf16[4,128,1024]{2,1,0:T(8,128)(2,1)S(1)} %broadcast_select_fusion.1), channel_id=1, source_target_pairs={{0,4},{15,11},{4,8},{11,7},{9,13},{6,2},{12,14},{3,1},{16,20},{31,... | collective-permute-start | bytes 3145736 | tf_op jit(solution)/shard_map/ppermute | solution.py:113
  34.0 37.9 %collective-permute-start.16 = (bf16[4,128,1024]{2,1,0:T(8,128)(2,1)}, bf16[4,128,1024]{2,1,0:T(8,128)(2,1)S(1)}, u32[]{:S(2)}, u32[]{:S(2)}) collective-permute-start(bf16[4,128,1024]{2,1,0:T(8,128)(2,1)} %refs_0_.1), channel_id=1, source_target_pairs={{5,1},{10,14},{21,17},{26,30}} | collective-permute-start | bytes 3145736 | tf_op jit(solution)/shard_map/ppermute | solution.py:113
  44.8 28.4 %collective-permute-start.13 = (bf16[4,128,1024]{2,1,0:T(8,128)(2,1)S(1)}, bf16[4,128,1024]{2,1,0:T(8,128)(2,1)S(1)}, u32[]{:S(2)}, u32[]{:S(2)}) collective-permute-start(bf16[4,128,1024]{2,1,0:T(8,128)(2,1)S(1)} %collective-permute-done.12), channel_id=1, source_target_pairs={{4,8},{11,7},{8,12},{7,3},{20,24},{27,23},{24,28},{23,19}} | collective-permute-start | bytes 3145736 | tf_op jit(solution)/shard_map/ppermute | solution.py:113
  49.5 23.7 %collective-permute-start.15 = (bf16[4,128,1024]{2,1,0:T(8,128)(2,1)S(1)}, bf16[4,128,1024]{2,1,0:T(8,128)(2,1)S(1)}, u32[]{:S(2)}, u32[]{:S(2)}) collective-permute-start(bf16[4,128,1024]{2,1,0:T(8,128)(2,1)S(1)} %collective-permute-done.14), channel_id=1, source_target_pairs={{13,9},{2,6},{1,3},{14,12},{29,25},{18,22},{17,19},{30,28}} | collective-permute-start | bytes 3145736 | tf_op jit(solution)/shard_map/ppermute | solution.py:113
  50.8 1.2 %copy-start = (bf16[4,128,1024]{2,1,0:T(8,128)(2,1)S(1)}, bf16[4,128,1024]{2,1,0:T(8,128)(2,1)}, u32[]{:S(2)}) copy-start(bf16[4,128,1024]{2,1,0:T(8,128)(2,1)} %refs_0_.1) | copy-start | bytes 3145732
  52.1 0.7 copy-start.2
  52.7 0.7 copy-start.3
  60.7 27.1 %collective-permute-start.11 = (bf16[4,128,1024]{2,1,0:T(8,128)(2,1)}, bf16[4,128,1024]{2,1,0:T(8,128)(2,1)S(1)}, u32[]{:S(2)}, u32[]{:S(2)}) collective-permute-start(bf16[4,128,1024]{2,1,0:T(8,128)(2,1)} %collective-permute-done.4.refs_2_), channel_id=1, source_target_pairs={{5,1},{10,14},{21,17},{26,30}} | collective-permute-start | bytes 3145736 | tf_op jit(solution)/shard_map/ppermute | solution.py:113
  62.0 25.8 %collective-permute-start.9 = (bf16[4,128,1024]{2,1,0:T(8,128)(2,1)S(1)}, bf16[4,128,1024]{2,1,0:T(8,128)(2,1)S(1)}, u32[]{:S(2)}, u32[]{:S(2)}) collective-permute-start(bf16[4,128,1024]{2,1,0:T(8,128)(2,1)S(1)} %collective-permute-done.6), channel_id=1, source_target_pairs={{4,8},{11,7},{8,12},{7,3},{20,24},{27,23},{24,28},{23,19}} | collective-permute-start | bytes 3145736 | tf_op jit(solution)/shard_map/ppermute | solution.py:113
  71.9 16.0 %collective-permute-start.10 = (bf16[4,128,1024]{2,1,0:T(8,128)(2,1)S(1)}, bf16[4,128,1024]{2,1,0:T(8,128)(2,1)S(1)}, u32[]{:S(2)}, u32[]{:S(2)}) collective-permute-start(bf16[4,128,1024]{2,1,0:T(8,128)(2,1)S(1)} %collective-permute-done.8), channel_id=1, source_target_pairs={{13,9},{2,6},{1,3},{14,12},{29,25},{18,22},{17,19},{30,28}} | collective-permute-start | bytes 3145736 | tf_op jit(solution)/shard_map/ppermute | solution.py:113
  73.2 1.2 %copy-start.1 = (bf16[4,128,1024]{2,1,0:T(8,128)(2,1)S(1)}, bf16[4,128,1024]{2,1,0:T(8,128)(2,1)}, u32[]{:S(2)}) copy-start(bf16[4,128,1024]{2,1,0:T(8,128)(2,1)} %refs_0_.1) | copy-start | bytes 3145732

commit v4 on v3

--- a/solution.py
+++ b/solution.py
@@ -10,8 +10,8 @@
 SLACK = 32
 LAGMAX = 64
 AXES = ("feat", "tm", "sub")
-VMEM_LIMIT = 28 * 1024 * 1024
-TILE = 512
+VMEM_LIMIT = 32 * 1024 * 1024
+TILES = (1024, 768, 256)
 DEPTH = 2
 ROWS_TILE = 1024
 
@@ -208,13 +208,10 @@
     )(part, starts, lags, x, count, *arrays[0], *arrays[1])
 
 
-def product_kernel(part_ref, place_ref, count_ref, masks_ref, mean_ref, zero_ref, late_ref, *refs, n_pieces):
+def product_kernel(part_ref, place_ref, count_ref, masks_ref, mean_ref, zero_ref, late_ref, *refs, n_pieces, tiles):
     pieces = refs[:n_pieces]
     cov_zero_ref, cov_late_ref, left_ref, columns_ref, made_ref, arrived, fetched, stored = refs[-8:]
     half, width = columns_ref.shape[0] // 2, columns_ref.shape[1]
-    tile = left_ref.shape[2]
-    steps = left_ref.shape[1]
-    depth_out = made_ref.shape[0]
     scale = 1.0 / count_ref[0]
     first = pl.multiple_of(part_ref[0] * width, width)
 
@@ -224,15 +221,16 @@
         )
 
     def left_copy(n, i):
+        rows = pl.ds(*tiles[i])
         return pltpu.make_async_copy(
-            (zero_ref, late_ref)[n].at[pl.ds(i * tile, tile)], left_ref.at[n, i], fetched.at[n, i]
+            (zero_ref, late_ref)[n].at[rows], left_ref.at[n, rows], fetched.at[n, i]
         )
 
     def out_copy(n, i):
-        slot = lax.rem(i, depth_out)
+        slot = i % DEPTH
         return pltpu.make_async_copy(
-            made_ref.at[slot, n],
-            (cov_zero_ref, cov_late_ref)[n].at[pl.ds(i * tile, tile), pl.ds(first, width)],
+            made_ref.at[slot, n, pl.ds(0, tiles[i][1])],
+            (cov_zero_ref, cov_late_ref)[n].at[pl.ds(*tiles[i]), pl.ds(first, width)],
             stored.at[slot, n],
         )
 
@@ -244,35 +242,25 @@
                 def _():
                     piece_copy(pieces[m], side).start()
 
-    def fetch(i):
-        for n in range(2):
-            left_copy(n, i).start()
-
-    fetch(0)
+    for n in range(2):
+        left_copy(n, 0).start()
     for side in range(2):
         piece_copy(pieces[0], side).wait()
-    means = dot(masks_ref[...], columns_ref[...]) * scale
-
-    def step(i, carry):
-        @pl.when(i + 1 < steps)
-        def _():
-            fetch(i + 1)
-
-        row_mean = mean_ref[pl.ds(pl.multiple_of(i * tile, tile), tile), :1]
+    for i, (top, tile) in enumerate(tiles):
+        if i + 1 < len(tiles):
+            for n in range(2):
+                left_copy(n, i + 1).start()
+        if i == 0:
+            means = dot(masks_ref[...], columns_ref[...]) * scale
+        row_mean = mean_ref[top : top + tile, :1]
         for n in range(2):
             left_copy(n, i).wait()
-
-            @pl.when(i >= depth_out)
-            def _():
-                out_copy(n, i - depth_out).wait()
-
-            total = dot(left_ref[n, i], columns_ref[...])
-            made_ref[lax.rem(i, depth_out), n] = total * scale - row_mean * means[8 * n : 8 * n + 1]
+            if i >= DEPTH:
+                out_copy(n, i - DEPTH).wait()
+            total = dot(left_ref[n, top : top + tile], columns_ref[...])
+            made_ref[i % DEPTH, n, :tile] = total * scale - row_mean * means[8 * n : 8 * n + 1]
             out_copy(n, i).start()
-        return carry
-
-    lax.fori_loop(0, steps, step, 0)
-    for i in range(max(0, steps - depth_out), steps):
+    for i in range(max(0, len(tiles) - DEPTH), len(tiles)):
         for n in range(2):
             out_copy(n, i).wait()
 
@@ -281,12 +269,16 @@
     zero, late, means = rows
     height, depth = zero.shape
     width = pieces[0].shape[-1]
-    tile = min(TILE, height)
-    steps = height // tile
+    tiles, top = [], 0
+    for tile in TILES:
+        tile = min(tile, height - top)
+        tiles.append((top, tile))
+        top += tile
+    steps, tile = len(tiles), max(TILES)
     out = jax.ShapeDtypeStruct((height, 2 * width), jnp.float32)
     anywhere = pl.BlockSpec(memory_space=pl.ANY)
     return pl.pallas_call(
-        functools.partial(product_kernel, n_pieces=len(pieces)),
+        functools.partial(product_kernel, n_pieces=len(pieces), tiles=tiles),
         out_shape=(out, out),
         grid_spec=pltpu.PrefetchScalarGridSpec(
             num_scalar_prefetch=3,
@@ -298,7 +290,7 @@
             + [anywhere] * (2 + len(pieces) + len(before)),
             out_specs=[anywhere] * 2,
             scratch_shapes=[
-                pltpu.VMEM((2, steps, tile, depth), jnp.bfloat16),
+                pltpu.VMEM((2, height, depth), jnp.bfloat16),
                 pltpu.VMEM((depth, width), jnp.bfloat16),
                 pltpu.VMEM((DEPTH, 2, tile, width), jnp.float32),
                 pltpu.SemaphoreType.DMA((2,)),
@@ -355,12 +347,12 @@
     near2_a, far2_a = send(jnp.where(s == 0, cross, near1_a), NEAR_2), send(far1_a, FAR_2)
     sib_cross = send(cross, CORES)
     near2_b, far2_b = send(jnp.where(s == 0, sib_cross, near1_b), NEAR_2), send(far1_b, FAR_2)
-    near3_a, back_a, close_a = send(near2_a, NEAR_3), send(far2_a, BACK_3), send(own, OWN_3)
+    near3_a, back_a, close_a = send(near2_a, NEAR_3), send(far2_a, BACK_3), send(after(own, near2_a, far2_a), OWN_3)
     rows = prepare_rows(
         part, window_starts, lag_frames, plane, count, ((own, cross), (sib, sib_cross)), window
     )
     near2_b, far2_b, *rows = lax.optimization_barrier((near2_b, far2_b, *rows))
-    near3_b, back_b, close_b = send(near2_b, NEAR_3), send(far2_b, BACK_3), send(sib, OWN_3)
+    near3_b, back_b, close_b = send(near2_b, NEAR_3), send(far2_b, BACK_3), send(after(sib, near2_b), OWN_3)
 
     outs = ()
     for where_to, pieces in (

time: 102 us -> 99.4 us (0.975)
  waiting for transfers between devices: 41 us -> 39.7 us
  Pallas kernels: 31.6 us -> 30.5 us
    ppermute x17, waiting for transfers between devices: 41 us -> 39.7 us  [send(): return lax.ppermute(x, AXES, pairs)]
    pallas_call x2, Pallas kernels: 26.7 us -> 25.6 us  [product(): pl.pallas_call(functools.partial(product_kernel, n_pieces=len(pieces), ti...]
where the time goes in v4:
time: 99.4 us; the launch traced here: 98.9 us
  waiting for transfers between devices  39.7 us (40%)
  Pallas kernels  30.5 us (31%)
  starting transfers between devices  20.9 us (21%)
  local copies, waits for them, and re-layouts  3.77 us (4%)
  other arithmetic  2.38 us (2%)
  between operations  1.69 us (2%)
    ppermute x17, waiting for transfers between devices, send(): return lax.ppermute(x, AXES, pairs)  39.7 us
    pallas_call x2, Pallas kernels, product(): pl.pallas_call(functools.partial(product_kernel, n_pieces=len(pieces), ti...  25.6 us
    ppermute x17, starting transfers between devices, send(): return lax.ppermute(x, AXES, pairs)  20.9 us
    pallas_call x1, Pallas kernels, prepare_rows(): pl.pallas_call(body, out_shape=(row, row, mean), grid_spec=pltpu.Prefetch...  4.85 us
    unnamed x8, local copies, waits for them, and re-layouts  3.76 us
  transfers between devices with their start and end apart: 17, of which 5 were waited for; matrix products, arithmetic and copies ran while one was open for 2% of the time, Pallas kernels for 18%

profile of v4, /device:TPU:1, one launch (start us, length us, event | category | flops | bytes accessed | tf_op | source)
XLA Modules:
  0.0 98.9 jit_solution(12855241029858790927)
XLA Ops:
  0.8 2.7 %collective-permute-start.2 = (bf16[4,128,1024]{2,1,0:T(8,128)(2,1)}, bf16[4,128,1024]{2,1,0:T(8,128)(2,1)S(1)}, u32[]{:S(2)}, u32[]{:S(2)}) collective-permute-start(bf16[4,128,1024]{2,1,0:T(8,128)(2,1)} %refs_0_.1), channel_id=1, source_target_pairs={{0,2},{1,3},{14,12},{15,13},{4,6},{5,7},{10,8},{11,9},{8,10},{9,11... | collective-permute-start | bytes 3145736 | tf_op jit(solution)/shard_map/ppermute | solution.py:113
  3.4 1.6 %collective-permute-start.1 = (bf16[4,128,1024]{2,1,0:T(8,128)(2,1)}, bf16[4,128,1024]{2,1,0:T(8,128)(2,1)}, u32[]{:S(2)}, u32[]{:S(2)}) collective-permute-start(bf16[4,128,1024]{2,1,0:T(8,128)(2,1)} %refs_0_.1), channel_id=1, source_target_pairs={{13,9},{2,6},{8,0},{7,15},{29,25},{18,22},{24,16},{23,31}} | collective-permute-start | bytes 3145736 | tf_op jit(solution)/shard_map/ppermute | solution.py:113
  5.1 1.6 %collective-permute-start = (bf16[4,128,1024]{2,1,0:T(8,128)(2,1)}, bf16[4,128,1024]{2,1,0:T(8,128)(2,1)}, u32[]{:S(2)}, u32[]{:S(2)}) collective-permute-start(bf16[4,128,1024]{2,1,0:T(8,128)(2,1)} %refs_0_.1), channel_id=1, source_target_pairs={{0,4},{15,11},{5,9},{10,6},{8,12},{7,3},{16,20},{31,27},{21,25},{2... | collective-permute-start | bytes 3145736 | tf_op jit(solution)/shard_map/ppermute | solution.py:113
  6.7 1.3 %fusion.4 = (s32[4]{0:T(128)S(1)}, s32[4]{0:T(128)S(1)}, s32[]{:T(128)}, s32[4]{0:T(128)S(1)}) fusion(s32[4]{0:T(128)} %lags_ref.1, s32[4]{0:T(128)} %starts_ref.1), kind=kLoop, calls=%fused_computation.19 | loop fusion | flops 15 | bytes 84 | tf_op jit(solution)/shard_map/sub | solution.py:29
  8.0 0.7 fusion.1
  8.8 1.6 %collective-permute-start.7 = (bf16[4,128,1024]{2,1,0:T(8,128)(2,1)}, bf16[4,128,1024]{2,1,0:T(8,128)(2,1)}, u32[]{:S(2)}, u32[]{:S(2)}) collective-permute-start(bf16[4,128,1024]{2,1,0:T(8,128)(2,1)} %collective-permute-done.4.refs_2_), channel_id=1, source_target_pairs={{13,9},{2,6},{8,0},{7,15},{29,25},{18,22},{24,16},{23,31}} | collective-permute-start | bytes 3145736 | tf_op jit(solution)/shard_map/ppermute | solution.py:113
  11.2 16.0 %collective-permute-done.2.refs_1_ = bf16[4,128,1024]{2,1,0:T(8,128)(2,1)S(1)} collective-permute-done((bf16[4,128,1024]{2,1,0:T(8,128)(2,1)}, bf16[4,128,1024]{2,1,0:T(8,128)(2,1)S(1)}, u32[]{:S(2)}, u32[]{:S(2)}) %collective-permute-start.2) | collective-permute-done | bytes 1048608 | tf_op jit(solution)/shard_map/ppermute | solution.py:113
  28.6 1.3 %collective-permute-start.12 = (bf16[4,128,1024]{2,1,0:T(8,128)(2,1)S(1)}, bf16[4,128,1024]{2,1,0:T(8,128)(2,1)S(1)}, u32[]{:S(2)}, u32[]{:S(2)}) collective-permute-start(bf16[4,128,1024]{2,1,0:T(8,128)(2,1)S(1)} %broadcast_select_fusion), channel_id=1, source_target_pairs={{0,4},{15,11},{4,8},{11,7},{9,13},{6,2},{12,14},{3,1},{16,20},{31,... | collective-permute-start | bytes 3145736 | tf_op jit(solution)/shard_map/ppermute | solution.py:113
  29.9 1.3 %collective-permute-start.14 = (bf16[4,128,1024]{2,1,0:T(8,128)(2,1)}, bf16[4,128,1024]{2,1,0:T(8,128)(2,1)S(1)}, u32[]{:S(2)}, u32[]{:S(2)}) collective-permute-start(bf16[4,128,1024]{2,1,0:T(8,128)(2,1)} %collective-permute-done.1), channel_id=1, source_target_pairs={{9,1},{6,14},{0,2},{15,13},{25,17},{22,30},{16,18},{31,29}} | collective-permute-start | bytes 3145736 | tf_op jit(solution)/shard_map/ppermute | solution.py:113
  31.2 1.3 %collective-permute-start.8 = (bf16[4,128,1024]{2,1,0:T(8,128)(2,1)}, bf16[4,128,1024]{2,1,0:T(8,128)(2,1)S(1)}, u32[]{:S(2)}, u32[]{:S(2)}) collective-permute-start(bf16[4,128,1024]{2,1,0:T(8,128)(2,1)} %collective-permute-done.7), channel_id=1, source_target_pairs={{9,1},{6,14},{0,2},{15,13},{25,17},{22,30},{16,18},{31,29}} | collective-permute-start | bytes 3145736 | tf_op jit(solution)/shard_map/ppermute | solution.py:113
  32.6 1.3 %collective-permute-start.6 = (bf16[4,128,1024]{2,1,0:T(8,128)(2,1)S(1)}, bf16[4,128,1024]{2,1,0:T(8,128)(2,1)S(1)}, u32[]{:S(2)}, u32[]{:S(2)}) collective-permute-start(bf16[4,128,1024]{2,1,0:T(8,128)(2,1)S(1)} %broadcast_select_fusion.1), channel_id=1, source_target_pairs={{0,4},{15,11},{4,8},{11,7},{9,13},{6,2},{12,14},{3,1},{16,20},{31,... | collective-permute-start | bytes 3145736 | tf_op jit(solution)/shard_map/ppermute | solution.py:113
  33.9 10.8 %collective-permute-done.12 = bf16[4,128,1024]{2,1,0:T(8,128)(2,1)S(1)} collective-permute-done((bf16[4,128,1024]{2,1,0:T(8,128)(2,1)S(1)}, bf16[4,128,1024]{2,1,0:T(8,128)(2,1)S(1)}, u32[]{:S(2)}, u32[]{:S(2)}) %collective-permute-start.12) | collective-permute-done | bytes 1048608 | tf_op jit(solution)/shard_map/ppermute | solution.py:113
  45.5 3.9 %collective-permute-done.14 = bf16[4,128,1024]{2,1,0:T(8,128)(2,1)S(1)} collective-permute-done((bf16[4,128,1024]{2,1,0:T(8,128)(2,1)}, bf16[4,128,1024]{2,1,0:T(8,128)(2,1)S(1)}, u32[]{:S(2)}, u32[]{:S(2)}) %collective-permute-start.14) | collective-permute-done | bytes 1048608 | tf_op jit(solution)/shard_map/ppermute | solution.py:113
  49.3 1.3 %collective-permute-start.16 = (bf16[4,128,1024]{2,1,0:T(8,128)(2,1)}, bf16[4,128,1024]{2,1,0:T(8,128)(2,1)S(1)}, u32[]{:S(2)}, u32[]{:S(2)}) collective-permute-start(bf16[4,128,1024]{2,1,0:T(8,128)(2,1)} %refs_0_.1), channel_id=1, source_target_pairs={{5,1},{10,14},{21,17},{26,30}} | collective-permute-start | bytes 3145736 | tf_op jit(solution)/shard_map/ppermute | solution.py:113
  50.6 1.4 %collective-permute-start.15 = (bf16[4,128,1024]{2,1,0:T(8,128)(2,1)S(1)}, bf16[4,128,1024]{2,1,0:T(8,128)(2,1)S(1)}, u32[]{:S(2)}, u32[]{:S(2)}) collective-permute-start(bf16[4,128,1024]{2,1,0:T(8,128)(2,1)S(1)} %collective-permute-done.14), channel_id=1, source_target_pairs={{13,9},{2,6},{1,3},{14,12},{29,25},{18,22},{17,19},{30,28}} | collective-permute-start | bytes 3145736 | tf_op jit(solution)/shard_map/ppermute | solution.py:113
  52.0 1.2 %copy-done = bf16[4,128,1024]{2,1,0:T(8,128)(2,1)S(1)} copy-done((bf16[4,128,1024]{2,1,0:T(8,128)(2,1)S(1)}, bf16[4,128,1024]{2,1,0:T(8,128)(2,1)}, u32[]{:S(2)}) %copy-start) | copy-done | bytes 1048600
  54.5 4.9 %rows.1 = (bf16[2048,1024]{1,0:T(8,128)(2,1)S(1)}, bf16[2048,1024]{1,0:T(8,128)(2,1)S(1)}, f32[2048,128]{1,0:T(8,128)S(1)}) custom-call(s32[1]{0:T(128)} %bitcast.part_ref, s32[4]{0:T(128)S(1)} %copy-done.2, s32[4]{0:T(128)S(1)} %copy-done.3, s32[1]{0:T(128)} %bitcast.8.x_ref, f32[1]{0:T(128)} %bitcast.5.count_ref, bf16[4,128,1024]{2,1,0:T(8,128)(2,1)S(1)} %copy-done, ...), custom_call_target="tpu_custom_call" | custom-call | bytes 14680064 | tf_op jit(solution)/shard_map/rows/pallas_call | solution.py:189
  59.4 1.3 %collective-permute-done.8 = bf16[4,128,1024]{2,1,0:T(8,128)(2,1)S(1)} collective-permute-done((bf16[4,128,1024]{2,1,0:T(8,128)(2,1)}, bf16[4,128,1024]{2,1,0:T(8,128)(2,1)S(1)}, u32[]{:S(2)}, u32[]{:S(2)}) %collective-permute-start.8) | collective-permute-done | bytes 1048608 | tf_op jit(solution)/shard_map/ppermute | solution.py:113
  60.7 1.3 %collective-permute-start.11 = (bf16[4,128,1024]{2,1,0:T(8,128)(2,1)}, bf16[4,128,1024]{2,1,0:T(8,128)(2,1)S(1)}, u32[]{:S(2)}, u32[]{:S(2)}) collective-permute-start(bf16[4,128,1024]{2,1,0:T(8,128)(2,1)} %collective-permute-done.4.refs_2_), channel_id=1, source_target_pairs={{5,1},{10,14},{21,17},{26,30}} | collective-permute-start | bytes 3145736 | tf_op jit(solution)/shard_map/ppermute | solution.py:113
  62.0 1.4 %collective-permute-start.10 = (bf16[4,128,1024]{2,1,0:T(8,128)(2,1)S(1)}, bf16[4,128,1024]{2,1,0:T(8,128)(2,1)S(1)}, u32[]{:S(2)}, u32[]{:S(2)}) collective-permute-start(bf16[4,128,1024]{2,1,0:T(8,128)(2,1)S(1)} %collective-permute-done.8), channel_id=1, source_target_pairs={{13,9},{2,6},{1,3},{14,12},{29,25},{18,22},{17,19},{30,28}} | collective-permute-start | bytes 3145736 | tf_op jit(solution)/shard_map/ppermute | solution.py:113
  64.1 7.7 %collective-permute-done.16 = bf16[4,128,1024]{2,1,0:T(8,128)(2,1)S(1)} collective-permute-done((bf16[4,128,1024]{2,1,0:T(8,128)(2,1)}, bf16[4,128,1024]{2,1,0:T(8,128)(2,1)S(1)}, u32[]{:S(2)}, u32[]{:S(2)}) %collective-permute-start.16) | collective-permute-done | bytes 1048608 | tf_op jit(solution)/shard_map/ppermute | solution.py:113
  71.8 1.2 %copy-done.1 = bf16[4,128,1024]{2,1,0:T(8,128)(2,1)S(1)} copy-done((bf16[4,128,1024]{2,1,0:T(8,128)(2,1)S(1)}, bf16[4,128,1024]{2,1,0:T(8,128)(2,1)}, u32[]{:S(2)}) %copy-start.1) | copy-done | bytes 1048600
  73.0 12.8 %covariances.2 = (f32[2048,2048]{1,0:T(8,128)}, f32[2048,2048]{1,0:T(8,128)}) custom-call(s32[1]{0:T(128)} %bitcast.part_ref, s32[2]{0:T(128)S(1)} %pad_add_fusion.place_ref, f32[1]{0:T(128)} %bitcast.5.count_ref, bf16[16,1024]{1,0:T(8,128)(2,1)S(1)} %pad_maximum_fusion.masks_ref, f32[2048,128]{1,0:T(8,128)S(1)} %get-tuple-element.25.mean_ref, ...), custom_call_target="tpu_custom_call" | custom-call | flops 8589934592 | bytes 25165824 | tf_op jit(solution)/shard_map/covariances/pallas_call | solution.py:280
  85.9 12.8 %covariances.3 = (f32[2048,2048]{1,0:T(8,128)}, f32[2048,2048]{1,0:T(8,128)}) custom-call(s32[1]{0:T(128)S(6)} %sub.13.part_ref, s32[2]{0:T(128)S(1)} %pad_add_fusion.place_ref, f32[1]{0:T(128)} %bitcast.5.count_ref, bf16[16,1024]{1,0:T(8,128)(2,1)S(1)} %pad_maximum_fusion.masks_ref, ...), custom_call_target="tpu_custom_call", output_to_operand_aliasing={{0}: (15, {}), {1}: (16, {})} | custom-call | flops 8589934592 | bytes 25165824 | tf_op jit(solution)/shard_map/covariances/pallas_call | solution.py:280
  (33 shorter events, 4.5 us)
Async XLA Ops:
  0.6 8.2 %collective-permute-start.4 = (bf16[4,128,1024]{2,1,0:T(8,128)(2,1)}, bf16[4,128,1024]{2,1,0:T(8,128)(2,1)}, u32[]{:S(2)}, u32[]{:S(2)}) collective-permute-start(bf16[4,128,1024]{2,1,0:T(8,128)(2,1)} %refs_0_.1), channel_id=1, source_target_pairs={{0,1},{1,0},{14,15},{15,14},{4,5},{5,4},{10,11},{11,10},{8,9},{9,8... | collective-permute-start | bytes 3145736 | tf_op jit(solution)/shard_map/ppermute | solution.py:113
  0.8 26.4 %collective-permute-start.2 = (bf16[4,128,1024]{2,1,0:T(8,128)(2,1)}, bf16[4,128,1024]{2,1,0:T(8,128)(2,1)S(1)}, u32[]{:S(2)}, u32[]{:S(2)}) collective-permute-start(bf16[4,128,1024]{2,1,0:T(8,128)(2,1)} %refs_0_.1), channel_id=1, source_target_pairs={{0,2},{1,3},{14,12},{15,13},{4,6},{5,7},{10,8},{11,9},{8,10},{9,11... | collective-permute-start | bytes 3145736 | tf_op jit(solution)/shard_map/ppermute | solution.py:113
  3.4 25.0 %collective-permute-start.1 = (bf16[4,128,1024]{2,1,0:T(8,128)(2,1)}, bf16[4,128,1024]{2,1,0:T(8,128)(2,1)}, u32[]{:S(2)}, u32[]{:S(2)}) collective-permute-start(bf16[4,128,1024]{2,1,0:T(8,128)(2,1)} %refs_0_.1), channel_id=1, source_target_pairs={{13,9},{2,6},{8,0},{7,15},{29,25},{18,22},{24,16},{23,31}} | collective-permute-start | bytes 3145736 | tf_op jit(solution)/shard_map/ppermute | solution.py:113
  5.1 23.4 %collective-permute-start = (bf16[4,128,1024]{2,1,0:T(8,128)(2,1)}, bf16[4,128,1024]{2,1,0:T(8,128)(2,1)}, u32[]{:S(2)}, u32[]{:S(2)}) collective-permute-start(bf16[4,128,1024]{2,1,0:T(8,128)(2,1)} %refs_0_.1), channel_id=1, source_target_pairs={{0,4},{15,11},{5,9},{10,6},{8,12},{7,3},{16,20},{31,27},{21,25},{2... | collective-permute-start | bytes 3145736 | tf_op jit(solution)/shard_map/ppermute | solution.py:113
  8.8 22.3 %collective-permute-start.7 = (bf16[4,128,1024]{2,1,0:T(8,128)(2,1)}, bf16[4,128,1024]{2,1,0:T(8,128)(2,1)}, u32[]{:S(2)}, u32[]{:S(2)}) collective-permute-start(bf16[4,128,1024]{2,1,0:T(8,128)(2,1)} %collective-permute-done.4.refs_2_), channel_id=1, source_target_pairs={{13,9},{2,6},{8,0},{7,15},{29,25},{18,22},{24,16},{23,31}} | collective-permute-start | bytes 3145736 | tf_op jit(solution)/shard_map/ppermute | solution.py:113
  10.5 22.0 %collective-permute-start.5 = (bf16[4,128,1024]{2,1,0:T(8,128)(2,1)}, bf16[4,128,1024]{2,1,0:T(8,128)(2,1)S(1)}, u32[]{:S(2)}, u32[]{:S(2)}) collective-permute-start(bf16[4,128,1024]{2,1,0:T(8,128)(2,1)} %collective-permute-done.4.refs_2_), channel_id=1, source_target_pairs={{0,4},{15,11},{5,9},{10,6},{8,12},{7,3},{16,20},{31,27},{21,25},{2... | collective-permute-start | bytes 3145736 | tf_op jit(solution)/shard_map/ppermute | solution.py:113
  27.2 5.3 %collective-permute-start.3 = (bf16[4,128,1024]{2,1,0:T(8,128)(2,1)S(1)}, bf16[4,128,1024]{2,1,0:T(8,128)(2,1)S(1)}, u32[]{:S(2)}, u32[]{:S(2)}) collective-permute-start(bf16[4,128,1024]{2,1,0:T(8,128)(2,1)S(1)} %collective-permute-done.2.refs_1_), channel_id=1, source_target_pairs={{0,1},{1,0},{14,15},{15,14},{4,5},{5,4},{10,11},{11,10},{8,9},{9,8... | collective-permute-start | bytes 3145736 | tf_op jit(solution)/shard_map/ppermute | solution.py:113
  28.6 16.2 %collective-permute-start.12 = (bf16[4,128,1024]{2,1,0:T(8,128)(2,1)S(1)}, bf16[4,128,1024]{2,1,0:T(8,128)(2,1)S(1)}, u32[]{:S(2)}, u32[]{:S(2)}) collective-permute-start(bf16[4,128,1024]{2,1,0:T(8,128)(2,1)S(1)} %broadcast_select_fusion), channel_id=1, source_target_pairs={{0,4},{15,11},{4,8},{11,7},{9,13},{6,2},{12,14},{3,1},{16,20},{31,... | collective-permute-start | bytes 3145736 | tf_op jit(solution)/shard_map/ppermute | solution.py:113
  29.9 19.4 %collective-permute-start.14 = (bf16[4,128,1024]{2,1,0:T(8,128)(2,1)}, bf16[4,128,1024]{2,1,0:T(8,128)(2,1)S(1)}, u32[]{:S(2)}, u32[]{:S(2)}) collective-permute-start(bf16[4,128,1024]{2,1,0:T(8,128)(2,1)} %collective-permute-done.1), channel_id=1, source_target_pairs={{9,1},{6,14},{0,2},{15,13},{25,17},{22,30},{16,18},{31,29}} | collective-permute-start | bytes 3145736 | tf_op jit(solution)/shard_map/ppermute | solution.py:113
  31.2 29.5 %collective-permute-start.8 = (bf16[4,128,1024]{2,1,0:T(8,128)(2,1)}, bf16[4,128,1024]{2,1,0:T(8,128)(2,1)S(1)}, u32[]{:S(2)}, u32[]{:S(2)}) collective-permute-start(bf16[4,128,1024]{2,1,0:T(8,128)(2,1)} %collective-permute-done.7), channel_id=1, source_target_pairs={{9,1},{6,14},{0,2},{15,13},{25,17},{22,30},{16,18},{31,29}} | collective-permute-start | bytes 3145736 | tf_op jit(solution)/shard_map/ppermute | solution.py:113
  32.6 28.0 %collective-permute-start.6 = (bf16[4,128,1024]{2,1,0:T(8,128)(2,1)S(1)}, bf16[4,128,1024]{2,1,0:T(8,128)(2,1)S(1)}, u32[]{:S(2)}, u32[]{:S(2)}) collective-permute-start(bf16[4,128,1024]{2,1,0:T(8,128)(2,1)S(1)} %broadcast_select_fusion.1), channel_id=1, source_target_pairs={{0,4},{15,11},{4,8},{11,7},{9,13},{6,2},{12,14},{3,1},{16,20},{31,... | collective-permute-start | bytes 3145736 | tf_op jit(solution)/shard_map/ppermute | solution.py:113
  44.7 18.6 %collective-permute-start.13 = (bf16[4,128,1024]{2,1,0:T(8,128)(2,1)S(1)}, bf16[4,128,1024]{2,1,0:T(8,128)(2,1)S(1)}, u32[]{:S(2)}, u32[]{:S(2)}) collective-permute-start(bf16[4,128,1024]{2,1,0:T(8,128)(2,1)S(1)} %collective-permute-done.12), channel_id=1, source_target_pairs={{4,8},{11,7},{8,12},{7,3},{20,24},{27,23},{24,28},{23,19}} | collective-permute-start | bytes 3145736 | tf_op jit(solution)/shard_map/ppermute | solution.py:113
  49.3 22.5 %collective-permute-start.16 = (bf16[4,128,1024]{2,1,0:T(8,128)(2,1)}, bf16[4,128,1024]{2,1,0:T(8,128)(2,1)S(1)}, u32[]{:S(2)}, u32[]{:S(2)}) collective-permute-start(bf16[4,128,1024]{2,1,0:T(8,128)(2,1)} %refs_0_.1), channel_id=1, source_target_pairs={{5,1},{10,14},{21,17},{26,30}} | collective-permute-start | bytes 3145736 | tf_op jit(solution)/shard_map/ppermute | solution.py:113
  50.6 21.2 %collective-permute-start.15 = (bf16[4,128,1024]{2,1,0:T(8,128)(2,1)S(1)}, bf16[4,128,1024]{2,1,0:T(8,128)(2,1)S(1)}, u32[]{:S(2)}, u32[]{:S(2)}) collective-permute-start(bf16[4,128,1024]{2,1,0:T(8,128)(2,1)S(1)} %collective-permute-done.14), channel_id=1, source_target_pairs={{13,9},{2,6},{1,3},{14,12},{29,25},{18,22},{17,19},{30,28}} | collective-permute-start | bytes 3145736 | tf_op jit(solution)/shard_map/ppermute | solution.py:113
  52.0 1.2 %copy-start = (bf16[4,128,1024]{2,1,0:T(8,128)(2,1)S(1)}, bf16[4,128,1024]{2,1,0:T(8,128)(2,1)}, u32[]{:S(2)}) copy-start(bf16[4,128,1024]{2,1,0:T(8,128)(2,1)} %refs_0_.1) | copy-start | bytes 3145732
  53.2 0.7 copy-start.2
  53.9 0.7 copy-start.3
  60.7 25.2 %collective-permute-start.11 = (bf16[4,128,1024]{2,1,0:T(8,128)(2,1)}, bf16[4,128,1024]{2,1,0:T(8,128)(2,1)S(1)}, u32[]{:S(2)}, u32[]{:S(2)}) collective-permute-start(bf16[4,128,1024]{2,1,0:T(8,128)(2,1)} %collective-permute-done.4.refs_2_), channel_id=1, source_target_pairs={{5,1},{10,14},{21,17},{26,30}} | collective-permute-start | bytes 3145736 | tf_op jit(solution)/shard_map/ppermute | solution.py:113
  62.0 23.9 %collective-permute-start.10 = (bf16[4,128,1024]{2,1,0:T(8,128)(2,1)S(1)}, bf16[4,128,1024]{2,1,0:T(8,128)(2,1)S(1)}, u32[]{:S(2)}, u32[]{:S(2)}) collective-permute-start(bf16[4,128,1024]{2,1,0:T(8,128)(2,1)S(1)} %collective-permute-done.8), channel_id=1, source_target_pairs={{13,9},{2,6},{1,3},{14,12},{29,25},{18,22},{17,19},{30,28}} | collective-permute-start | bytes 3145736 | tf_op jit(solution)/shard_map/ppermute | solution.py:113
  63.3 22.5 %collective-permute-start.9 = (bf16[4,128,1024]{2,1,0:T(8,128)(2,1)S(1)}, bf16[4,128,1024]{2,1,0:T(8,128)(2,1)S(1)}, u32[]{:S(2)}, u32[]{:S(2)}) collective-permute-start(bf16[4,128,1024]{2,1,0:T(8,128)(2,1)S(1)} %collective-permute-done.6), channel_id=1, source_target_pairs={{4,8},{11,7},{8,12},{7,3},{20,24},{27,23},{24,28},{23,19}} | collective-permute-start | bytes 3145736 | tf_op jit(solution)/shard_map/ppermute | solution.py:113
  71.8 1.2 %copy-start.1 = (bf16[4,128,1024]{2,1,0:T(8,128)(2,1)S(1)}, bf16[4,128,1024]{2,1,0:T(8,128)(2,1)}, u32[]{:S(2)}) copy-start(bf16[4,128,1024]{2,1,0:T(8,128)(2,1)} %refs_0_.1) | copy-start | bytes 3145732

commit v5 on v4

--- a/solution.py
+++ b/solution.py
@@ -210,7 +210,7 @@
 
 def product_kernel(part_ref, place_ref, count_ref, masks_ref, mean_ref, zero_ref, late_ref, *refs, n_pieces, tiles):
     pieces = refs[:n_pieces]
-    cov_zero_ref, cov_late_ref, left_ref, columns_ref, made_ref, arrived, fetched, stored = refs[-8:]
+    cov_zero_ref, cov_late_ref, columns_ref, made_ref, arrived, stored = refs[-6:]
     half, width = columns_ref.shape[0] // 2, columns_ref.shape[1]
     scale = 1.0 / count_ref[0]
     first = pl.multiple_of(part_ref[0] * width, width)
@@ -218,12 +218,6 @@
     def piece_copy(piece, side):
         return pltpu.make_async_copy(
             piece, columns_ref.at[pl.ds(side * half, half)], arrived.at[side]
-        )
-
-    def left_copy(n, i):
-        rows = pl.ds(*tiles[i])
-        return pltpu.make_async_copy(
-            (zero_ref, late_ref)[n].at[rows], left_ref.at[n, rows], fetched.at[n, i]
         )
 
     def out_copy(n, i):
@@ -242,22 +236,16 @@
                 def _():
                     piece_copy(pieces[m], side).start()
 
-    for n in range(2):
-        left_copy(n, 0).start()
     for side in range(2):
         piece_copy(pieces[0], side).wait()
     for i, (top, tile) in enumerate(tiles):
-        if i + 1 < len(tiles):
-            for n in range(2):
-                left_copy(n, i + 1).start()
         if i == 0:
             means = dot(masks_ref[...], columns_ref[...]) * scale
         row_mean = mean_ref[top : top + tile, :1]
         for n in range(2):
-            left_copy(n, i).wait()
             if i >= DEPTH:
                 out_copy(n, i - DEPTH).wait()
-            total = dot(left_ref[n, top : top + tile], columns_ref[...])
+            total = dot((zero_ref, late_ref)[n][top : top + tile], columns_ref[...])
             made_ref[i % DEPTH, n, :tile] = total * scale - row_mean * means[8 * n : 8 * n + 1]
             out_copy(n, i).start()
     for i in range(max(0, len(tiles) - DEPTH), len(tiles)):
@@ -274,30 +262,23 @@
         tile = min(tile, height - top)
         tiles.append((top, tile))
         top += tile
-    steps, tile = len(tiles), max(TILES)
+    tile = max(TILES)
     out = jax.ShapeDtypeStruct((height, 2 * width), jnp.float32)
     anywhere = pl.BlockSpec(memory_space=pl.ANY)
     return pl.pallas_call(
         functools.partial(product_kernel, n_pieces=len(pieces), tiles=tiles),
         out_shape=(out, out),
-        grid_spec=pltpu.PrefetchScalarGridSpec(
-            num_scalar_prefetch=3,
-            grid=(1,),
-            in_specs=[
-                pl.BlockSpec((16, depth), lambda i, *_: (0, 0)),
-                pl.BlockSpec((height, 128), lambda i, *_: (0, 0)),
-            ]
-            + [anywhere] * (2 + len(pieces) + len(before)),
-            out_specs=[anywhere] * 2,
-            scratch_shapes=[
-                pltpu.VMEM((2, height, depth), jnp.bfloat16),
-                pltpu.VMEM((depth, width), jnp.bfloat16),
-                pltpu.VMEM((DEPTH, 2, tile, width), jnp.float32),
-                pltpu.SemaphoreType.DMA((2,)),
-                pltpu.SemaphoreType.DMA((2, steps)),
-                pltpu.SemaphoreType.DMA((DEPTH, 2)),
-            ],
-        ),
+        in_specs=[pl.BlockSpec(memory_space=pltpu.SMEM)] * 3
+        + [pl.BlockSpec(memory_space=pltpu.VMEM)] * 4
+        + [pl.BlockSpec(memory_space=pltpu.HBM)]
+        + [anywhere] * (len(pieces) - 1 + len(before)),
+        out_specs=[anywhere] * 2,
+        scratch_shapes=[
+            pltpu.VMEM((depth, width), jnp.bfloat16),
+            pltpu.VMEM((DEPTH, 2, tile, width), jnp.float32),
+            pltpu.SemaphoreType.DMA((2,)),
+            pltpu.SemaphoreType.DMA((DEPTH, 2)),
+        ],
         input_output_aliases={7 + len(pieces) + i: i for i in range(len(before))},
         compiler_params=pltpu.CompilerParams(vmem_limit_bytes=VMEM_LIMIT),
         cost_estimate=pl.CostEstimate(
@@ -352,7 +333,7 @@
         part, window_starts, lag_frames, plane, count, ((own, cross), (sib, sib_cross)), window
     )
     near2_b, far2_b, *rows = lax.optimization_barrier((near2_b, far2_b, *rows))
-    near3_b, back_b, close_b = send(near2_b, NEAR_3), send(far2_b, BACK_3), send(after(sib, near2_b), OWN_3)
+    near3_b, back_b, close_b = send(near2_b, NEAR_3), send(far2_b, BACK_3), send(after(sib, near2_b, far2_b), OWN_3)
 
     outs = ()
     for where_to, pieces in (

time: 99.4 us -> 96.9 us (0.975)
  waiting for transfers between devices: 39.7 us -> 32 us
  starting transfers between devices: 20.9 us -> 28.5 us
  Pallas kernels: 30.5 us -> 28 us
    ppermute x17, waiting for transfers between devices: 39.7 us -> 32 us  [send(): return lax.ppermute(x, AXES, pairs)]
    ppermute x17, starting transfers between devices: 20.9 us -> 28.5 us  [send(): return lax.ppermute(x, AXES, pairs)]
    pallas_call x2, Pallas kernels: 25.6 us -> 23.1 us  [product(): pl.pallas_call(functools.partial(product_kernel, n_pieces=len(pieces), ti...]
  transfers between devices with their start and end apart: 17 -> 17, of which waited for: 5 -> 5; matrix products, arithmetic and copies ran while one was open for 2% -> 2% of each run, Pallas kernels for 18% -> 17%
where the time goes in v5:
time: 96.9 us; the launch traced here: 96.4 us
  waiting for transfers between devices  32 us (33%)
  starting transfers between devices  28.5 us (29%)
  Pallas kernels  28 us (29%)
  local copies, waits for them, and re-layouts  3.77 us (4%)
  other arithmetic  2.38 us (2%)
  between operations  1.69 us (2%)
    ppermute x17, waiting for transfers between devices, send(): return lax.ppermute(x, AXES, pairs)  32 us
    ppermute x17, starting transfers between devices, send(): return lax.ppermute(x, AXES, pairs)  28.5 us
    pallas_call x2, Pallas kernels, product(): pl.pallas_call(functools.partial(product_kernel, n_pieces=len(pieces), ti...  23.1 us
    pallas_call x1, Pallas kernels, prepare_rows(): pl.pallas_call(body, out_shape=(row, row, mean), grid_spec=pltpu.Prefetch...  4.85 us
    unnamed x8, local copies, waits for them, and re-layouts  3.76 us
  transfers between devices with their start and end apart: 17, of which 5 were waited for; matrix products, arithmetic and copies ran while one was open for 2% of the time, Pallas kernels for 17%

profile of v5, /device:TPU:1, one launch (start us, length us, event | category | flops | bytes accessed | tf_op | source)
XLA Modules:
  0.0 96.4 jit_solution(325773745548177801)
XLA Ops:
  0.8 2.7 %collective-permute-start.2 = (bf16[4,128,1024]{2,1,0:T(8,128)(2,1)}, bf16[4,128,1024]{2,1,0:T(8,128)(2,1)S(1)}, u32[]{:S(2)}, u32[]{:S(2)}) collective-permute-start(bf16[4,128,1024]{2,1,0:T(8,128)(2,1)} %refs_0_.1), channel_id=1, source_target_pairs={{0,2},{1,3},{14,12},{15,13},{4,6},{5,7},{10,8},{11,9},{8,10},{9,11... | collective-permute-start | bytes 3145736 | tf_op jit(solution)/shard_map/ppermute | solution.py:113
  3.4 1.6 %collective-permute-start.1 = (bf16[4,128,1024]{2,1,0:T(8,128)(2,1)}, bf16[4,128,1024]{2,1,0:T(8,128)(2,1)}, u32[]{:S(2)}, u32[]{:S(2)}) collective-permute-start(bf16[4,128,1024]{2,1,0:T(8,128)(2,1)} %refs_0_.1), channel_id=1, source_target_pairs={{13,9},{2,6},{8,0},{7,15},{29,25},{18,22},{24,16},{23,31}} | collective-permute-start | bytes 3145736 | tf_op jit(solution)/shard_map/ppermute | solution.py:113
  5.1 1.6 %collective-permute-start = (bf16[4,128,1024]{2,1,0:T(8,128)(2,1)}, bf16[4,128,1024]{2,1,0:T(8,128)(2,1)}, u32[]{:S(2)}, u32[]{:S(2)}) collective-permute-start(bf16[4,128,1024]{2,1,0:T(8,128)(2,1)} %refs_0_.1), channel_id=1, source_target_pairs={{0,4},{15,11},{5,9},{10,6},{8,12},{7,3},{16,20},{31,27},{21,25},{2... | collective-permute-start | bytes 3145736 | tf_op jit(solution)/shard_map/ppermute | solution.py:113
  6.7 1.3 %fusion.4 = (s32[4]{0:T(128)S(1)}, s32[4]{0:T(128)S(1)}, s32[]{:T(128)}, s32[4]{0:T(128)S(1)}) fusion(s32[4]{0:T(128)} %lags_ref.1, s32[4]{0:T(128)} %starts_ref.1), kind=kLoop, calls=%fused_computation.19 | loop fusion | flops 15 | bytes 84 | tf_op jit(solution)/shard_map/sub | solution.py:29
  8.0 0.7 fusion.1
  8.8 1.6 %collective-permute-start.7 = (bf16[4,128,1024]{2,1,0:T(8,128)(2,1)}, bf16[4,128,1024]{2,1,0:T(8,128)(2,1)}, u32[]{:S(2)}, u32[]{:S(2)}) collective-permute-start(bf16[4,128,1024]{2,1,0:T(8,128)(2,1)} %collective-permute-done.4.refs_2_), channel_id=1, source_target_pairs={{13,9},{2,6},{8,0},{7,15},{29,25},{18,22},{24,16},{23,31}} | collective-permute-start | bytes 3145736 | tf_op jit(solution)/shard_map/ppermute | solution.py:113
  11.2 16.0 %collective-permute-done.2.refs_1_ = bf16[4,128,1024]{2,1,0:T(8,128)(2,1)S(1)} collective-permute-done((bf16[4,128,1024]{2,1,0:T(8,128)(2,1)}, bf16[4,128,1024]{2,1,0:T(8,128)(2,1)S(1)}, u32[]{:S(2)}, u32[]{:S(2)}) %collective-permute-start.2) | collective-permute-done | bytes 1048608 | tf_op jit(solution)/shard_map/ppermute | solution.py:113
  28.6 1.3 %collective-permute-start.12 = (bf16[4,128,1024]{2,1,0:T(8,128)(2,1)S(1)}, bf16[4,128,1024]{2,1,0:T(8,128)(2,1)S(1)}, u32[]{:S(2)}, u32[]{:S(2)}) collective-permute-start(bf16[4,128,1024]{2,1,0:T(8,128)(2,1)S(1)} %broadcast_select_fusion), channel_id=1, source_target_pairs={{0,4},{15,11},{4,8},{11,7},{9,13},{6,2},{12,14},{3,1},{16,20},{31,... | collective-permute-start | bytes 3145736 | tf_op jit(solution)/shard_map/ppermute | solution.py:113
  29.9 1.3 %collective-permute-start.14 = (bf16[4,128,1024]{2,1,0:T(8,128)(2,1)}, bf16[4,128,1024]{2,1,0:T(8,128)(2,1)S(1)}, u32[]{:S(2)}, u32[]{:S(2)}) collective-permute-start(bf16[4,128,1024]{2,1,0:T(8,128)(2,1)} %collective-permute-done.1), channel_id=1, source_target_pairs={{9,1},{6,14},{0,2},{15,13},{25,17},{22,30},{16,18},{31,29}} | collective-permute-start | bytes 3145736 | tf_op jit(solution)/shard_map/ppermute | solution.py:113
  31.2 1.3 %collective-permute-start.8 = (bf16[4,128,1024]{2,1,0:T(8,128)(2,1)}, bf16[4,128,1024]{2,1,0:T(8,128)(2,1)S(1)}, u32[]{:S(2)}, u32[]{:S(2)}) collective-permute-start(bf16[4,128,1024]{2,1,0:T(8,128)(2,1)} %collective-permute-done.7), channel_id=1, source_target_pairs={{9,1},{6,14},{0,2},{15,13},{25,17},{22,30},{16,18},{31,29}} | collective-permute-start | bytes 3145736 | tf_op jit(solution)/shard_map/ppermute | solution.py:113
  32.6 1.3 %collective-permute-start.6 = (bf16[4,128,1024]{2,1,0:T(8,128)(2,1)S(1)}, bf16[4,128,1024]{2,1,0:T(8,128)(2,1)S(1)}, u32[]{:S(2)}, u32[]{:S(2)}) collective-permute-start(bf16[4,128,1024]{2,1,0:T(8,128)(2,1)S(1)} %broadcast_select_fusion.1), channel_id=1, source_target_pairs={{0,4},{15,11},{4,8},{11,7},{9,13},{6,2},{12,14},{3,1},{16,20},{31,... | collective-permute-start | bytes 3145736 | tf_op jit(solution)/shard_map/ppermute | solution.py:113
  33.9 10.8 %collective-permute-done.12 = bf16[4,128,1024]{2,1,0:T(8,128)(2,1)S(1)} collective-permute-done((bf16[4,128,1024]{2,1,0:T(8,128)(2,1)S(1)}, bf16[4,128,1024]{2,1,0:T(8,128)(2,1)S(1)}, u32[]{:S(2)}, u32[]{:S(2)}) %collective-permute-start.12) | collective-permute-done | bytes 1048608 | tf_op jit(solution)/shard_map/ppermute | solution.py:113
  45.5 3.9 %collective-permute-done.14 = bf16[4,128,1024]{2,1,0:T(8,128)(2,1)S(1)} collective-permute-done((bf16[4,128,1024]{2,1,0:T(8,128)(2,1)}, bf16[4,128,1024]{2,1,0:T(8,128)(2,1)S(1)}, u32[]{:S(2)}, u32[]{:S(2)}) %collective-permute-start.14) | collective-permute-done | bytes 1048608 | tf_op jit(solution)/shard_map/ppermute | solution.py:113
  49.3 1.3 %collective-permute-start.16 = (bf16[4,128,1024]{2,1,0:T(8,128)(2,1)}, bf16[4,128,1024]{2,1,0:T(8,128)(2,1)S(1)}, u32[]{:S(2)}, u32[]{:S(2)}) collective-permute-start(bf16[4,128,1024]{2,1,0:T(8,128)(2,1)} %refs_0_.1), channel_id=1, source_target_pairs={{5,1},{10,14},{21,17},{26,30}} | collective-permute-start | bytes 3145736 | tf_op jit(solution)/shard_map/ppermute | solution.py:113
  50.6 1.4 %collective-permute-start.15 = (bf16[4,128,1024]{2,1,0:T(8,128)(2,1)S(1)}, bf16[4,128,1024]{2,1,0:T(8,128)(2,1)S(1)}, u32[]{:S(2)}, u32[]{:S(2)}) collective-permute-start(bf16[4,128,1024]{2,1,0:T(8,128)(2,1)S(1)} %collective-permute-done.14), channel_id=1, source_target_pairs={{13,9},{2,6},{1,3},{14,12},{29,25},{18,22},{17,19},{30,28}} | collective-permute-start | bytes 3145736 | tf_op jit(solution)/shard_map/ppermute | solution.py:113
  52.0 1.2 %copy-done = bf16[4,128,1024]{2,1,0:T(8,128)(2,1)S(1)} copy-done((bf16[4,128,1024]{2,1,0:T(8,128)(2,1)S(1)}, bf16[4,128,1024]{2,1,0:T(8,128)(2,1)}, u32[]{:S(2)}) %copy-start) | copy-done | bytes 1048600
  54.5 4.9 %rows.1 = (bf16[2048,1024]{1,0:T(8,128)(2,1)S(1)}, bf16[2048,1024]{1,0:T(8,128)(2,1)S(1)}, f32[2048,128]{1,0:T(8,128)S(1)}) custom-call(s32[1]{0:T(128)} %bitcast.part_ref, s32[4]{0:T(128)S(1)} %copy-done.2, s32[4]{0:T(128)S(1)} %copy-done.3, s32[1]{0:T(128)} %bitcast.8.x_ref, f32[1]{0:T(128)} %bitcast.5.count_ref, bf16[4,128,1024]{2,1,0:T(8,128)(2,1)S(1)} %copy-done, ...), custom_call_target="tpu_custom_call" | custom-call | bytes 14680064 | tf_op jit(solution)/shard_map/rows/pallas_call | solution.py:189
  59.4 1.3 %collective-permute-done.8 = bf16[4,128,1024]{2,1,0:T(8,128)(2,1)S(1)} collective-permute-done((bf16[4,128,1024]{2,1,0:T(8,128)(2,1)}, bf16[4,128,1024]{2,1,0:T(8,128)(2,1)S(1)}, u32[]{:S(2)}, u32[]{:S(2)}) %collective-permute-start.8) | collective-permute-done | bytes 1048608 | tf_op jit(solution)/shard_map/ppermute | solution.py:113
  60.7 0.7 collective-permute-start.9
  61.4 1.3 %collective-permute-start.11 = (bf16[4,128,1024]{2,1,0:T(8,128)(2,1)}, bf16[4,128,1024]{2,1,0:T(8,128)(2,1)S(1)}, u32[]{:S(2)}, u32[]{:S(2)}) collective-permute-start(bf16[4,128,1024]{2,1,0:T(8,128)(2,1)} %collective-permute-done.4.refs_2_), channel_id=1, source_target_pairs={{5,1},{10,14},{21,17},{26,30}} | collective-permute-start | bytes 3145736 | tf_op jit(solution)/shard_map/ppermute | solution.py:113
  62.7 9.0 %collective-permute-start.10 = (bf16[4,128,1024]{2,1,0:T(8,128)(2,1)S(1)}, bf16[4,128,1024]{2,1,0:T(8,128)(2,1)S(1)}, u32[]{:S(2)}, u32[]{:S(2)}) collective-permute-start(bf16[4,128,1024]{2,1,0:T(8,128)(2,1)S(1)} %collective-permute-done.8), channel_id=1, source_target_pairs={{13,9},{2,6},{1,3},{14,12},{29,25},{18,22},{17,19},{30,28}} | collective-permute-start | bytes 3145736 | tf_op jit(solution)/shard_map/ppermute | solution.py:113
  71.8 1.2 %copy-done.1 = bf16[4,128,1024]{2,1,0:T(8,128)(2,1)S(1)} copy-done((bf16[4,128,1024]{2,1,0:T(8,128)(2,1)S(1)}, bf16[4,128,1024]{2,1,0:T(8,128)(2,1)}, u32[]{:S(2)}) %copy-start.1) | copy-done | bytes 1048600
  73.0 11.5 %covariances.2 = (f32[2048,2048]{1,0:T(8,128)}, f32[2048,2048]{1,0:T(8,128)}) custom-call(s32[1]{0:T(128)} %bitcast.part_ref, s32[2]{0:T(128)S(1)} %pad_add_fusion.place_ref, f32[1]{0:T(128)} %bitcast.5.count_ref, bf16[16,1024]{1,0:T(8,128)(2,1)S(1)} %pad_maximum_fusion.masks_ref, f32[2048,128]{1,0:T(8,128)S(1)} %get-tuple-element.25.mean_ref, ...), custom_call_target="tpu_custom_call" | custom-call | flops 8589934592 | bytes 25165824 | tf_op jit(solution)/shard_map/covariances/pallas_call | solution.py:268
  84.6 11.6 %covariances.3 = (f32[2048,2048]{1,0:T(8,128)}, f32[2048,2048]{1,0:T(8,128)}) custom-call(s32[1]{0:T(128)S(6)} %sub.13.part_ref, s32[2]{0:T(128)S(1)} %pad_add_fusion.place_ref, f32[1]{0:T(128)} %bitcast.5.count_ref, bf16[16,1024]{1,0:T(8,128)(2,1)S(1)} %pad_maximum_fusion.masks_ref, ...), custom_call_target="tpu_custom_call", output_to_operand_aliasing={{0}: (15, {}), {1}: (16, {})} | custom-call | flops 8589934592 | bytes 25165824 | tf_op jit(solution)/shard_map/covariances/pallas_call | solution.py:268
  (33 shorter events, 3.9 us)
Async XLA Ops:
  0.6 8.2 %collective-permute-start.4 = (bf16[4,128,1024]{2,1,0:T(8,128)(2,1)}, bf16[4,128,1024]{2,1,0:T(8,128)(2,1)}, u32[]{:S(2)}, u32[]{:S(2)}) collective-permute-start(bf16[4,128,1024]{2,1,0:T(8,128)(2,1)} %refs_0_.1), channel_id=1, source_target_pairs={{0,1},{1,0},{14,15},{15,14},{4,5},{5,4},{10,11},{11,10},{8,9},{9,8... | collective-permute-start | bytes 3145736 | tf_op jit(solution)/shard_map/ppermute | solution.py:113
  0.8 26.4 %collective-permute-start.2 = (bf16[4,128,1024]{2,1,0:T(8,128)(2,1)}, bf16[4,128,1024]{2,1,0:T(8,128)(2,1)S(1)}, u32[]{:S(2)}, u32[]{:S(2)}) collective-permute-start(bf16[4,128,1024]{2,1,0:T(8,128)(2,1)} %refs_0_.1), channel_id=1, source_target_pairs={{0,2},{1,3},{14,12},{15,13},{4,6},{5,7},{10,8},{11,9},{8,10},{9,11... | collective-permute-start | bytes 3145736 | tf_op jit(solution)/shard_map/ppermute | solution.py:113
  3.4 25.0 %collective-permute-start.1 = (bf16[4,128,1024]{2,1,0:T(8,128)(2,1)}, bf16[4,128,1024]{2,1,0:T(8,128)(2,1)}, u32[]{:S(2)}, u32[]{:S(2)}) collective-permute-start(bf16[4,128,1024]{2,1,0:T(8,128)(2,1)} %refs_0_.1), channel_id=1, source_target_pairs={{13,9},{2,6},{8,0},{7,15},{29,25},{18,22},{24,16},{23,31}} | collective-permute-start | bytes 3145736 | tf_op jit(solution)/shard_map/ppermute | solution.py:113
  5.1 23.4 %collective-permute-start = (bf16[4,128,1024]{2,1,0:T(8,128)(2,1)}, bf16[4,128,1024]{2,1,0:T(8,128)(2,1)}, u32[]{:S(2)}, u32[]{:S(2)}) collective-permute-start(bf16[4,128,1024]{2,1,0:T(8,128)(2,1)} %refs_0_.1), channel_id=1, source_target_pairs={{0,4},{15,11},{5,9},{10,6},{8,12},{7,3},{16,20},{31,27},{21,25},{2... | collective-permute-start | bytes 3145736 | tf_op jit(solution)/shard_map/ppermute | solution.py:113
  8.8 22.3 %collective-permute-start.7 = (bf16[4,128,1024]{2,1,0:T(8,128)(2,1)}, bf16[4,128,1024]{2,1,0:T(8,128)(2,1)}, u32[]{:S(2)}, u32[]{:S(2)}) collective-permute-start(bf16[4,128,1024]{2,1,0:T(8,128)(2,1)} %collective-permute-done.4.refs_2_), channel_id=1, source_target_pairs={{13,9},{2,6},{8,0},{7,15},{29,25},{18,22},{24,16},{23,31}} | collective-permute-start | bytes 3145736 | tf_op jit(solution)/shard_map/ppermute | solution.py:113
  10.5 22.0 %collective-permute-start.5 = (bf16[4,128,1024]{2,1,0:T(8,128)(2,1)}, bf16[4,128,1024]{2,1,0:T(8,128)(2,1)S(1)}, u32[]{:S(2)}, u32[]{:S(2)}) collective-permute-start(bf16[4,128,1024]{2,1,0:T(8,128)(2,1)} %collective-permute-done.4.refs_2_), channel_id=1, source_target_pairs={{0,4},{15,11},{5,9},{10,6},{8,12},{7,3},{16,20},{31,27},{21,25},{2... | collective-permute-start | bytes 3145736 | tf_op jit(solution)/shard_map/ppermute | solution.py:113
  27.2 5.3 %collective-permute-start.3 = (bf16[4,128,1024]{2,1,0:T(8,128)(2,1)S(1)}, bf16[4,128,1024]{2,1,0:T(8,128)(2,1)S(1)}, u32[]{:S(2)}, u32[]{:S(2)}) collective-permute-start(bf16[4,128,1024]{2,1,0:T(8,128)(2,1)S(1)} %collective-permute-done.2.refs_1_), channel_id=1, source_target_pairs={{0,1},{1,0},{14,15},{15,14},{4,5},{5,4},{10,11},{11,10},{8,9},{9,8... | collective-permute-start | bytes 3145736 | tf_op jit(solution)/shard_map/ppermute | solution.py:113
  28.6 16.2 %collective-permute-start.12 = (bf16[4,128,1024]{2,1,0:T(8,128)(2,1)S(1)}, bf16[4,128,1024]{2,1,0:T(8,128)(2,1)S(1)}, u32[]{:S(2)}, u32[]{:S(2)}) collective-permute-start(bf16[4,128,1024]{2,1,0:T(8,128)(2,1)S(1)} %broadcast_select_fusion), channel_id=1, source_target_pairs={{0,4},{15,11},{4,8},{11,7},{9,13},{6,2},{12,14},{3,1},{16,20},{31,... | collective-permute-start | bytes 3145736 | tf_op jit(solution)/shard_map/ppermute | solution.py:113
  29.9 19.4 %collective-permute-start.14 = (bf16[4,128,1024]{2,1,0:T(8,128)(2,1)}, bf16[4,128,1024]{2,1,0:T(8,128)(2,1)S(1)}, u32[]{:S(2)}, u32[]{:S(2)}) collective-permute-start(bf16[4,128,1024]{2,1,0:T(8,128)(2,1)} %collective-permute-done.1), channel_id=1, source_target_pairs={{9,1},{6,14},{0,2},{15,13},{25,17},{22,30},{16,18},{31,29}} | collective-permute-start | bytes 3145736 | tf_op jit(solution)/shard_map/ppermute | solution.py:113
  31.2 29.5 %collective-permute-start.8 = (bf16[4,128,1024]{2,1,0:T(8,128)(2,1)}, bf16[4,128,1024]{2,1,0:T(8,128)(2,1)S(1)}, u32[]{:S(2)}, u32[]{:S(2)}) collective-permute-start(bf16[4,128,1024]{2,1,0:T(8,128)(2,1)} %collective-permute-done.7), channel_id=1, source_target_pairs={{9,1},{6,14},{0,2},{15,13},{25,17},{22,30},{16,18},{31,29}} | collective-permute-start | bytes 3145736 | tf_op jit(solution)/shard_map/ppermute | solution.py:113
  32.6 28.0 %collective-permute-start.6 = (bf16[4,128,1024]{2,1,0:T(8,128)(2,1)S(1)}, bf16[4,128,1024]{2,1,0:T(8,128)(2,1)S(1)}, u32[]{:S(2)}, u32[]{:S(2)}) collective-permute-start(bf16[4,128,1024]{2,1,0:T(8,128)(2,1)S(1)} %broadcast_select_fusion.1), channel_id=1, source_target_pairs={{0,4},{15,11},{4,8},{11,7},{9,13},{6,2},{12,14},{3,1},{16,20},{31,... | collective-permute-start | bytes 3145736 | tf_op jit(solution)/shard_map/ppermute | solution.py:113
  44.7 18.0 %collective-permute-start.13 = (bf16[4,128,1024]{2,1,0:T(8,128)(2,1)S(1)}, bf16[4,128,1024]{2,1,0:T(8,128)(2,1)S(1)}, u32[]{:S(2)}, u32[]{:S(2)}) collective-permute-start(bf16[4,128,1024]{2,1,0:T(8,128)(2,1)S(1)} %collective-permute-done.12), channel_id=1, source_target_pairs={{4,8},{11,7},{8,12},{7,3},{20,24},{27,23},{24,28},{23,19}} | collective-permute-start | bytes 3145736 | tf_op jit(solution)/shard_map/ppermute | solution.py:113
  49.3 22.5 %collective-permute-start.16 = (bf16[4,128,1024]{2,1,0:T(8,128)(2,1)}, bf16[4,128,1024]{2,1,0:T(8,128)(2,1)S(1)}, u32[]{:S(2)}, u32[]{:S(2)}) collective-permute-start(bf16[4,128,1024]{2,1,0:T(8,128)(2,1)} %refs_0_.1), channel_id=1, source_target_pairs={{5,1},{10,14},{21,17},{26,30}} | collective-permute-start | bytes 3145736 | tf_op jit(solution)/shard_map/ppermute | solution.py:113
  50.6 21.2 %collective-permute-start.15 = (bf16[4,128,1024]{2,1,0:T(8,128)(2,1)S(1)}, bf16[4,128,1024]{2,1,0:T(8,128)(2,1)S(1)}, u32[]{:S(2)}, u32[]{:S(2)}) collective-permute-start(bf16[4,128,1024]{2,1,0:T(8,128)(2,1)S(1)} %collective-permute-done.14), channel_id=1, source_target_pairs={{13,9},{2,6},{1,3},{14,12},{29,25},{18,22},{17,19},{30,28}} | collective-permute-start | bytes 3145736 | tf_op jit(solution)/shard_map/ppermute | solution.py:113
  52.0 1.2 %copy-start = (bf16[4,128,1024]{2,1,0:T(8,128)(2,1)S(1)}, bf16[4,128,1024]{2,1,0:T(8,128)(2,1)}, u32[]{:S(2)}) copy-start(bf16[4,128,1024]{2,1,0:T(8,128)(2,1)} %refs_0_.1) | copy-start | bytes 3145732
  53.2 0.7 copy-start.2
  53.9 0.7 copy-start.3
  60.7 23.9 %collective-permute-start.9 = (bf16[4,128,1024]{2,1,0:T(8,128)(2,1)S(1)}, bf16[4,128,1024]{2,1,0:T(8,128)(2,1)S(1)}, u32[]{:S(2)}, u32[]{:S(2)}) collective-permute-start(bf16[4,128,1024]{2,1,0:T(8,128)(2,1)S(1)} %collective-permute-done.6), channel_id=1, source_target_pairs={{4,8},{11,7},{8,12},{7,3},{20,24},{27,23},{24,28},{23,19}} | collective-permute-start | bytes 3145736 | tf_op jit(solution)/shard_map/ppermute | solution.py:113
  61.4 23.2 %collective-permute-start.11 = (bf16[4,128,1024]{2,1,0:T(8,128)(2,1)}, bf16[4,128,1024]{2,1,0:T(8,128)(2,1)S(1)}, u32[]{:S(2)}, u32[]{:S(2)}) collective-permute-start(bf16[4,128,1024]{2,1,0:T(8,128)(2,1)} %collective-permute-done.4.refs_2_), channel_id=1, source_target_pairs={{5,1},{10,14},{21,17},{26,30}} | collective-permute-start | bytes 3145736 | tf_op jit(solution)/shard_map/ppermute | solution.py:113
  62.7 21.9 %collective-permute-start.10 = (bf16[4,128,1024]{2,1,0:T(8,128)(2,1)S(1)}, bf16[4,128,1024]{2,1,0:T(8,128)(2,1)S(1)}, u32[]{:S(2)}, u32[]{:S(2)}) collective-permute-start(bf16[4,128,1024]{2,1,0:T(8,128)(2,1)S(1)} %collective-permute-done.8), channel_id=1, source_target_pairs={{13,9},{2,6},{1,3},{14,12},{29,25},{18,22},{17,19},{30,28}} | collective-permute-start | bytes 3145736 | tf_op jit(solution)/shard_map/ppermute | solution.py:113
  71.8 1.2 %copy-start.1 = (bf16[4,128,1024]{2,1,0:T(8,128)(2,1)S(1)}, bf16[4,128,1024]{2,1,0:T(8,128)(2,1)}, u32[]{:S(2)}) copy-start(bf16[4,128,1024]{2,1,0:T(8,128)(2,1)} %refs_0_.1) | copy-start | bytes 3145732

commit v6 on v5

--- a/solution.py
+++ b/solution.py
@@ -270,8 +270,7 @@
         out_shape=(out, out),
         in_specs=[pl.BlockSpec(memory_space=pltpu.SMEM)] * 3
         + [pl.BlockSpec(memory_space=pltpu.VMEM)] * 4
-        + [pl.BlockSpec(memory_space=pltpu.HBM)]
-        + [anywhere] * (len(pieces) - 1 + len(before)),
+        + [anywhere] * (len(pieces) + len(before)),
         out_specs=[anywhere] * 2,
         scratch_shapes=[
             pltpu.VMEM((depth, width), jnp.bfloat16),
@@ -322,22 +321,23 @@
     cross = send(own, PLANES)
     sib = send(own, CORES)
     near1_b, far1_b = send(sib, NEAR_1), send(sib, FAR_1)
-    near1_a, far1_a, masks, count, place = lax.optimization_barrier(
-        (near1_a, far1_a, masks, count, place)
+    kept = jnp.where(s < 0, jnp.zeros_like(own), own)
+    near1_a, far1_a, masks, count, place, kept = lax.optimization_barrier(
+        (near1_a, far1_a, masks, count, place, kept)
     )
     near2_a, far2_a = send(jnp.where(s == 0, cross, near1_a), NEAR_2), send(far1_a, FAR_2)
     sib_cross = send(cross, CORES)
     near2_b, far2_b = send(jnp.where(s == 0, sib_cross, near1_b), NEAR_2), send(far1_b, FAR_2)
     near3_a, back_a, close_a = send(near2_a, NEAR_3), send(far2_a, BACK_3), send(after(own, near2_a, far2_a), OWN_3)
     rows = prepare_rows(
-        part, window_starts, lag_frames, plane, count, ((own, cross), (sib, sib_cross)), window
+        part, window_starts, lag_frames, plane, count, ((kept, cross), (sib, sib_cross)), window
     )
     near2_b, far2_b, *rows = lax.optimization_barrier((near2_b, far2_b, *rows))
     near3_b, back_b, close_b = send(near2_b, NEAR_3), send(far2_b, BACK_3), send(after(sib, near2_b, far2_b), OWN_3)
 
     outs = ()
     for where_to, pieces in (
-        (part, (own, cross, near1_a, near2_a, near3_a, back_a, far2_a, close_a)),
+        (part, (kept, cross, near1_a, near2_a, near3_a, back_a, far2_a, close_a)),
         (1 - part, (sib, sib_cross, near1_b, near2_b, near3_b, back_b, far2_b, close_b)),
     ):
         pieces = [piece.reshape(trajectories * half, features) for piece in pieces]

time: 96.9 us -> 95.8 us (0.989)
  waiting for transfers between devices: 32 us -> 26.6 us
  starting transfers between devices: 28.5 us -> 33.1 us
  local copies, waits for them, and re-layouts: 3.77 us -> 1.32 us
  other arithmetic: 2.38 us -> 3.75 us
    ppermute x17, waiting for transfers between devices: 32 us -> 26.6 us  [send(): return lax.ppermute(x, AXES, pairs)]
    ppermute x17, starting transfers between devices: 28.5 us -> 33.1 us  [send(): return lax.ppermute(x, AXES, pairs)]
    unnamed x8 -> x4, local copies, waits for them, and re-layouts: 3.76 us -> 1.31 us
    select_n x0 -> x1, other arithmetic: none -> 1.3 us  [line_of_four(): kept = jnp.where(s < 0, jnp.zeros_like(own), own)]
  transfers between devices with their start and end apart: 17 -> 17, of which waited for: 5 -> 5; matrix products, arithmetic and copies ran while one was open for 2% -> 4% of each run, Pallas kernels for 17% -> 17%
where the time goes in v6:
time: 95.8 us; the launch traced here: 94.8 us
  starting transfers between devices  33.1 us (35%)
  Pallas kernels  28.2 us (29%)
  waiting for transfers between devices  26.6 us (28%)
  other arithmetic  3.75 us (4%)
  between operations  1.75 us (2%)
  local copies, waits for them, and re-layouts  1.32 us (1%)
    ppermute x17, starting transfers between devices, send(): return lax.ppermute(x, AXES, pairs)  33.1 us
    ppermute x17, waiting for transfers between devices, send(): return lax.ppermute(x, AXES, pairs)  26.6 us
    pallas_call x2, Pallas kernels, product(): pl.pallas_call(functools.partial(product_kernel, n_pieces=len(pieces), ti...  23.4 us
    pallas_call x1, Pallas kernels, prepare_rows(): pl.pallas_call(body, out_shape=(row, row, mean), grid_spec=pltpu.Prefetch...  4.88 us
  transfers between devices with their start and end apart: 17, of which 5 were waited for; matrix products, arithmetic and copies ran while one was open for 4% of the time, Pallas kernels for 17%

profile of v6, /device:TPU:1, one launch (start us, length us, event | category | flops | bytes accessed | tf_op | source)
XLA Modules:
  0.0 94.8 jit_solution(10623718337861067136)
XLA Ops:
  0.6 2.1 %collective-permute-start.2 = (bf16[4,128,1024]{2,1,0:T(8,128)(2,1)}, bf16[4,128,1024]{2,1,0:T(8,128)(2,1)S(1)}, u32[]{:S(2)}, u32[]{:S(2)}) collective-permute-start(bf16[4,128,1024]{2,1,0:T(8,128)(2,1)} %param.3), channel_id=1, source_target_pairs={{0,2},{1,3},{14,12},{15,13},{4,6},{5,7},{10,8},{11,9},{8,10},{9,11... | collective-permute-start | bytes 3145736 | tf_op jit(solution)/shard_map/ppermute | solution.py:113
  2.7 1.6 %collective-permute-start.1 = (bf16[4,128,1024]{2,1,0:T(8,128)(2,1)}, bf16[4,128,1024]{2,1,0:T(8,128)(2,1)}, u32[]{:S(2)}, u32[]{:S(2)}) collective-permute-start(bf16[4,128,1024]{2,1,0:T(8,128)(2,1)} %param.3), channel_id=1, source_target_pairs={{13,9},{2,6},{8,0},{7,15},{29,25},{18,22},{24,16},{23,31}} | collective-permute-start | bytes 3145736 | tf_op jit(solution)/shard_map/ppermute | solution.py:113
  4.4 1.6 %collective-permute-start = (bf16[4,128,1024]{2,1,0:T(8,128)(2,1)}, bf16[4,128,1024]{2,1,0:T(8,128)(2,1)}, u32[]{:S(2)}, u32[]{:S(2)}) collective-permute-start(bf16[4,128,1024]{2,1,0:T(8,128)(2,1)} %param.3), channel_id=1, source_target_pairs={{0,4},{15,11},{5,9},{10,6},{8,12},{7,3},{16,20},{31,27},{21,25},{2... | collective-permute-start | bytes 3145736 | tf_op jit(solution)/shard_map/ppermute | solution.py:113
  6.0 3.8 %collective-permute-start.4 = (bf16[4,128,1024]{2,1,0:T(8,128)(2,1)}, bf16[4,128,1024]{2,1,0:T(8,128)(2,1)}, u32[]{:S(2)}, u32[]{:S(2)}) collective-permute-start(bf16[4,128,1024]{2,1,0:T(8,128)(2,1)} %param.3), channel_id=1, source_target_pairs={{0,1},{1,0},{14,15},{15,14},{4,5},{5,4},{10,11},{11,10},{8,9},{9,8... | collective-permute-start | bytes 3145736 | tf_op jit(solution)/shard_map/ppermute | solution.py:113
  9.8 1.4 %fusion.4 = (s32[4]{0:T(128)S(1)}, s32[4]{0:T(128)S(1)}, s32[]{:T(128)}, s32[4]{0:T(128)S(1)}) fusion(s32[4]{0:T(128)} %lags_ref.1, s32[4]{0:T(128)} %starts_ref.1), kind=kLoop, calls=%fused_computation.20 | loop fusion | flops 15 | bytes 84 | tf_op jit(solution)/shard_map/sub | solution.py:29
  12.0 1.3 %broadcast_select_fusion.2.refs_0_ = bf16[4,128,1024]{2,1,0:T(8,128)(2,1)S(1)} fusion(bf16[4,128,1024]{2,1,0:T(8,128)(2,1)} %param.3, pred[]{:T(512)S(6)} %lt.14), kind=kLoop, calls=%fused_computation.2 | loop fusion | flops 524288 | bytes 2097153 | tf_op jit(solution)/shard_map/jit(_where)/select_n | solution.py:324
  13.3 1.7 %collective-permute-start.7 = (bf16[4,128,1024]{2,1,0:T(8,128)(2,1)}, bf16[4,128,1024]{2,1,0:T(8,128)(2,1)}, u32[]{:S(2)}, u32[]{:S(2)}) collective-permute-start(bf16[4,128,1024]{2,1,0:T(8,128)(2,1)} %collective-permute-done.4.refs_2_), channel_id=1, source_target_pairs={{13,9},{2,6},{8,0},{7,15},{29,25},{18,22},{24,16},{23,31}} | collective-permute-start | bytes 3145736 | tf_op jit(solution)/shard_map/ppermute | solution.py:113
  15.0 1.6 %collective-permute-start.5 = (bf16[4,128,1024]{2,1,0:T(8,128)(2,1)}, bf16[4,128,1024]{2,1,0:T(8,128)(2,1)}, u32[]{:S(2)}, u32[]{:S(2)}) collective-permute-start(bf16[4,128,1024]{2,1,0:T(8,128)(2,1)} %collective-permute-done.4.refs_2_), channel_id=1, source_target_pairs={{0,4},{15,11},{5,9},{10,6},{8,12},{7,3},{16,20},{31,27},{21,25},{2... | collective-permute-start | bytes 3145736 | tf_op jit(solution)/shard_map/ppermute | solution.py:113
  16.6 9.4 %collective-permute-done.2.refs_1_ = bf16[4,128,1024]{2,1,0:T(8,128)(2,1)S(1)} collective-permute-done((bf16[4,128,1024]{2,1,0:T(8,128)(2,1)}, bf16[4,128,1024]{2,1,0:T(8,128)(2,1)S(1)}, u32[]{:S(2)}, u32[]{:S(2)}) %collective-permute-start.2) | collective-permute-done | bytes 1048608 | tf_op jit(solution)/shard_map/ppermute | solution.py:113
  25.9 1.1 %collective-permute-start.3 = (bf16[4,128,1024]{2,1,0:T(8,128)(2,1)S(1)}, bf16[4,128,1024]{2,1,0:T(8,128)(2,1)S(1)}, u32[]{:S(2)}, u32[]{:S(2)}) collective-permute-start(bf16[4,128,1024]{2,1,0:T(8,128)(2,1)S(1)} %collective-permute-done.2.refs_1_), channel_id=1, source_target_pairs={{0,1},{1,0},{14,15},{15,14},{4,5},{5,4},{10,11},{11,10},{8,9},{9,8... | collective-permute-start | bytes 3145736 | tf_op jit(solution)/shard_map/ppermute | solution.py:113
  28.0 1.3 %collective-permute-start.12 = (bf16[4,128,1024]{2,1,0:T(8,128)(2,1)S(1)}, bf16[4,128,1024]{2,1,0:T(8,128)(2,1)S(1)}, u32[]{:S(2)}, u32[]{:S(2)}) collective-permute-start(bf16[4,128,1024]{2,1,0:T(8,128)(2,1)S(1)} %broadcast_select_fusion), channel_id=1, source_target_pairs={{0,4},{15,11},{4,8},{11,7},{9,13},{6,2},{12,14},{3,1},{16,20},{31,... | collective-permute-start | bytes 3145736 | tf_op jit(solution)/shard_map/ppermute | solution.py:113
  29.3 1.3 %collective-permute-start.14 = (bf16[4,128,1024]{2,1,0:T(8,128)(2,1)}, bf16[4,128,1024]{2,1,0:T(8,128)(2,1)S(1)}, u32[]{:S(2)}, u32[]{:S(2)}) collective-permute-start(bf16[4,128,1024]{2,1,0:T(8,128)(2,1)} %collective-permute-done.1), channel_id=1, source_target_pairs={{9,1},{6,14},{0,2},{15,13},{25,17},{22,30},{16,18},{31,29}} | collective-permute-start | bytes 3145736 | tf_op jit(solution)/shard_map/ppermute | solution.py:113
  30.6 1.3 %collective-permute-start.8 = (bf16[4,128,1024]{2,1,0:T(8,128)(2,1)}, bf16[4,128,1024]{2,1,0:T(8,128)(2,1)S(1)}, u32[]{:S(2)}, u32[]{:S(2)}) collective-permute-start(bf16[4,128,1024]{2,1,0:T(8,128)(2,1)} %collective-permute-done.7), channel_id=1, source_target_pairs={{9,1},{6,14},{0,2},{15,13},{25,17},{22,30},{16,18},{31,29}} | collective-permute-start | bytes 3145736 | tf_op jit(solution)/shard_map/ppermute | solution.py:113
  32.0 1.3 %collective-permute-start.6 = (bf16[4,128,1024]{2,1,0:T(8,128)(2,1)S(1)}, bf16[4,128,1024]{2,1,0:T(8,128)(2,1)S(1)}, u32[]{:S(2)}, u32[]{:S(2)}) collective-permute-start(bf16[4,128,1024]{2,1,0:T(8,128)(2,1)S(1)} %broadcast_select_fusion.1), channel_id=1, source_target_pairs={{0,4},{15,11},{4,8},{11,7},{9,13},{6,2},{12,14},{3,1},{16,20},{31,... | collective-permute-start | bytes 3145736 | tf_op jit(solution)/shard_map/ppermute | solution.py:113
  33.3 10.8 %collective-permute-done.12 = bf16[4,128,1024]{2,1,0:T(8,128)(2,1)S(1)} collective-permute-done((bf16[4,128,1024]{2,1,0:T(8,128)(2,1)S(1)}, bf16[4,128,1024]{2,1,0:T(8,128)(2,1)S(1)}, u32[]{:S(2)}, u32[]{:S(2)}) %collective-permute-start.12) | collective-permute-done | bytes 1048608 | tf_op jit(solution)/shard_map/ppermute | solution.py:113
  44.8 3.9 %collective-permute-done.14 = bf16[4,128,1024]{2,1,0:T(8,128)(2,1)S(1)} collective-permute-done((bf16[4,128,1024]{2,1,0:T(8,128)(2,1)}, bf16[4,128,1024]{2,1,0:T(8,128)(2,1)S(1)}, u32[]{:S(2)}, u32[]{:S(2)}) %collective-permute-start.14) | collective-permute-done | bytes 1048608 | tf_op jit(solution)/shard_map/ppermute | solution.py:113
  48.7 1.3 %collective-permute-start.16 = (bf16[4,128,1024]{2,1,0:T(8,128)(2,1)}, bf16[4,128,1024]{2,1,0:T(8,128)(2,1)S(1)}, u32[]{:S(2)}, u32[]{:S(2)}) collective-permute-start(bf16[4,128,1024]{2,1,0:T(8,128)(2,1)} %param.3), channel_id=1, source_target_pairs={{5,1},{10,14},{21,17},{26,30}} | collective-permute-start | bytes 3145736 | tf_op jit(solution)/shard_map/ppermute | solution.py:113
  50.0 1.4 %collective-permute-start.15 = (bf16[4,128,1024]{2,1,0:T(8,128)(2,1)S(1)}, bf16[4,128,1024]{2,1,0:T(8,128)(2,1)S(1)}, u32[]{:S(2)}, u32[]{:S(2)}) collective-permute-start(bf16[4,128,1024]{2,1,0:T(8,128)(2,1)S(1)} %collective-permute-done.14), channel_id=1, source_target_pairs={{13,9},{2,6},{1,3},{14,12},{29,25},{18,22},{17,19},{30,28}} | collective-permute-start | bytes 3145736 | tf_op jit(solution)/shard_map/ppermute | solution.py:113
  52.7 4.9 %rows.1 = (bf16[2048,1024]{1,0:T(8,128)(2,1)S(1)}, bf16[2048,1024]{1,0:T(8,128)(2,1)S(1)}, f32[2048,128]{1,0:T(8,128)S(1)}) custom-call(s32[1]{0:T(128)} %bitcast.part_ref, s32[4]{0:T(128)S(1)} %copy-done, s32[4]{0:T(128)S(1)} %copy-done.1, s32[1]{0:T(128)} %bitcast.8.x_ref, f32[1]{0:T(128)} %bitcast.5.count_ref, ...), custom_call_target="tpu_custom_call" | custom-call | bytes 14680064 | tf_op jit(solution)/shard_map/rows/pallas_call | solution.py:189
  57.6 2.5 %collective-permute-done.8 = bf16[4,128,1024]{2,1,0:T(8,128)(2,1)S(1)} collective-permute-done((bf16[4,128,1024]{2,1,0:T(8,128)(2,1)}, bf16[4,128,1024]{2,1,0:T(8,128)(2,1)S(1)}, u32[]{:S(2)}, u32[]{:S(2)}) %collective-permute-start.8) | collective-permute-done | bytes 1048608 | tf_op jit(solution)/shard_map/ppermute | solution.py:113
  60.8 1.3 %collective-permute-start.11 = (bf16[4,128,1024]{2,1,0:T(8,128)(2,1)}, bf16[4,128,1024]{2,1,0:T(8,128)(2,1)S(1)}, u32[]{:S(2)}, u32[]{:S(2)}) collective-permute-start(bf16[4,128,1024]{2,1,0:T(8,128)(2,1)} %collective-permute-done.4.refs_2_), channel_id=1, source_target_pairs={{5,1},{10,14},{21,17},{26,30}} | collective-permute-start | bytes 3145736 | tf_op jit(solution)/shard_map/ppermute | solution.py:113
  62.1 9.0 %collective-permute-start.10 = (bf16[4,128,1024]{2,1,0:T(8,128)(2,1)S(1)}, bf16[4,128,1024]{2,1,0:T(8,128)(2,1)S(1)}, u32[]{:S(2)}, u32[]{:S(2)}) collective-permute-start(bf16[4,128,1024]{2,1,0:T(8,128)(2,1)S(1)} %collective-permute-done.8), channel_id=1, source_target_pairs={{13,9},{2,6},{1,3},{14,12},{29,25},{18,22},{17,19},{30,28}} | collective-permute-start | bytes 3145736 | tf_op jit(solution)/shard_map/ppermute | solution.py:113
  71.2 11.7 %covariances.2 = (f32[2048,2048]{1,0:T(8,128)}, f32[2048,2048]{1,0:T(8,128)}) custom-call(s32[1]{0:T(128)} %bitcast.part_ref, s32[2]{0:T(128)S(1)} %pad_add_fusion.place_ref, f32[1]{0:T(128)} %bitcast.5.count_ref, bf16[16,1024]{1,0:T(8,128)(2,1)S(1)} %pad_maximum_fusion.masks_ref, f32[2048,128]{1,0:T(8,128)S(1)} %get-tuple-element.27.mean_ref, ...), custom_call_target="tpu_custom_call" | custom-call | flops 8589934592 | bytes 25165824 | tf_op jit(solution)/shard_map/covariances/pallas_call | solution.py:268
  82.9 11.7 %covariances.3 = (f32[2048,2048]{1,0:T(8,128)}, f32[2048,2048]{1,0:T(8,128)}) custom-call(s32[1]{0:T(128)S(6)} %sub.13.part_ref, s32[2]{0:T(128)S(1)} %pad_add_fusion.place_ref, f32[1]{0:T(128)} %bitcast.5.count_ref, bf16[16,1024]{1,0:T(8,128)(2,1)S(1)} %pad_maximum_fusion.masks_ref, ...), custom_call_target="tpu_custom_call", output_to_operand_aliasing={{0}: (15, {}), {1}: (16, {})} | custom-call | flops 8589934592 | bytes 25165824 | tf_op jit(solution)/shard_map/covariances/pallas_call | solution.py:268
  (30 shorter events, 3.9 us)
Async XLA Ops:
  0.6 25.3 %collective-permute-start.2 = (bf16[4,128,1024]{2,1,0:T(8,128)(2,1)}, bf16[4,128,1024]{2,1,0:T(8,128)(2,1)S(1)}, u32[]{:S(2)}, u32[]{:S(2)}) collective-permute-start(bf16[4,128,1024]{2,1,0:T(8,128)(2,1)} %param.3), channel_id=1, source_target_pairs={{0,2},{1,3},{14,12},{15,13},{4,6},{5,7},{10,8},{11,9},{8,10},{9,11... | collective-permute-start | bytes 3145736 | tf_op jit(solution)/shard_map/ppermute | solution.py:113
  2.7 25.1 %collective-permute-start.1 = (bf16[4,128,1024]{2,1,0:T(8,128)(2,1)}, bf16[4,128,1024]{2,1,0:T(8,128)(2,1)}, u32[]{:S(2)}, u32[]{:S(2)}) collective-permute-start(bf16[4,128,1024]{2,1,0:T(8,128)(2,1)} %param.3), channel_id=1, source_target_pairs={{13,9},{2,6},{8,0},{7,15},{29,25},{18,22},{24,16},{23,31}} | collective-permute-start | bytes 3145736 | tf_op jit(solution)/shard_map/ppermute | solution.py:113
  4.4 23.5 %collective-permute-start = (bf16[4,128,1024]{2,1,0:T(8,128)(2,1)}, bf16[4,128,1024]{2,1,0:T(8,128)(2,1)}, u32[]{:S(2)}, u32[]{:S(2)}) collective-permute-start(bf16[4,128,1024]{2,1,0:T(8,128)(2,1)} %param.3), channel_id=1, source_target_pairs={{0,4},{15,11},{5,9},{10,6},{8,12},{7,3},{16,20},{31,27},{21,25},{2... | collective-permute-start | bytes 3145736 | tf_op jit(solution)/shard_map/ppermute | solution.py:113
  6.0 7.3 %collective-permute-start.4 = (bf16[4,128,1024]{2,1,0:T(8,128)(2,1)}, bf16[4,128,1024]{2,1,0:T(8,128)(2,1)}, u32[]{:S(2)}, u32[]{:S(2)}) collective-permute-start(bf16[4,128,1024]{2,1,0:T(8,128)(2,1)} %param.3), channel_id=1, source_target_pairs={{0,1},{1,0},{14,15},{15,14},{4,5},{5,4},{10,11},{11,10},{8,9},{9,8... | collective-permute-start | bytes 3145736 | tf_op jit(solution)/shard_map/ppermute | solution.py:113
  13.3 17.3 %collective-permute-start.7 = (bf16[4,128,1024]{2,1,0:T(8,128)(2,1)}, bf16[4,128,1024]{2,1,0:T(8,128)(2,1)}, u32[]{:S(2)}, u32[]{:S(2)}) collective-permute-start(bf16[4,128,1024]{2,1,0:T(8,128)(2,1)} %collective-permute-done.4.refs_2_), channel_id=1, source_target_pairs={{13,9},{2,6},{8,0},{7,15},{29,25},{18,22},{24,16},{23,31}} | collective-permute-start | bytes 3145736 | tf_op jit(solution)/shard_map/ppermute | solution.py:113
  15.0 16.9 %collective-permute-start.5 = (bf16[4,128,1024]{2,1,0:T(8,128)(2,1)}, bf16[4,128,1024]{2,1,0:T(8,128)(2,1)}, u32[]{:S(2)}, u32[]{:S(2)}) collective-permute-start(bf16[4,128,1024]{2,1,0:T(8,128)(2,1)} %collective-permute-done.4.refs_2_), channel_id=1, source_target_pairs={{0,4},{15,11},{5,9},{10,6},{8,12},{7,3},{16,20},{31,27},{21,25},{2... | collective-permute-start | bytes 3145736 | tf_op jit(solution)/shard_map/ppermute | solution.py:113
  25.9 5.9 %collective-permute-start.3 = (bf16[4,128,1024]{2,1,0:T(8,128)(2,1)S(1)}, bf16[4,128,1024]{2,1,0:T(8,128)(2,1)S(1)}, u32[]{:S(2)}, u32[]{:S(2)}) collective-permute-start(bf16[4,128,1024]{2,1,0:T(8,128)(2,1)S(1)} %collective-permute-done.2.refs_1_), channel_id=1, source_target_pairs={{0,1},{1,0},{14,15},{15,14},{4,5},{5,4},{10,11},{11,10},{8,9},{9,8... | collective-permute-start | bytes 3145736 | tf_op jit(solution)/shard_map/ppermute | solution.py:113
  28.0 16.1 %collective-permute-start.12 = (bf16[4,128,1024]{2,1,0:T(8,128)(2,1)S(1)}, bf16[4,128,1024]{2,1,0:T(8,128)(2,1)S(1)}, u32[]{:S(2)}, u32[]{:S(2)}) collective-permute-start(bf16[4,128,1024]{2,1,0:T(8,128)(2,1)S(1)} %broadcast_select_fusion), channel_id=1, source_target_pairs={{0,4},{15,11},{4,8},{11,7},{9,13},{6,2},{12,14},{3,1},{16,20},{31,... | collective-permute-start | bytes 3145736 | tf_op jit(solution)/shard_map/ppermute | solution.py:113
  29.3 19.4 %collective-permute-start.14 = (bf16[4,128,1024]{2,1,0:T(8,128)(2,1)}, bf16[4,128,1024]{2,1,0:T(8,128)(2,1)S(1)}, u32[]{:S(2)}, u32[]{:S(2)}) collective-permute-start(bf16[4,128,1024]{2,1,0:T(8,128)(2,1)} %collective-permute-done.1), channel_id=1, source_target_pairs={{9,1},{6,14},{0,2},{15,13},{25,17},{22,30},{16,18},{31,29}} | collective-permute-start | bytes 3145736 | tf_op jit(solution)/shard_map/ppermute | solution.py:113
  30.6 29.4 %collective-permute-start.8 = (bf16[4,128,1024]{2,1,0:T(8,128)(2,1)}, bf16[4,128,1024]{2,1,0:T(8,128)(2,1)S(1)}, u32[]{:S(2)}, u32[]{:S(2)}) collective-permute-start(bf16[4,128,1024]{2,1,0:T(8,128)(2,1)} %collective-permute-done.7), channel_id=1, source_target_pairs={{9,1},{6,14},{0,2},{15,13},{25,17},{22,30},{16,18},{31,29}} | collective-permute-start | bytes 3145736 | tf_op jit(solution)/shard_map/ppermute | solution.py:113
  32.0 28.0 %collective-permute-start.6 = (bf16[4,128,1024]{2,1,0:T(8,128)(2,1)S(1)}, bf16[4,128,1024]{2,1,0:T(8,128)(2,1)S(1)}, u32[]{:S(2)}, u32[]{:S(2)}) collective-permute-start(bf16[4,128,1024]{2,1,0:T(8,128)(2,1)S(1)} %broadcast_select_fusion.1), channel_id=1, source_target_pairs={{0,4},{15,11},{4,8},{11,7},{9,13},{6,2},{12,14},{3,1},{16,20},{31,... | collective-permute-start | bytes 3145736 | tf_op jit(solution)/shard_map/ppermute | solution.py:113
  44.1 18.0 %collective-permute-start.13 = (bf16[4,128,1024]{2,1,0:T(8,128)(2,1)S(1)}, bf16[4,128,1024]{2,1,0:T(8,128)(2,1)S(1)}, u32[]{:S(2)}, u32[]{:S(2)}) collective-permute-start(bf16[4,128,1024]{2,1,0:T(8,128)(2,1)S(1)} %collective-permute-done.12), channel_id=1, source_target_pairs={{4,8},{11,7},{8,12},{7,3},{20,24},{27,23},{24,28},{23,19}} | collective-permute-start | bytes 3145736 | tf_op jit(solution)/shard_map/ppermute | solution.py:113
  48.7 22.5 %collective-permute-start.16 = (bf16[4,128,1024]{2,1,0:T(8,128)(2,1)}, bf16[4,128,1024]{2,1,0:T(8,128)(2,1)S(1)}, u32[]{:S(2)}, u32[]{:S(2)}) collective-permute-start(bf16[4,128,1024]{2,1,0:T(8,128)(2,1)} %param.3), channel_id=1, source_target_pairs={{5,1},{10,14},{21,17},{26,30}} | collective-permute-start | bytes 3145736 | tf_op jit(solution)/shard_map/ppermute | solution.py:113
  50.0 21.2 %collective-permute-start.15 = (bf16[4,128,1024]{2,1,0:T(8,128)(2,1)S(1)}, bf16[4,128,1024]{2,1,0:T(8,128)(2,1)S(1)}, u32[]{:S(2)}, u32[]{:S(2)}) collective-permute-start(bf16[4,128,1024]{2,1,0:T(8,128)(2,1)S(1)} %collective-permute-done.14), channel_id=1, source_target_pairs={{13,9},{2,6},{1,3},{14,12},{29,25},{18,22},{17,19},{30,28}} | collective-permute-start | bytes 3145736 | tf_op jit(solution)/shard_map/ppermute | solution.py:113
  51.3 0.7 copy-start
  52.0 0.7 copy-start.1
  60.0 22.8 %collective-permute-start.9 = (bf16[4,128,1024]{2,1,0:T(8,128)(2,1)S(1)}, bf16[4,128,1024]{2,1,0:T(8,128)(2,1)S(1)}, u32[]{:S(2)}, u32[]{:S(2)}) collective-permute-start(bf16[4,128,1024]{2,1,0:T(8,128)(2,1)S(1)} %collective-permute-done.6), channel_id=1, source_target_pairs={{4,8},{11,7},{8,12},{7,3},{20,24},{27,23},{24,28},{23,19}} | collective-permute-start | bytes 3145736 | tf_op jit(solution)/shard_map/ppermute | solution.py:113
  60.8 22.1 %collective-permute-start.11 = (bf16[4,128,1024]{2,1,0:T(8,128)(2,1)}, bf16[4,128,1024]{2,1,0:T(8,128)(2,1)S(1)}, u32[]{:S(2)}, u32[]{:S(2)}) collective-permute-start(bf16[4,128,1024]{2,1,0:T(8,128)(2,1)} %collective-permute-done.4.refs_2_), channel_id=1, source_target_pairs={{5,1},{10,14},{21,17},{26,30}} | collective-permute-start | bytes 3145736 | tf_op jit(solution)/shard_map/ppermute | solution.py:113
  62.1 20.8 %collective-permute-start.10 = (bf16[4,128,1024]{2,1,0:T(8,128)(2,1)S(1)}, bf16[4,128,1024]{2,1,0:T(8,128)(2,1)S(1)}, u32[]{:S(2)}, u32[]{:S(2)}) collective-permute-start(bf16[4,128,1024]{2,1,0:T(8,128)(2,1)S(1)} %collective-permute-done.8), channel_id=1, source_target_pairs={{13,9},{2,6},{1,3},{14,12},{29,25},{18,22},{17,19},{30,28}} | collective-permute-start | bytes 3145736 | tf_op jit(solution)/shard_map/ppermute | solution.py:113
